TPU v7x, 256 devices: a whole 4x4x8 slice. The times are simulated.
256 devices in a mesh: space: 32 (over y, x, core), rx: 8 (over z).
Axes of the slice: x: 4, y: 4, z: 8, core: 2. Of those that a mesh axis runs over, the one named last changes fastest.
Arguments:
- lambda_next: float32 [64, 3, 64, 32, 128], P('rx', None, 'space'), may hold values from -40 to 40
- class_ids: int32 [64, 32, 128], P('space'), may hold values from 0 to 15
- class_rate: float32 [16], replicated, may hold values from 0.2 to 4
- coil_x: int32 [64], P('rx'), may hold values from 0 to 62
- coil_y: int32 [64], P('rx'), may hold values from 0 to 30
- coil_z: int32 [64], P('rx'), may hold values from 0 to 127
- coil_amp: float32 [64], P('rx'), may hold values from -12 to 12
Outputs:
- adjoint: float32 [64, 3, 64, 32, 128], P('rx', None, 'space')
All inputs are finite; a program needn't handle non-finite values.
Results may differ from a plain program's by a relative error of at most 0.0003.
Values sent between devices are 32-bit elements; how exact they have to be, the bound alone decides.
No kernel may reach another device: no remote copies, remote signals or barrier semaphores. Data moves between devices by JAX's collectives and lax.ppermute only.
A program may use at most 128 MiB of HBM per device.

v0:
```python
import functools

import jax
import jax.numpy as jnp
from jax import lax
from jax.experimental import pallas as pl
from jax.experimental.pallas import tpu as pltpu
from jax.sharding import PartitionSpec as P

SHIFT = 6.0
LANES = 128
HALF = 64
PLANE = 32
GHOST = 11
F32 = jnp.float32
BF16 = jnp.bfloat16
NT = (((1,), (1,)), ((), ()))
NN = (((1,), (0,)), ((), ()))


def lane_ids():
    lane = lax.broadcasted_iota(jnp.int32, (8, LANES), 1)
    return lane & 31, (lane >> 5) & 1, lane >> 6


def turn(a, shift):
    return pltpu.roll(a, shift, axis=a.ndim - 1)


def y_next(a):
    return jnp.where(lane_ids()[0] == 31, 0.0, turn(a, LANES - 1))


def y_prev(a):
    return jnp.where(lane_ids()[0] == 0, 0.0, turn(a, 1))


def z_both(a):
    half = turn(a, HALF)
    mixed = jnp.where(lane_ids()[2] == 0, half[:-1], half[1:])
    return jnp.concatenate([mixed, half[-1:]], axis=0), jnp.concatenate([half[:1], mixed], axis=0)


def x_next(a, beyond):
    return jnp.where(lane_ids()[1] == 0, turn(a, LANES - PLANE), beyond)


def x_prev(a, beyond):
    return jnp.where(lane_ids()[1] == 1, turn(a, PLANE), beyond)


def pack_up(a, b):
    return jnp.where(lane_ids()[1] == 1, a, turn(b, LANES - PLANE))


def pack_down(a, b):
    return jnp.where(lane_ids()[1] == 0, a, turn(b, PLANE))


def unpack(m, second, up):
    if second:
        return m
    return turn(m, LANES - PLANE) if up else turn(m, PLANE)


def slopes(v):
    return v[1] + y_next(v[0]) - v[0], v[2] + z_both(v[0])[0] - v[0]


def apply_tiles(v, shifted, beyond, before):
    g1, g2 = slopes(v)
    e1 = v[1] - x_next(v[1], beyond[0])
    e2 = v[2] - x_next(v[2], beyond[1])
    q2 = z_both(v[2])[1] - v[2]
    q1 = y_prev(v[1]) - v[1]
    v1_next, v1_prev = z_both(v[1])
    r0 = 2.0 * v[0] + v[1] + v[2] - g1 - g2 + y_prev(e1 - v[0]) + z_both(e2 - v[0])[1] - e1 - e2
    r1 = g1 - x_prev(g1, before[0]) + e1 + 2.0 * v[1] - v1_next - v1_prev - y_next(q2) + q2
    r2 = g2 - x_prev(g2, before[1]) + e2 + 2.0 * v[2] - y_next(v[2]) - y_prev(v[2]) - z_both(q1)[0] + q1
    return [shifted * v[0] + r0, shifted * v[1] + r1, shifted * v[2] + r2]


def halves(a):
    high = a.astype(BF16)
    return high, (a - high.astype(F32)).astype(BF16)


def enter_kernel(rate, coil_x, coil_y, coil_z, amp, field, ids, out, mass_out, flipped, padded, mass_pad):
    lane = lax.broadcasted_iota(jnp.int32, (64, LANES), 1)
    row = lax.broadcasted_iota(jnp.int32, (64, LANES), 0)
    classes = ids[...].reshape(64, LANES)
    mass = jnp.zeros((64, LANES), F32)
    for k in range(rate.shape[0]):
        mass = jnp.where(classes == k, rate[k], mass)
    left = lane < HALF
    flipped[...] = jnp.transpose(jnp.concatenate([mass, mass], axis=0))
    rows = jnp.where(left, flipped[pl.ds(0, 64, stride=2), :], flipped[pl.ds(1, 64, stride=2), :])
    mass_pad[0:8, :] = jnp.zeros((8, LANES), F32)
    mass_pad[8 * 65 :, :] = jnp.zeros((16, LANES), F32)
    for r in range(8):
        mass_pad[pl.ds(8 + r, 64, stride=8), :] = rows
    first = pl.multiple_of(lax.axis_index("rx") * 64, 64)
    mass_out[...] = mass_pad[pl.ds(first, 8 * GHOST), :].reshape(GHOST, 8, LANES) - SHIFT
    base = lax.axis_index("space") * 2

    def right(r, c):
        values = mass * field[r, c].reshape(64, LANES)
        if c == 2:
            return values
        near = coil_x[r] - base
        far = near + 1
        spot = jnp.where((near >= 0) & (near < 2), near * 32 + coil_y[r], -100)
        if c == 0:
            plus, minus = spot, spot + 1
        else:
            plus, minus = jnp.where((far >= 0) & (far < 2), far * 32 + coil_y[r], -100), spot
        strength = jnp.where(row == plus, amp[r], jnp.where(row == minus, -amp[r], 0.0))
        return values + jnp.where(lane == coil_z[r], strength, 0.0)

    for c in range(3):
        padded[0:8, :] = jnp.zeros((8, LANES), F32)
        padded[8 * 65 :, :] = jnp.zeros((16, LANES), F32)
        for r in range(4):
            flipped[...] = jnp.transpose(jnp.concatenate([right(r, c), right(r + 4, c)], axis=0))
            even = flipped[pl.ds(0, 64, stride=2), :]
            odd = flipped[pl.ds(1, 64, stride=2), :]
            padded[pl.ds(8 + r, 64, stride=8), :] = jnp.where(left, even, turn(odd, HALF))
            padded[pl.ds(12 + r, 64, stride=8), :] = jnp.where(left, turn(even, HALF), odd)
        for d in range(8):
            out[d, c] = padded[64 * d : 64 * d + 8 * GHOST, :].reshape(GHOST, 8, LANES)


def leave_kernel(tiles, out, gathered, flipped):
    left = lax.broadcasted_iota(jnp.int32, (64, LANES), 1) < HALF
    for c in range(3):
        for s in range(8):
            gathered[64 * s : 64 * s + 64, :] = tiles[s, c].reshape(64, LANES)
        for r in range(4):
            one = gathered[pl.ds(r, 64, stride=8), :]
            two = gathered[pl.ds(r + 4, 64, stride=8), :]
            flipped[pl.ds(0, 64, stride=2), :] = jnp.where(left, one, turn(two, HALF))
            flipped[pl.ds(1, 64, stride=2), :] = jnp.where(left, turn(one, HALF), two)
            back = jnp.transpose(flipped[...])
            out[r, c] = back[:64].reshape(2, PLANE, LANES)
            out[r + 4, c] = back[64:].reshape(2, PLANE, LANES)


def send_up(up, s, v, w, first, last):
    for c, (a, b) in enumerate(zip(slopes(v), slopes(w), strict=True)):
        up[s, c] = pack_up(a[first:last], b[first:last])


def send_down(down, s, v, w, first, last):
    for c in range(2):
        down[s, c] = pack_down(v[c + 1][first:last], w[c + 1][first:last])


def first_kernel(v0, up, down):
    def step(s, carry):
        v, w = ([v0[s + 4 * k, c] for c in range(3)] for k in range(2))
        send_up(up, s, v, w, 0, GHOST - 1)
        send_down(down, s, v, w, 0, GHOST - 1)
        return carry

    lax.fori_loop(0, 4, step, 0)


def inside(values, first_tile, last_tile):
    index = lax.axis_index("rx")
    rows = values.shape[0]
    low = jnp.where(index == 0, 0.0, 1.0)
    high = jnp.where(index == lax.axis_size("rx") - 1, 0.0, 1.0)
    pieces = [values]
    if first_tile:
        pieces = [values[:1] * low, values[1:]]
    if last_tile:
        pieces = [*pieces[:-1], pieces[-1][:-1], pieces[-1][-1:] * high]
    return jnp.concatenate(pieces, axis=0) if rows else values


def second_kernel(v0, mass, below, above, v1, up, down):
    def step(s, carry):
        fields = []
        for k in range(2):
            v = [v0[s + 4 * k, c] for c in range(3)]
            zero = jnp.zeros((1, 8, LANES), F32)
            beyond = [jnp.concatenate([unpack(above[s, c], k, False), zero], axis=0) for c in range(2)]
            before = [jnp.concatenate([unpack(below[s, c], k, True), zero], axis=0) for c in range(2)]
            result = apply_tiles(v, mass[...], beyond, before)
            result = [inside(r[: GHOST - 1], True, True) for r in result]
            for c in range(3):
                v1[s + 4 * k, c] = result[c]
            fields.append(result)
        send_up(up, s, *fields, 1, GHOST - 1)
        send_down(down, s, *fields, 0, GHOST - 1)
        return carry

    lax.fori_loop(0, 4, step, 0)


def third_kernel(v1, mass, below, above, v2, down):
    def step(s, carry):
        fields = []
        for k in range(2):
            v = [v1[s + 4 * k, c] for c in range(3)]
            zero = jnp.zeros((1, 8, LANES), F32)
            beyond = [unpack(above[s, c], k, False) for c in range(2)]
            before = [jnp.concatenate([zero, unpack(below[s, c], k, True)], axis=0) for c in range(2)]
            result = apply_tiles(v, mass[: GHOST - 1], beyond, before)
            result = [inside(r[1:], False, True) for r in result]
            for c in range(3):
                v2[s + 4 * k, c] = result[c]
            fields.append(result)
        send_down(down, s, *fields, 0, 8)
        return carry

    lax.fori_loop(0, 4, step, 0)


def columns(ref, c, first):
    return jnp.concatenate([ref[:, c, first + k].reshape(64, LANES) for k in range(2)], axis=1)


def moments_kernel(v0, v1, v2, out):
    total = jnp.zeros((192, 384), F32)
    for c in range(3):
        for k in range(0, 8, 2):
            stack = jnp.concatenate([columns(v0, c, k + 1), columns(v1, c, k + 1), columns(v2, c, k)], axis=0)
            high, low = halves(stack)
            total = total + lax.dot_general(
                high, jnp.concatenate([high, low], axis=0), NT, preferred_element_type=F32
            )
    main, cross = total[:, :192], total[:, 192:]

    def block(i, j):
        at = lambda m, p, q: m[64 * p : 64 * p + 64, 64 * q : 64 * q + 64]
        return at(main, i, j) + at(cross, i, j) + at(cross, j, i)

    out[0:64, :] = jnp.concatenate([block(0, 0), block(0, 1)], axis=1)
    out[64:128, :] = jnp.concatenate([block(1, 1), block(1, 2)], axis=1)
    out[128:192, :] = jnp.concatenate([block(2, 2), jnp.zeros((64, 64), F32)], axis=1)


def energy_kernel(v2, mass, above, moments, out, curl, scaled):
    y, x, parity = lane_ids()
    first_x = jnp.where((x == 0) & (lax.axis_index("space") == 0), 1.0, 0.0)
    first_y = jnp.where(y == 0, 1.0, 0.0)
    tile = lax.broadcasted_iota(jnp.int32, (8, 8, LANES), 0)
    first_z = jnp.where((tile == 0) & (parity == 0) & (lax.axis_index("rx") == 0), 1.0, 0.0)
    own = mass[1:9]
    faces = [first_y + first_z, first_x + first_z, first_x + first_y]

    def step(s, carry):
        for k in range(2):
            v = [v2[s + 4 * k, c] for c in range(3)]
            z1 = z_both(v[1])[0][:8]
            z0 = z_both(v[0])[0][:8]
            v = [a[:8] for a in v]
            x1 = x_next(v[1], unpack(above[s, 0], k, False))
            x2 = x_next(v[2], unpack(above[s, 1], k, False))
            curl[s + 4 * k, 0] = y_next(v[2]) - v[2] - z1 + v[1]
            curl[s + 4 * k, 1] = z0 - v[0] - x2 + v[2]
            curl[s + 4 * k, 2] = x1 - v[1] - y_next(v[0]) + v[0]
            for c in range(3):
                scaled[s + 4 * k, c] = v[c] * (own + faces[c])
        return carry

    lax.fori_loop(0, 4, step, 0)
    bends = jnp.zeros((64, 128), F32)
    mixed = jnp.zeros((128, 128), F32)
    for c in range(3):
        for k in range(0, 8, 2):
            high, low = halves(columns(curl, c, k))
            bends = bends + lax.dot_general(high, jnp.concatenate([high, low], axis=0), NT, preferred_element_type=F32)
            wide = jnp.concatenate(halves(columns(scaled, c, k)), axis=0)
            field = jnp.concatenate(halves(columns(v2, c, k)), axis=0)
            mixed = mixed + lax.dot_general(wide, field, NT, preferred_element_type=F32)
    last = bends[:, :64] + 2.0 * bends[:, 64:] + mixed[:64, :64] + mixed[:64, 64:] + mixed[64:, :64]
    out[0:128, :] = moments[0:128, :]
    out[128:192, :] = jnp.concatenate([moments[128:192, :64], last], axis=1)


def spread(a, lane):
    return jnp.broadcast_to(a[:, lane : lane + 1], (8, LANES))


def solve_tiles(tiles):
    sub = lax.broadcasted_iota(jnp.int32, (8, LANES), 0)
    origin = [list(pair) for pair in tiles]
    for p in range(24):
        side, lane0 = p // 16, 8 * (p % 16)
        sides = range(side, 2)
        rows = list(tiles[p])
        for k in range(8):
            lane = lane0 + k
            column = spread(rows[side], lane)
            pivot = jnp.broadcast_to(column[k : k + 1], (8, LANES))
            floor = jnp.broadcast_to(spread(origin[p][side], lane)[k : k + 1], (8, LANES)) * 2e-7
            inverse = jnp.where(pivot > floor, 1.0 / jnp.where(pivot > floor, pivot, 1.0), 0.0)
            for t in sides:
                scaled = jnp.broadcast_to(rows[t][k : k + 1], (8, LANES)) * inverse
                rows[t] = jnp.where(sub == k, scaled, rows[t] - column * scaled)
        tiles[p] = rows
        lines = [[jnp.broadcast_to(rows[t][k : k + 1], (8, LANES)) for k in range(8)] if t in sides else None for t in range(2)]
        for i in range(24):
            if i == p:
                continue
            factors = [spread(tiles[i][side], lane0 + k) for k in range(8)]
            new = list(tiles[i])
            for t in sides:
                one = factors[0] * lines[t][0]
                for k in range(1, 8):
                    one = one + factors[k] * lines[t][k]
                new[t] = new[t] - one
            tiles[i] = new
    return jnp.concatenate([pair[1] for pair in tiles], axis=0)


def finish_kernel(moments, v0, v1, v2, out):
    n = []
    for b in range(3):
        block = moments[64 * b : 64 * b + 64, :]
        other = jnp.transpose(jnp.concatenate([block, block], axis=0))
        n.append(0.5 * (block[:, :64] + other[:64, :64]))
        n.append(0.5 * (block[:, 64:] + other[64:, :64]))
    h = [n[m + 1] + SHIFT * n[m] for m in range(5)]
    tiles = []
    for i in range(3):
        lefts = jnp.concatenate([h[i], h[i + 1]], axis=1)
        rights = jnp.concatenate([h[i + 2], n[i]], axis=1)
        tiles += [[lefts[8 * j : 8 * j + 8], rights[8 * j : 8 * j + 8]] for j in range(8)]
    weights = jnp.transpose(solve_tiles(tiles))[64:]
    high, low = halves(weights)
    both = jnp.concatenate([high, low], axis=0)
    for c in range(3):
        for k in range(0, 8, 2):
            stack = jnp.concatenate([columns(v0, c, k + 1), columns(v1, c, k + 1), columns(v2, c, k)], axis=0)
            fine, rest = halves(stack)
            one = lax.dot_general(both, fine, NN, preferred_element_type=F32)
            two = lax.dot_general(high, rest, NN, preferred_element_type=F32)
            mixed = one[:64] + one[64:] + two
            for j in range(2):
                out[:, c, k + j] = mixed[:, LANES * j : LANES * j + LANES].reshape(8, 8, LANES)


def call(kernel, outs, scratch=(), smem=0, n_in=1, flops=0):
    single = not isinstance(outs, list)
    shapes = [outs] if single else outs
    vmem = pl.BlockSpec(memory_space=pltpu.VMEM)
    done = pl.pallas_call(
        kernel,
        out_shape=[jax.ShapeDtypeStruct(s, F32) for s in shapes],
        in_specs=[pl.BlockSpec(memory_space=pltpu.SMEM)] * smem + [vmem] * n_in,
        out_specs=[vmem] * len(shapes),
        scratch_shapes=[pltpu.VMEM(s, F32) for s in scratch],
        compiler_params=pltpu.CompilerParams(vmem_limit_bytes=48 * 1024 * 1024),
        cost_estimate=pl.CostEstimate(flops=flops, bytes_accessed=4 * 1024 * 1024, transcendentals=0),
    )
    return (lambda *a: done(*a)[0]) if single else done


def exchange(x, axis):
    return lax.all_to_all(x, axis, split_axis=0, concat_axis=0, tiled=True)


def reduce_bricks(parts):
    space, rx = (lax.axis_size("space"), lax.axis_size("rx"))
    rows = parts.shape[0]
    pieces = exchange(parts.reshape(space, rows // space, LANES), "space")
    own = jnp.sum(pieces, axis=0)
    pieces = exchange(jnp.broadcast_to(own[None], (rx, *own.shape)), "rx")
    own = jnp.sum(pieces, axis=0)
    pieces = exchange(jnp.broadcast_to(own[None], (space, *own.shape)), "space")
    return pieces.reshape(rows, LANES)


def body(lambda_next, class_ids, class_rate, coil_x, coil_y, coil_z, coil_amp):
    size = lax.axis_size("space")
    rise = [(i, i + 1) for i in range(size - 1)]
    fall = [(j, i) for i, j in rise]
    outgoing, mass = call(
        enter_kernel,
        [(8, 3, GHOST, 8, LANES), (GHOST, 8, LANES)],
        [(LANES, LANES), (67 * 8, LANES), (67 * 8, LANES)],
        smem=5,
        n_in=2,
    )(class_rate, coil_x, coil_y, coil_z, coil_amp, lambda_next, class_ids)
    v0 = exchange(outgoing, "rx")
    up, down = call(first_kernel, [(4, 2, 10, 8, LANES), (4, 2, 10, 8, LANES)])(v0)
    below = lax.ppermute(up, "space", rise)
    above = lax.ppermute(down, "space", fall)
    v1, up, down = call(second_kernel, [(8, 3, 10, 8, LANES), (4, 2, 9, 8, LANES), (4, 2, 10, 8, LANES)], n_in=4)(
        v0, mass, below, above
    )
    below = lax.ppermute(up, "space", rise)
    above = lax.ppermute(down, "space", fall)
    v2, down = call(third_kernel, [(8, 3, 9, 8, LANES), (4, 2, 8, 8, LANES)], n_in=4)(v1, mass, below, above)
    above = lax.ppermute(down, "space", fall)
    moments = call(moments_kernel, (192, LANES), n_in=3, flops=10**8)(v0, v1, v2)
    moments = call(energy_kernel, (192, LANES), [(8, 3, 8, 8, LANES)] * 2, n_in=4)(v2, mass, above, moments)
    moments = reduce_bricks(moments)
    mixed = call(finish_kernel, (8, 3, 8, 8, LANES), n_in=4)(moments, v0, v1, v2)
    mixed = exchange(mixed, "rx")
    return call(leave_kernel, (8, 3, 2, PLANE, LANES), [(512, LANES), (LANES, LANES)])(mixed)


def solution(mesh):
    in_specs = (
        P("rx", None, "space", None, None),
        P("space", None, None),
        P(),
        P("rx"),
        P("rx"),
        P("rx"),
        P("rx"),
    )
    out_specs = P("rx", None, "space", None, None)
    return jax.shard_map(body, mesh=mesh, in_specs=in_specs, out_specs=out_specs, check_vma=False)
```

profile of v0, /device:TPU:1, one launch (start us, length us, event | category | flops | bytes accessed | tf_op | source)
XLA Modules:
  0.0 177.1 jit_solution(226641578350731102)
XLA Ops:
  0.0 1.1 copy-done
  1.1 0.8 copy-done.1
  5.2 1.2 shard_map.73
  6.4 36.5 %all_to_all.25.v0 = f32[8,3,11,8,128]{4,3,2,1,0:T(8,128)S(1)} all-to-all(f32[8,3,11,8,128]{4,3,2,1,0:T(8,128)S(1)} %get-tuple-element.14), channel_id=1, replica_groups=mesh['space'=32,'rx'=8] {'rx'}, dimensions={0} | all-to-all | bytes 2162688 | tf_op jit(solution)/shard_map/all_to_all | solution.py:363
  42.9 0.8 shard_map.74
  43.7 5.7 %collective-permute-start = (f32[4,2,10,8,128]{4,3,2,1,0:T(8,128)S(1)}, f32[4,2,10,8,128]{4,3,2,1,0:T(8,128)S(1)}, u32[]{:S(2)}, u32[]{:S(2)}) collective-permute-start(f32[4,2,10,8,128]{4,3,2,1,0:T(8,128)S(1)} %get-tuple-element.16), channel_id=1, source_target_pairs={{0,8},{8,16},{16,24},{24,32},{32,40},{40,48},{48,56},{56,64},{64,7... | collective-permute-start | bytes 983048 | tf_op jit(solution)/shard_map/ppermute | solution.py:390
  49.4 1.9 %collective-permute-start.1 = (f32[4,2,10,8,128]{4,3,2,1,0:T(8,128)S(1)}, f32[4,2,10,8,128]{4,3,2,1,0:T(8,128)S(1)}, u32[]{:S(2)}, u32[]{:S(2)}) collective-permute-start(f32[4,2,10,8,128]{4,3,2,1,0:T(8,128)S(1)} %get-tuple-element.17), channel_id=1, source_target_pairs={{8,0},{16,8},{24,16},{32,24},{40,32},{48,40},{56,48},{64,56},{72,6... | collective-permute-start | bytes 983048 | tf_op jit(solution)/shard_map/ppermute | solution.py:391
  51.3 2.1 %collective-permute-done.below = f32[4,2,10,8,128]{4,3,2,1,0:T(8,128)S(1)} collective-permute-done((f32[4,2,10,8,128]{4,3,2,1,0:T(8,128)S(1)}, f32[4,2,10,8,128]{4,3,2,1,0:T(8,128)S(1)}, u32[]{:S(2)}, u32[]{:S(2)}) %collective-permute-start) | collective-permute-done | bytes 327712 | tf_op jit(solution)/shard_map/ppermute | solution.py:390
  53.4 4.4 %collective-permute-done.1.above = f32[4,2,10,8,128]{4,3,2,1,0:T(8,128)S(1)} collective-permute-done((f32[4,2,10,8,128]{4,3,2,1,0:T(8,128)S(1)}, f32[4,2,10,8,128]{4,3,2,1,0:T(8,128)S(1)}, u32[]{:S(2)}, u32[]{:S(2)}) %collective-permute-start.1) | collective-permute-done | bytes 327712 | tf_op jit(solution)/shard_map/ppermute | solution.py:391
  57.8 2.4 %shard_map.75 = (f32[8,3,10,8,128]{4,3,2,1,0:T(8,128)S(1)}, f32[4,2,9,8,128]{4,3,2,1,0:T(8,128)S(1)}, f32[4,2,10,8,128]{4,3,2,1,0:T(8,128)S(1)}) custom-call(f32[8,3,11,8,128]{4,3,2,1,0:T(8,128)S(1)} %all_to_all.25.v0, f32[11,8,128]{2,1,0:T(8,128)S(1)} %get-tuple-element.15.mass, f32[4,2,10,8,128]{4,3,2,1,0:T(8,128)S(1)} %collective-permute-done.below, ...), custom_call_target="tpu_custom_call" | custom-call | bytes 4194304 | tf_op jit(solution)/shard_map/pallas_call | solution.py:392
  60.2 1.9 %collective-permute-start.3 = (f32[4,2,10,8,128]{4,3,2,1,0:T(8,128)S(1)}, f32[4,2,10,8,128]{4,3,2,1,0:T(8,128)S(1)}, u32[]{:S(2)}, u32[]{:S(2)}) collective-permute-start(f32[4,2,10,8,128]{4,3,2,1,0:T(8,128)S(1)} %get-tuple-element.20), channel_id=1, source_target_pairs={{8,0},{16,8},{24,16},{32,24},{40,32},{48,40},{56,48},{64,56},{72,6... | collective-permute-start | bytes 983048 | tf_op jit(solution)/shard_map/ppermute | solution.py:396
  62.1 3.6 %collective-permute-start.2 = (f32[4,2,9,8,128]{4,3,2,1,0:T(8,128)S(1)}, f32[4,2,9,8,128]{4,3,2,1,0:T(8,128)S(1)}, u32[]{:S(2)}, u32[]{:S(2)}) collective-permute-start(f32[4,2,9,8,128]{4,3,2,1,0:T(8,128)S(1)} %get-tuple-element.19), channel_id=1, source_target_pairs={{0,8},{8,16},{16,24},{24,32},{32,40},{40,48},{48,56},{56,64},{64,7... | collective-permute-start | bytes 884744 | tf_op jit(solution)/shard_map/ppermute | solution.py:395
  65.7 3.6 %collective-permute-done.2.below = f32[4,2,9,8,128]{4,3,2,1,0:T(8,128)S(1)} collective-permute-done((f32[4,2,9,8,128]{4,3,2,1,0:T(8,128)S(1)}, f32[4,2,9,8,128]{4,3,2,1,0:T(8,128)S(1)}, u32[]{:S(2)}, u32[]{:S(2)}) %collective-permute-start.2) | collective-permute-done | bytes 294944 | tf_op jit(solution)/shard_map/ppermute | solution.py:395
  69.4 2.0 %shard_map.76 = (f32[8,3,9,8,128]{4,3,2,1,0:T(8,128)S(1)}, f32[4,2,8,8,128]{4,3,2,1,0:T(8,128)S(1)}) custom-call(f32[8,3,10,8,128]{4,3,2,1,0:T(8,128)S(1)} %get-tuple-element.18.v1, f32[11,8,128]{2,1,0:T(8,128)S(1)} %get-tuple-element.15.mass, f32[4,2,9,8,128]{4,3,2,1,0:T(8,128)S(1)} %collective-permute-done.2.below, ...), custom_call_target="tpu_custom_call" | custom-call | bytes 4194304 | tf_op jit(solution)/shard_map/pallas_call | solution.py:397
  71.4 1.9 %collective-permute-start.4 = (f32[4,2,8,8,128]{4,3,2,1,0:T(8,128)S(1)}, f32[4,2,8,8,128]{4,3,2,1,0:T(8,128)S(1)}, u32[]{:S(2)}, u32[]{:S(2)}) collective-permute-start(f32[4,2,8,8,128]{4,3,2,1,0:T(8,128)S(1)} %get-tuple-element.22), channel_id=1, source_target_pairs={{8,0},{16,8},{24,16},{32,24},{40,32},{48,40},{56,48},{64,56},{72,6... | collective-permute-start | bytes 786440 | tf_op jit(solution)/shard_map/ppermute | solution.py:398
  73.4 1.1 shard_map.77.moments
  74.4 5.4 %collective-permute-done.4.above = f32[4,2,8,8,128]{4,3,2,1,0:T(8,128)S(1)} collective-permute-done((f32[4,2,8,8,128]{4,3,2,1,0:T(8,128)S(1)}, f32[4,2,8,8,128]{4,3,2,1,0:T(8,128)S(1)}, u32[]{:S(2)}, u32[]{:S(2)}) %collective-permute-start.4) | collective-permute-done | bytes 262176 | tf_op jit(solution)/shard_map/ppermute | solution.py:398
  79.9 1.5 shard_map.78
  81.4 20.4 %all_to_all.26 = f32[32,6,128]{2,1,0:T(8,128)S(1)} all-to-all(f32[32,6,128]{2,1,0:T(8,128)S(1)} %reshape.8), channel_id=1, replica_groups=mesh['space'=32,'rx'=8] {'space'}, dimensions={0} | all-to-all | bytes 196608 | tf_op jit(solution)/shard_map/all_to_all | solution.py:363
  101.9 9.2 %all_to_all.27 = f32[8,6,128]{2,1,0:T(8,128)S(1)} all-to-all(f32[8,6,128]{2,1,0:T(8,128)S(1)} %broadcast_in_dim.4), channel_id=1, replica_groups=mesh['space'=32,'rx'=8] {'rx'}, dimensions={0} | all-to-all | bytes 49152 | tf_op jit(solution)/shard_map/all_to_all | solution.py:363
  111.2 12.4 %all_to_all.28 = f32[32,6,128]{2,1,0:T(8,128)S(1)} all-to-all(f32[32,6,128]{2,1,0:T(8,128)S(1)} %broadcast_in_dim.5), channel_id=1, replica_groups=mesh['space'=32,'rx'=8] {'space'}, dimensions={0} | all-to-all | bytes 196608 | tf_op jit(solution)/shard_map/all_to_all | solution.py:363
  123.6 26.1 %shard_map.79 = f32[8,3,8,8,128]{4,3,2,1,0:T(8,128)S(1)} custom-call(f32[192,128]{1,0:T(8,128)S(1)} %reshape.9.moments, f32[8,3,11,8,128]{4,3,2,1,0:T(8,128)S(1)} %all_to_all.25.v0, f32[8,3,10,8,128]{4,3,2,1,0:T(8,128)S(1)} %get-tuple-element.18.v1, f32[8,3,9,8,128]{4,3,2,1,0:T(8,128)S(1)} %get-tuple-element.21.v2), custom_call_target="tpu_custom_call" | custom-call | bytes 4194304 | tf_op jit(solution)/shard_map/pallas_call | solution.py:359
  149.7 26.0 %all_to_all.29.tiles = f32[8,3,8,8,128]{4,3,2,1,0:T(8,128)S(1)} all-to-all(f32[8,3,8,8,128]{4,3,2,1,0:T(8,128)S(1)} %shard_map.79), channel_id=1, replica_groups=mesh['space'=32,'rx'=8] {'rx'}, dimensions={0} | all-to-all | bytes 1572864 | tf_op jit(solution)/shard_map/all_to_all | solution.py:363
  175.7 1.5 shard_map.80
  (19 shorter events, 3.4 us)
Async XLA Ops:
  0.0 1.1 copy-start
  1.1 0.8 copy-start.1
  1.9 0.7 copy-start.2
  2.5 0.7 copy-start.3
  3.2 0.7 copy-start.4
  3.9 0.7 copy-start.5
  4.5 0.7 copy-start.6
  43.7 9.7 %collective-permute-start = (f32[4,2,10,8,128]{4,3,2,1,0:T(8,128)S(1)}, f32[4,2,10,8,128]{4,3,2,1,0:T(8,128)S(1)}, u32[]{:S(2)}, u32[]{:S(2)}) collective-permute-start(f32[4,2,10,8,128]{4,3,2,1,0:T(8,128)S(1)} %get-tuple-element.16), channel_id=1, source_target_pairs={{0,8},{8,16},{16,24},{24,32},{32,40},{40,48},{48,56},{56,64},{64,7... | collective-permute-start | bytes 983048 | tf_op jit(solution)/shard_map/ppermute | solution.py:390
  49.4 8.4 %collective-permute-start.1 = (f32[4,2,10,8,128]{4,3,2,1,0:T(8,128)S(1)}, f32[4,2,10,8,128]{4,3,2,1,0:T(8,128)S(1)}, u32[]{:S(2)}, u32[]{:S(2)}) collective-permute-start(f32[4,2,10,8,128]{4,3,2,1,0:T(8,128)S(1)} %get-tuple-element.17), channel_id=1, source_target_pairs={{8,0},{16,8},{24,16},{32,24},{40,32},{48,40},{56,48},{64,56},{72,6... | collective-permute-start | bytes 983048 | tf_op jit(solution)/shard_map/ppermute | solution.py:391
  60.2 9.2 %collective-permute-start.3 = (f32[4,2,10,8,128]{4,3,2,1,0:T(8,128)S(1)}, f32[4,2,10,8,128]{4,3,2,1,0:T(8,128)S(1)}, u32[]{:S(2)}, u32[]{:S(2)}) collective-permute-start(f32[4,2,10,8,128]{4,3,2,1,0:T(8,128)S(1)} %get-tuple-element.20), channel_id=1, source_target_pairs={{8,0},{16,8},{24,16},{32,24},{40,32},{48,40},{56,48},{64,56},{72,6... | collective-permute-start | bytes 983048 | tf_op jit(solution)/shard_map/ppermute | solution.py:396
  62.1 7.3 %collective-permute-start.2 = (f32[4,2,9,8,128]{4,3,2,1,0:T(8,128)S(1)}, f32[4,2,9,8,128]{4,3,2,1,0:T(8,128)S(1)}, u32[]{:S(2)}, u32[]{:S(2)}) collective-permute-start(f32[4,2,9,8,128]{4,3,2,1,0:T(8,128)S(1)} %get-tuple-element.19), channel_id=1, source_target_pairs={{0,8},{8,16},{16,24},{24,32},{32,40},{40,48},{48,56},{56,64},{64,7... | collective-permute-start | bytes 884744 | tf_op jit(solution)/shard_map/ppermute | solution.py:395
  71.4 8.4 %collective-permute-start.4 = (f32[4,2,8,8,128]{4,3,2,1,0:T(8,128)S(1)}, f32[4,2,8,8,128]{4,3,2,1,0:T(8,128)S(1)}, u32[]{:S(2)}, u32[]{:S(2)}) collective-permute-start(f32[4,2,8,8,128]{4,3,2,1,0:T(8,128)S(1)} %get-tuple-element.22), channel_id=1, source_target_pairs={{8,0},{16,8},{24,16},{32,24},{40,32},{48,40},{56,48},{64,56},{72,6... | collective-permute-start | bytes 786440 | tf_op jit(solution)/shard_map/ppermute | solution.py:398
where the time goes:
time: 178 us; the launch traced here: 177 us
  blocking collectives  105 us (59%)
  Pallas kernels  36.6 us (21%)
  waiting for transfers between devices  15.5 us (9%)
  starting transfers between devices  15.1 us (8%)
  local copies, waits for them, and re-layouts  5.21 us (3%)
    all_to_all x5, blocking collectives, exchange(): return lax.all_to_all(x, axis, split_axis=0, concat_axis=0, tiled=True)  105 us
    pallas_call x4, Pallas kernels, call(): return (lambda *a: done(*a)[0]) if single else done  30.2 us
    ppermute x3, waiting for transfers between devices, body(): above = lax.ppermute(down, 'space', fall)  9.83 us
    ppermute x2, starting transfers between devices, body(): below = lax.ppermute(up, 'space', rise)  9.33 us
    ppermute x3, starting transfers between devices, body(): above = lax.ppermute(down, 'space', fall)  5.76 us
    ppermute x2, waiting for transfers between devices, body(): below = lax.ppermute(up, 'space', rise)  5.71 us
    unnamed x14, local copies, waits for them, and re-layouts  5.16 us
  transfers between devices with their start and end apart: 5, of which 4 were waited for; matrix products, arithmetic and copies ran while one was open for 0% of the time, Pallas kernels for 1%

commit v1 on v0

--- a/solution.py
+++ b/solution.py
@@ -1,5 +1,3 @@
-import functools
-
 import jax
 import jax.numpy as jnp
 from jax import lax
@@ -85,7 +83,30 @@
     return high, (a - high.astype(F32)).astype(BF16)
 
 
-def enter_kernel(rate, coil_x, coil_y, coil_z, amp, field, ids, out, mass_out, flipped, padded, mass_pad):
+def thirds(a):
+    high = a.astype(BF16)
+    rest = a - high.astype(F32)
+    middle = rest.astype(BF16)
+    return high, middle, (rest - middle.astype(F32)).astype(BF16)
+
+
+def multiply(a, b):
+    ah, am, al = thirds(a)
+    bh, bm, bl = thirds(b)
+    left = jnp.concatenate([ah, ah, am, am, ah, al], axis=1)
+    right = jnp.concatenate([bh, bm, bh, bm, bl, bh], axis=0)
+    return lax.dot_general(left, right, NN, preferred_element_type=F32)
+
+
+def enter_kernel(*refs):
+    sources, (out, mass_out), rest = refs[:7], refs[7:9], refs[9:]
+    targets, (flipped, padded, mass_pad, sems) = rest[:7], rest[7:]
+    copies = [pltpu.make_async_copy(a, b, sems.at[i]) for i, (a, b) in enumerate(zip(sources, targets, strict=True))]
+    for copy in copies:
+        copy.start()
+    for copy in copies:
+        copy.wait()
+    field, ids, rate, coil_x, coil_y, coil_z, amp = targets
     lane = lax.broadcasted_iota(jnp.int32, (64, LANES), 1)
     row = lax.broadcasted_iota(jnp.int32, (64, LANES), 0)
     classes = ids[...].reshape(64, LANES)
@@ -145,21 +166,28 @@
             out[r + 4, c] = back[64:].reshape(2, PLANE, LANES)
 
 
-def send_up(up, s, v, w, first, last):
-    for c, (a, b) in enumerate(zip(slopes(v), slopes(w), strict=True)):
-        up[s, c] = pack_up(a[first:last], b[first:last])
-
-
-def send_down(down, s, v, w, first, last):
+def is_even():
+    return lax.axis_index("space") % 2 == 0
+
+
+def send(inner, outer, s, v, w, last):
+    even = is_even()
+    rises = [pack_up(a[:last], b[:last]) for a, b in zip(slopes(v), slopes(w), strict=True)]
     for c in range(2):
-        down[s, c] = pack_down(v[c + 1][first:last], w[c + 1][first:last])
-
-
-def first_kernel(v0, up, down):
+        falls = pack_down(v[c + 1][:last], w[c + 1][:last])
+        inner[s, c] = jnp.where(even, rises[c], falls)
+        outer[s, c] = jnp.where(even, falls, rises[c])
+
+
+def receive(inner, outer, s, c):
+    even = is_even()
+    return jnp.where(even, outer[s, c], inner[s, c]), jnp.where(even, inner[s, c], outer[s, c])
+
+
+def first_kernel(v0, inner, outer):
     def step(s, carry):
         v, w = ([v0[s + 4 * k, c] for c in range(3)] for k in range(2))
-        send_up(up, s, v, w, 0, GHOST - 1)
-        send_down(down, s, v, w, 0, GHOST - 1)
+        send(inner, outer, s, v, w, GHOST - 1)
         return carry
 
     lax.fori_loop(0, 4, step, 0)
@@ -178,40 +206,41 @@
     return jnp.concatenate(pieces, axis=0) if rows else values
 
 
-def second_kernel(v0, mass, below, above, v1, up, down):
+def second_kernel(v0, mass, inner, outer, v1, next_inner, next_outer):
     def step(s, carry):
         fields = []
+        below, above = zip(*(receive(inner, outer, s, c) for c in range(2)), strict=True)
         for k in range(2):
             v = [v0[s + 4 * k, c] for c in range(3)]
             zero = jnp.zeros((1, 8, LANES), F32)
-            beyond = [jnp.concatenate([unpack(above[s, c], k, False), zero], axis=0) for c in range(2)]
-            before = [jnp.concatenate([unpack(below[s, c], k, True), zero], axis=0) for c in range(2)]
+            beyond = [jnp.concatenate([unpack(above[c], k, False), zero], axis=0) for c in range(2)]
+            before = [jnp.concatenate([unpack(below[c], k, True), zero], axis=0) for c in range(2)]
             result = apply_tiles(v, mass[...], beyond, before)
             result = [inside(r[: GHOST - 1], True, True) for r in result]
             for c in range(3):
                 v1[s + 4 * k, c] = result[c]
             fields.append(result)
-        send_up(up, s, *fields, 1, GHOST - 1)
-        send_down(down, s, *fields, 0, GHOST - 1)
+        send(next_inner, next_outer, s, *fields, GHOST - 1)
         return carry
 
     lax.fori_loop(0, 4, step, 0)
 
 
-def third_kernel(v1, mass, below, above, v2, down):
+def third_kernel(v1, mass, inner, outer, v2, down):
     def step(s, carry):
         fields = []
+        below, above = zip(*(receive(inner, outer, s, c) for c in range(2)), strict=True)
         for k in range(2):
             v = [v1[s + 4 * k, c] for c in range(3)]
-            zero = jnp.zeros((1, 8, LANES), F32)
-            beyond = [unpack(above[s, c], k, False) for c in range(2)]
-            before = [jnp.concatenate([zero, unpack(below[s, c], k, True)], axis=0) for c in range(2)]
+            beyond = [unpack(above[c], k, False) for c in range(2)]
+            before = [unpack(below[c], k, True) for c in range(2)]
             result = apply_tiles(v, mass[: GHOST - 1], beyond, before)
             result = [inside(r[1:], False, True) for r in result]
             for c in range(3):
                 v2[s + 4 * k, c] = result[c]
             fields.append(result)
-        send_down(down, s, *fields, 0, 8)
+        for c in range(2):
+            down[s, c] = pack_down(fields[0][c + 1][:8], fields[1][c + 1][:8])
         return carry
 
     lax.fori_loop(0, 4, step, 0)
@@ -222,15 +251,17 @@
 
 
 def moments_kernel(v0, v1, v2, out):
-    total = jnp.zeros((192, 384), F32)
+    total = jnp.zeros((192, 576), F32)
+    middles = jnp.zeros((192, 192), F32)
     for c in range(3):
         for k in range(0, 8, 2):
             stack = jnp.concatenate([columns(v0, c, k + 1), columns(v1, c, k + 1), columns(v2, c, k)], axis=0)
-            high, low = halves(stack)
+            parts = thirds(stack)
             total = total + lax.dot_general(
-                high, jnp.concatenate([high, low], axis=0), NT, preferred_element_type=F32
+                parts[0], jnp.concatenate(parts, axis=0), NT, preferred_element_type=F32
             )
-    main, cross = total[:, :192], total[:, 192:]
+            middles = middles + lax.dot_general(parts[1], parts[1], NT, preferred_element_type=F32)
+    main, cross = total[:, :192] + middles, total[:, 192:384] + total[:, 384:]
 
     def block(i, j):
         at = lambda m, p, q: m[64 * p : 64 * p + 64, 64 * q : 64 * q + 64]
@@ -266,16 +297,18 @@
         return carry
 
     lax.fori_loop(0, 4, step, 0)
-    bends = jnp.zeros((64, 128), F32)
-    mixed = jnp.zeros((128, 128), F32)
+    bends = jnp.zeros((128, 192), F32)
+    mixed = jnp.zeros((192, 192), F32)
     for c in range(3):
         for k in range(0, 8, 2):
-            high, low = halves(columns(curl, c, k))
-            bends = bends + lax.dot_general(high, jnp.concatenate([high, low], axis=0), NT, preferred_element_type=F32)
-            wide = jnp.concatenate(halves(columns(scaled, c, k)), axis=0)
-            field = jnp.concatenate(halves(columns(v2, c, k)), axis=0)
+            parts = jnp.concatenate(thirds(columns(curl, c, k)), axis=0)
+            bends = bends + lax.dot_general(parts[:128], parts, NT, preferred_element_type=F32)
+            wide = jnp.concatenate(thirds(columns(scaled, c, k)), axis=0)
+            field = jnp.concatenate(thirds(columns(v2, c, k)), axis=0)
             mixed = mixed + lax.dot_general(wide, field, NT, preferred_element_type=F32)
-    last = bends[:, :64] + 2.0 * bends[:, 64:] + mixed[:64, :64] + mixed[:64, 64:] + mixed[64:, :64]
+    last = bends[:64, :64] + 2.0 * (bends[:64, 64:128] + bends[:64, 128:]) + bends[64:, 64:128]
+    for i, j in ((0, 0), (0, 1), (1, 0), (1, 1), (0, 2), (2, 0)):
+        last = last + mixed[64 * i : 64 * i + 64, 64 * j : 64 * j + 64]
     out[0:128, :] = moments[0:128, :]
     out[128:192, :] = jnp.concatenate([moments[128:192, :64], last], axis=1)
 
@@ -284,36 +317,58 @@
     return jnp.broadcast_to(a[:, lane : lane + 1], (8, LANES))
 
 
-def solve_tiles(tiles):
+def line(a, k):
+    return jnp.broadcast_to(a[k : k + 1], (8, LANES))
+
+
+def invert(matrix):
+    unit = lax.broadcasted_iota(jnp.int32, (64, 64), 0) == lax.broadcasted_iota(jnp.int32, (64, 64), 1)
+    both = jnp.concatenate([matrix, jnp.where(unit, 1.0, 0.0)], axis=1)
+    tiles = [both[8 * i : 8 * i + 8] for i in range(8)]
+    origin = list(tiles)
     sub = lax.broadcasted_iota(jnp.int32, (8, LANES), 0)
-    origin = [list(pair) for pair in tiles]
-    for p in range(24):
-        side, lane0 = p // 16, 8 * (p % 16)
-        sides = range(side, 2)
-        rows = list(tiles[p])
+    lane = lax.broadcasted_iota(jnp.int32, (8, LANES), 1)
+    zero = jnp.zeros((8, LANES), F32)
+    for p in range(8):
+        rows, first = tiles[p], 8 * p
+        cols = [spread(rows, first + k) for k in range(8)]
         for k in range(8):
-            lane = lane0 + k
-            column = spread(rows[side], lane)
-            pivot = jnp.broadcast_to(column[k : k + 1], (8, LANES))
-            floor = jnp.broadcast_to(spread(origin[p][side], lane)[k : k + 1], (8, LANES)) * 2e-7
-            inverse = jnp.where(pivot > floor, 1.0 / jnp.where(pivot > floor, pivot, 1.0), 0.0)
-            for t in sides:
-                scaled = jnp.broadcast_to(rows[t][k : k + 1], (8, LANES)) * inverse
-                rows[t] = jnp.where(sub == k, scaled, rows[t] - column * scaled)
+            floor = line(spread(origin[p], first + k), k) * 2e-7
+            pivot = line(cols[k], k)
+            sound = pivot > floor
+            inverse = jnp.where(sound, 1.0 / jnp.where(sound, pivot, 1.0), 0.0)
+            own, hit = cols[k], sub == k
+            for j in range(k + 1, 8):
+                scaled = line(cols[j], k) * inverse
+                cols[j] = jnp.where(hit, scaled, cols[j] - own * scaled)
+            scaled = line(rows, k) * inverse
+            rows = jnp.where(hit, scaled, rows - own * scaled)
         tiles[p] = rows
-        lines = [[jnp.broadcast_to(rows[t][k : k + 1], (8, LANES)) for k in range(8)] if t in sides else None for t in range(2)]
-        for i in range(24):
-            if i == p:
-                continue
-            factors = [spread(tiles[i][side], lane0 + k) for k in range(8)]
-            new = list(tiles[i])
-            for t in sides:
-                one = factors[0] * lines[t][0]
-                for k in range(1, 8):
-                    one = one + factors[k] * lines[t][k]
-                new[t] = new[t] - one
-            tiles[i] = new
-    return jnp.concatenate([pair[1] for pair in tiles], axis=0)
+        inside_panel = (lane >= first) & (lane < first + 8)
+        apart = [zero if i in (p, p + 1) else jnp.where(inside_panel, tiles[i], 0.0) for i in range(8)]
+        placed = [rows if i == p else zero for i in range(8)]
+        change = multiply(jnp.concatenate(apart, axis=0)[:, :64], jnp.concatenate(placed, axis=0))
+        for i in range(8):
+            if i == p + 1:
+                f = [spread(tiles[i], first + k) * line(rows, k) for k in range(8)]
+                tiles[i] = tiles[i] - (((f[0] + f[1]) + (f[2] + f[3])) + ((f[4] + f[5]) + (f[6] + f[7])))
+            elif i != p:
+                tiles[i] = tiles[i] - change[8 * i : 8 * i + 8]
+    return jnp.concatenate(tiles, axis=0)[:, 64:]
+
+
+def solve_blocks(n, h):
+    first = multiply(invert(h[0]), jnp.concatenate([h[1], h[2], n[0]], axis=1))
+    change = multiply(jnp.concatenate([h[1], h[2]], axis=0), first)
+    second = jnp.concatenate([h[2], h[3], n[1]], axis=1) - change[:64]
+    third = jnp.concatenate([h[3], h[4], n[2]], axis=1) - change[64:]
+    below = third[:, :64]
+    second = multiply(invert(second[:, :64]), second[:, 64:])
+    third = third[:, 64:] - multiply(below, second)
+    y2 = multiply(invert(third[:, :64]), third[:, 64:])
+    y1 = second[:, 64:] - multiply(second[:, :64], y2)
+    y0 = first[:, 128:] - multiply(first[:, :64], y1) - multiply(first[:, 64:128], y2)
+    return jnp.concatenate([y0, y1, y2], axis=0)
 
 
 def finish_kernel(moments, v0, v1, v2, out):
@@ -324,12 +379,8 @@
         n.append(0.5 * (block[:, :64] + other[:64, :64]))
         n.append(0.5 * (block[:, 64:] + other[64:, :64]))
     h = [n[m + 1] + SHIFT * n[m] for m in range(5)]
-    tiles = []
-    for i in range(3):
-        lefts = jnp.concatenate([h[i], h[i + 1]], axis=1)
-        rights = jnp.concatenate([h[i + 2], n[i]], axis=1)
-        tiles += [[lefts[8 * j : 8 * j + 8], rights[8 * j : 8 * j + 8]] for j in range(8)]
-    weights = jnp.transpose(solve_tiles(tiles))[64:]
+    solved = solve_blocks(n, h)
+    weights = jnp.transpose(jnp.concatenate([solved, solved], axis=1))[64:]
     high, low = halves(weights)
     both = jnp.concatenate([high, low], axis=0)
     for c in range(3):
@@ -343,16 +394,17 @@
                 out[:, c, k + j] = mixed[:, LANES * j : LANES * j + LANES].reshape(8, 8, LANES)
 
 
-def call(kernel, outs, scratch=(), smem=0, n_in=1, flops=0):
+def call(kernel, outs, scratch=(), n_in=1, flops=0, where=pltpu.VMEM):
     single = not isinstance(outs, list)
     shapes = [outs] if single else outs
     vmem = pl.BlockSpec(memory_space=pltpu.VMEM)
+    scratch = [pltpu.VMEM(a, F32) if isinstance(a, tuple) else a for a in scratch]
     done = pl.pallas_call(
         kernel,
         out_shape=[jax.ShapeDtypeStruct(s, F32) for s in shapes],
-        in_specs=[pl.BlockSpec(memory_space=pltpu.SMEM)] * smem + [vmem] * n_in,
+        in_specs=[pl.BlockSpec(memory_space=where)] * n_in,
         out_specs=[vmem] * len(shapes),
-        scratch_shapes=[pltpu.VMEM(s, F32) for s in scratch],
+        scratch_shapes=scratch,
         compiler_params=pltpu.CompilerParams(vmem_limit_bytes=48 * 1024 * 1024),
         cost_estimate=pl.CostEstimate(flops=flops, bytes_accessed=4 * 1024 * 1024, transcendentals=0),
     )
@@ -376,25 +428,28 @@
 
 def body(lambda_next, class_ids, class_rate, coil_x, coil_y, coil_z, coil_amp):
     size = lax.axis_size("space")
-    rise = [(i, i + 1) for i in range(size - 1)]
-    fall = [(j, i) for i, j in rise]
+    chips = [(i, i ^ 1) for i in range(size)]
+    fall = [(i + 1, i) for i in range(size - 1)]
+    beside = [pair for i in range(1, size - 1, 2) for pair in ((i, i + 1), (i + 1, i))]
+    arrays = (lambda_next, class_ids, class_rate, coil_x, coil_y, coil_z, coil_amp)
+    spaces = [pltpu.VMEM] * 2 + [pltpu.SMEM] * 5
     outgoing, mass = call(
         enter_kernel,
         [(8, 3, GHOST, 8, LANES), (GHOST, 8, LANES)],
-        [(LANES, LANES), (67 * 8, LANES), (67 * 8, LANES)],
-        smem=5,
-        n_in=2,
-    )(class_rate, coil_x, coil_y, coil_z, coil_amp, lambda_next, class_ids)
+        [space(a.shape, a.dtype) for space, a in zip(spaces, arrays, strict=True)]
+        + [(LANES, LANES), (67 * 8, LANES), (67 * 8, LANES), pltpu.SemaphoreType.DMA((7,))],
+        n_in=7,
+        where=pl.ANY,
+    )(*arrays)
     v0 = exchange(outgoing, "rx")
-    up, down = call(first_kernel, [(4, 2, 10, 8, LANES), (4, 2, 10, 8, LANES)])(v0)
-    below = lax.ppermute(up, "space", rise)
-    above = lax.ppermute(down, "space", fall)
-    v1, up, down = call(second_kernel, [(8, 3, 10, 8, LANES), (4, 2, 9, 8, LANES), (4, 2, 10, 8, LANES)], n_in=4)(
-        v0, mass, below, above
-    )
-    below = lax.ppermute(up, "space", rise)
-    above = lax.ppermute(down, "space", fall)
-    v2, down = call(third_kernel, [(8, 3, 9, 8, LANES), (4, 2, 8, 8, LANES)], n_in=4)(v1, mass, below, above)
+    message = (4, 2, 10, 8, LANES)
+    inner, outer = call(first_kernel, [message] * 2)(v0)
+    outer = lax.ppermute(outer, "space", beside)
+    inner = lax.ppermute(inner, "space", chips)
+    v1, inner, outer = call(second_kernel, [(8, 3, 10, 8, LANES), message, message], n_in=4)(v0, mass, inner, outer)
+    outer = lax.ppermute(outer, "space", beside)
+    inner = lax.ppermute(inner, "space", chips)
+    v2, down = call(third_kernel, [(8, 3, 9, 8, LANES), (4, 2, 8, 8, LANES)], n_in=4)(v1, mass, inner, outer)
     above = lax.ppermute(down, "space", fall)
     moments = call(moments_kernel, (192, LANES), n_in=3, flops=10**8)(v0, v1, v2)
     moments = call(energy_kernel, (192, LANES), [(8, 3, 8, 8, LANES)] * 2, n_in=4)(v2, mass, above, moments)

time: 178 us -> 156 us (0.88)
  Pallas kernels: 36.6 us -> 20.3 us
  starting transfers between devices: 15.1 us -> 11.3 us
    pallas_call x4, Pallas kernels: 30.2 us -> 13.7 us  [call(): return (lambda *a: done(*a)[0]) if single else done]
    ppermute x3 -> x1, waiting for transfers between devices: 9.83 us -> 3.87 us  [body(): above = lax.ppermute(down, 'space', fall)]
    ppermute x2 -> x4, waiting for transfers between devices: 5.71 us -> 10.2 us  [the longest x2 10.2 us: body(): outer = lax.ppermute(outer, 'space', beside)]
    ppermute x3 -> x1, starting transfers between devices: 5.76 us -> 1.92 us  [body(): above = lax.ppermute(down, 'space', fall)]
    ppermute x2 -> x4, starting transfers between devices: 9.33 us -> 9.37 us  [the longest x2 6.51 us: body(): outer = lax.ppermute(outer, 'space', beside)]
  transfers between devices with their start and end apart: 5 -> 5, of which waited for: 4 -> 3; matrix products, arithmetic and copies ran while one was open for 0% -> 0% of each run, Pallas kernels for 1% -> 1%
where the time goes in v1:
time: 156 us
  blocking collectives  105 us (67%)
  Pallas kernels  20.3 us (13%)
  waiting for transfers between devices  14.1 us (9%)
  starting transfers between devices  11.3 us (7%)
  local copies, waits for them, and re-layouts  5.21 us (3%)
    all_to_all x5, blocking collectives, exchange(): return lax.all_to_all(x, axis, split_axis=0, concat_axis=0, tiled=True)  105 us
    pallas_call x4, Pallas kernels, call(): return (lambda *a: done(*a)[0]) if single else done  13.7 us
    ppermute x2, waiting for transfers between devices, body(): outer = lax.ppermute(outer, 'space', beside)  10.2 us
    ppermute x2, starting transfers between devices, body(): outer = lax.ppermute(outer, 'space', beside)  6.51 us
    unnamed x14, local copies, waits for them, and re-layouts  5.16 us
    ppermute x1, waiting for transfers between devices, body(): above = lax.ppermute(down, 'space', fall)  3.87 us
  transfers between devices with their start and end apart: 5, of which 3 were waited for; matrix products, arithmetic and copies ran while one was open for 0% of the time, Pallas kernels for 1%

profile of v1, /device:TPU:1, one launch (start us, length us, event | category | flops | bytes accessed | tf_op | source)
XLA Modules:
  0.0 155.9 jit_solution(11876230169605310231)
XLA Ops:
  0.0 1.1 copy-done
  1.1 0.8 copy-done.1
  1.9 0.7 copy-done.2
  2.6 0.7 copy-done.3
  5.2 1.4 shard_map.73
  6.6 36.5 %all_to_all.25.v0 = f32[8,3,11,8,128]{4,3,2,1,0:T(8,128)S(1)} all-to-all(f32[8,3,11,8,128]{4,3,2,1,0:T(8,128)S(1)} %get-tuple-element.14), channel_id=1, replica_groups=mesh['space'=32,'rx'=8] {'rx'}, dimensions={0} | all-to-all | bytes 2162688 | tf_op jit(solution)/shard_map/all_to_all | solution.py:415
  43.1 0.8 shard_map.74
  43.9 2.8 %collective-permute-start = (f32[4,2,10,8,128]{4,3,2,1,0:T(8,128)S(1)}, f32[4,2,10,8,128]{4,3,2,1,0:T(8,128)S(1)}, u32[]{:S(2)}, u32[]{:S(2)}) collective-permute-start(f32[4,2,10,8,128]{4,3,2,1,0:T(8,128)S(1)} %get-tuple-element.16), channel_id=1, source_target_pairs={{0,8},{8,0},{16,24},{24,16},{32,40},{40,32},{48,56},{56,48},{64,72... | collective-permute-start | bytes 983048 | tf_op jit(solution)/shard_map/ppermute | solution.py:448
  46.6 3.0 %collective-permute-start.1 = (f32[4,2,10,8,128]{4,3,2,1,0:T(8,128)S(1)}, f32[4,2,10,8,128]{4,3,2,1,0:T(8,128)S(1)}, u32[]{:S(2)}, u32[]{:S(2)}) collective-permute-start(f32[4,2,10,8,128]{4,3,2,1,0:T(8,128)S(1)} %get-tuple-element.17), channel_id=1, source_target_pairs={{8,16},{16,8},{24,32},{32,24},{40,48},{48,40},{56,64},{64,56},{72,... | collective-permute-start | bytes 983048 | tf_op jit(solution)/shard_map/ppermute | solution.py:447
  49.7 5.3 %collective-permute-done.1.outer = f32[4,2,10,8,128]{4,3,2,1,0:T(8,128)S(1)} collective-permute-done((f32[4,2,10,8,128]{4,3,2,1,0:T(8,128)S(1)}, f32[4,2,10,8,128]{4,3,2,1,0:T(8,128)S(1)}, u32[]{:S(2)}, u32[]{:S(2)}) %collective-permute-start.1) | collective-permute-done | bytes 327712 | tf_op jit(solution)/shard_map/ppermute | solution.py:447
  55.0 2.5 %shard_map.75 = (f32[8,3,10,8,128]{4,3,2,1,0:T(8,128)S(1)}, f32[4,2,10,8,128]{4,3,2,1,0:T(8,128)S(1)}, f32[4,2,10,8,128]{4,3,2,1,0:T(8,128)S(1)}) custom-call(f32[8,3,11,8,128]{4,3,2,1,0:T(8,128)S(1)} %all_to_all.25.v0, f32[11,8,128]{2,1,0:T(8,128)S(1)} %get-tuple-element.15.mass, f32[4,2,10,8,128]{4,3,2,1,0:T(8,128)S(1)} %collective-permute-done.inner, ...), custom_call_target="tpu_custom_call" | custom-call | bytes 4194304 | tf_op jit(solution)/shard_map/pallas_call | solution.py:449
  57.6 3.5 %collective-permute-start.3 = (f32[4,2,10,8,128]{4,3,2,1,0:T(8,128)S(1)}, f32[4,2,10,8,128]{4,3,2,1,0:T(8,128)S(1)}, u32[]{:S(2)}, u32[]{:S(2)}) collective-permute-start(f32[4,2,10,8,128]{4,3,2,1,0:T(8,128)S(1)} %get-tuple-element.20), channel_id=1, source_target_pairs={{8,16},{16,8},{24,32},{32,24},{40,48},{48,40},{56,64},{64,56},{72,... | collective-permute-start | bytes 983048 | tf_op jit(solution)/shard_map/ppermute | solution.py:450
  61.1 4.9 %collective-permute-done.3.outer = f32[4,2,10,8,128]{4,3,2,1,0:T(8,128)S(1)} collective-permute-done((f32[4,2,10,8,128]{4,3,2,1,0:T(8,128)S(1)}, f32[4,2,10,8,128]{4,3,2,1,0:T(8,128)S(1)}, u32[]{:S(2)}, u32[]{:S(2)}) %collective-permute-start.3) | collective-permute-done | bytes 327712 | tf_op jit(solution)/shard_map/ppermute | solution.py:450
  66.0 2.1 %shard_map.76 = (f32[8,3,9,8,128]{4,3,2,1,0:T(8,128)S(1)}, f32[4,2,8,8,128]{4,3,2,1,0:T(8,128)S(1)}) custom-call(f32[8,3,10,8,128]{4,3,2,1,0:T(8,128)S(1)} %get-tuple-element.18.v1, f32[11,8,128]{2,1,0:T(8,128)S(1)} %get-tuple-element.15.mass, f32[4,2,10,8,128]{4,3,2,1,0:T(8,128)S(1)} %collective-permute-done.2.inner, ...), custom_call_target="tpu_custom_call" | custom-call | bytes 4194304 | tf_op jit(solution)/shard_map/pallas_call | solution.py:452
  68.0 1.9 %collective-permute-start.4 = (f32[4,2,8,8,128]{4,3,2,1,0:T(8,128)S(1)}, f32[4,2,8,8,128]{4,3,2,1,0:T(8,128)S(1)}, u32[]{:S(2)}, u32[]{:S(2)}) collective-permute-start(f32[4,2,8,8,128]{4,3,2,1,0:T(8,128)S(1)} %get-tuple-element.22), channel_id=1, source_target_pairs={{8,0},{16,8},{24,16},{32,24},{40,32},{48,40},{56,48},{64,56},{72,6... | collective-permute-start | bytes 786440 | tf_op jit(solution)/shard_map/ppermute | solution.py:453
  70.0 1.9 %shard_map.77.moments = f32[192,128]{1,0:T(8,128)S(1)} custom-call(f32[8,3,11,8,128]{4,3,2,1,0:T(8,128)S(1)} %all_to_all.25.v0, f32[8,3,10,8,128]{4,3,2,1,0:T(8,128)S(1)} %get-tuple-element.18.v1, f32[8,3,9,8,128]{4,3,2,1,0:T(8,128)S(1)} %get-tuple-element.21.v2), custom_call_target="tpu_custom_call" | custom-call | flops 100000000 | bytes 4194304 | tf_op jit(solution)/shard_map/pallas_call | solution.py:411
  71.9 3.9 %collective-permute-done.4.above = f32[4,2,8,8,128]{4,3,2,1,0:T(8,128)S(1)} collective-permute-done((f32[4,2,8,8,128]{4,3,2,1,0:T(8,128)S(1)}, f32[4,2,8,8,128]{4,3,2,1,0:T(8,128)S(1)}, u32[]{:S(2)}, u32[]{:S(2)}) %collective-permute-start.4) | collective-permute-done | bytes 262176 | tf_op jit(solution)/shard_map/ppermute | solution.py:453
  75.7 1.8 %shard_map.78 = f32[192,128]{1,0:T(8,128)S(1)} custom-call(f32[8,3,9,8,128]{4,3,2,1,0:T(8,128)S(1)} %get-tuple-element.21.v2, f32[11,8,128]{2,1,0:T(8,128)S(1)} %get-tuple-element.15.mass, f32[4,2,8,8,128]{4,3,2,1,0:T(8,128)S(1)} %collective-permute-done.4.above, f32[192,128]{1,0:T(8,128)S(1)} %shard_map.77.moments), custom_call_target="tpu_custom_call" | custom-call | bytes 4194304 | tf_op jit(solution)/shard_map/pallas_call | solution.py:411
  77.6 20.7 %all_to_all.26 = f32[32,6,128]{2,1,0:T(8,128)S(1)} all-to-all(f32[32,6,128]{2,1,0:T(8,128)S(1)} %reshape.8), channel_id=1, replica_groups=mesh['space'=32,'rx'=8] {'space'}, dimensions={0} | all-to-all | bytes 196608 | tf_op jit(solution)/shard_map/all_to_all | solution.py:415
  98.3 9.2 %all_to_all.27 = f32[8,6,128]{2,1,0:T(8,128)S(1)} all-to-all(f32[8,6,128]{2,1,0:T(8,128)S(1)} %broadcast_in_dim.4), channel_id=1, replica_groups=mesh['space'=32,'rx'=8] {'rx'}, dimensions={0} | all-to-all | bytes 49152 | tf_op jit(solution)/shard_map/all_to_all | solution.py:415
  107.6 12.4 %all_to_all.28 = f32[32,6,128]{2,1,0:T(8,128)S(1)} all-to-all(f32[32,6,128]{2,1,0:T(8,128)S(1)} %broadcast_in_dim.5), channel_id=1, replica_groups=mesh['space'=32,'rx'=8] {'space'}, dimensions={0} | all-to-all | bytes 196608 | tf_op jit(solution)/shard_map/all_to_all | solution.py:415
  120.0 8.5 %shard_map.79 = f32[8,3,8,8,128]{4,3,2,1,0:T(8,128)S(1)} custom-call(f32[192,128]{1,0:T(8,128)S(1)} %reshape.9.moments, f32[8,3,11,8,128]{4,3,2,1,0:T(8,128)S(1)} %all_to_all.25.v0, f32[8,3,10,8,128]{4,3,2,1,0:T(8,128)S(1)} %get-tuple-element.18.v1, f32[8,3,9,8,128]{4,3,2,1,0:T(8,128)S(1)} %get-tuple-element.21.v2), custom_call_target="tpu_custom_call" | custom-call | bytes 4194304 | tf_op jit(solution)/shard_map/pallas_call | solution.py:411
  128.5 26.0 %all_to_all.29.tiles = f32[8,3,8,8,128]{4,3,2,1,0:T(8,128)S(1)} all-to-all(f32[8,3,8,8,128]{4,3,2,1,0:T(8,128)S(1)} %shard_map.79), channel_id=1, replica_groups=mesh['space'=32,'rx'=8] {'rx'}, dimensions={0} | all-to-all | bytes 1572864 | tf_op jit(solution)/shard_map/all_to_all | solution.py:415
  154.5 1.5 shard_map.80
  (19 shorter events, 2.2 us)
Async XLA Ops:
  0.0 1.1 copy-start
  1.1 0.8 copy-start.1
  1.9 0.7 copy-start.2
  2.5 0.7 copy-start.3
  3.2 0.7 copy-start.4
  3.9 0.7 copy-start.5
  4.5 0.7 copy-start.6
  43.9 5.8 %collective-permute-start = (f32[4,2,10,8,128]{4,3,2,1,0:T(8,128)S(1)}, f32[4,2,10,8,128]{4,3,2,1,0:T(8,128)S(1)}, u32[]{:S(2)}, u32[]{:S(2)}) collective-permute-start(f32[4,2,10,8,128]{4,3,2,1,0:T(8,128)S(1)} %get-tuple-element.16), channel_id=1, source_target_pairs={{0,8},{8,0},{16,24},{24,16},{32,40},{40,32},{48,56},{56,48},{64,72... | collective-permute-start | bytes 983048 | tf_op jit(solution)/shard_map/ppermute | solution.py:448
  46.6 8.4 %collective-permute-start.1 = (f32[4,2,10,8,128]{4,3,2,1,0:T(8,128)S(1)}, f32[4,2,10,8,128]{4,3,2,1,0:T(8,128)S(1)}, u32[]{:S(2)}, u32[]{:S(2)}) collective-permute-start(f32[4,2,10,8,128]{4,3,2,1,0:T(8,128)S(1)} %get-tuple-element.17), channel_id=1, source_target_pairs={{8,16},{16,8},{24,32},{32,24},{40,48},{48,40},{56,64},{64,56},{72,... | collective-permute-start | bytes 983048 | tf_op jit(solution)/shard_map/ppermute | solution.py:447
  57.5 3.6 %collective-permute-start.2 = (f32[4,2,10,8,128]{4,3,2,1,0:T(8,128)S(1)}, f32[4,2,10,8,128]{4,3,2,1,0:T(8,128)S(1)}, u32[]{:S(2)}, u32[]{:S(2)}) collective-permute-start(f32[4,2,10,8,128]{4,3,2,1,0:T(8,128)S(1)} %get-tuple-element.19), channel_id=1, source_target_pairs={{0,8},{8,0},{16,24},{24,16},{32,40},{40,32},{48,56},{56,48},{64,72... | collective-permute-start | bytes 983048 | tf_op jit(solution)/shard_map/ppermute | solution.py:451
  57.6 8.4 %collective-permute-start.3 = (f32[4,2,10,8,128]{4,3,2,1,0:T(8,128)S(1)}, f32[4,2,10,8,128]{4,3,2,1,0:T(8,128)S(1)}, u32[]{:S(2)}, u32[]{:S(2)}) collective-permute-start(f32[4,2,10,8,128]{4,3,2,1,0:T(8,128)S(1)} %get-tuple-element.20), channel_id=1, source_target_pairs={{8,16},{16,8},{24,32},{32,24},{40,48},{48,40},{56,64},{64,56},{72,... | collective-permute-start | bytes 983048 | tf_op jit(solution)/shard_map/ppermute | solution.py:450
  68.0 7.7 %collective-permute-start.4 = (f32[4,2,8,8,128]{4,3,2,1,0:T(8,128)S(1)}, f32[4,2,8,8,128]{4,3,2,1,0:T(8,128)S(1)}, u32[]{:S(2)}, u32[]{:S(2)}) collective-permute-start(f32[4,2,8,8,128]{4,3,2,1,0:T(8,128)S(1)} %get-tuple-element.22), channel_id=1, source_target_pairs={{8,0},{16,8},{24,16},{32,24},{40,32},{48,40},{56,48},{64,56},{72,6... | collective-permute-start | bytes 786440 | tf_op jit(solution)/shard_map/ppermute | solution.py:453

commit v2 on v1

--- a/solution.py
+++ b/solution.py
@@ -1,3 +1,5 @@
+import functools
+
 import jax
 import jax.numpy as jnp
 from jax import lax
@@ -56,25 +58,25 @@
 
 
 def unpack(m, second, up):
-    if second:
-        return m
-    return turn(m, LANES - PLANE) if up else turn(m, PLANE)
+    if not second:
+        m = turn(m, LANES - PLANE) if up else turn(m, PLANE)
+    return jnp.where(lane_ids()[1] == (0 if up else 1), m, 0.0)
 
 
 def slopes(v):
     return v[1] + y_next(v[0]) - v[0], v[2] + z_both(v[0])[0] - v[0]
 
 
-def apply_tiles(v, shifted, beyond, before):
+def apply_tiles(v, shifted):
     g1, g2 = slopes(v)
-    e1 = v[1] - x_next(v[1], beyond[0])
-    e2 = v[2] - x_next(v[2], beyond[1])
+    e1 = v[1] - x_next(v[1], 0.0)
+    e2 = v[2] - x_next(v[2], 0.0)
     q2 = z_both(v[2])[1] - v[2]
     q1 = y_prev(v[1]) - v[1]
     v1_next, v1_prev = z_both(v[1])
     r0 = 2.0 * v[0] + v[1] + v[2] - g1 - g2 + y_prev(e1 - v[0]) + z_both(e2 - v[0])[1] - e1 - e2
-    r1 = g1 - x_prev(g1, before[0]) + e1 + 2.0 * v[1] - v1_next - v1_prev - y_next(q2) + q2
-    r2 = g2 - x_prev(g2, before[1]) + e2 + 2.0 * v[2] - y_next(v[2]) - y_prev(v[2]) - z_both(q1)[0] + q1
+    r1 = g1 - x_prev(g1, 0.0) + e1 + 2.0 * v[1] - v1_next - v1_prev - y_next(q2) + q2
+    r2 = g2 - x_prev(g2, 0.0) + e2 + 2.0 * v[2] - y_next(v[2]) - y_prev(v[2]) - z_both(q1)[0] + q1
     return [shifted * v[0] + r0, shifted * v[1] + r1, shifted * v[2] + r2]
 
 
@@ -170,27 +172,32 @@
     return lax.axis_index("space") % 2 == 0
 
 
-def send(inner, outer, s, v, w, last):
-    even = is_even()
-    rises = [pack_up(a[:last], b[:last]) for a, b in zip(slopes(v), slopes(w), strict=True)]
-    for c in range(2):
-        falls = pack_down(v[c + 1][:last], w[c + 1][:last])
-        inner[s, c] = jnp.where(even, rises[c], falls)
-        outer[s, c] = jnp.where(even, falls, rises[c])
+def send(message, to_above, s, v, w):
+    last = GHOST - 1
+
+    @pl.when(to_above)
+    def _():
+        for c, (a, b) in enumerate(zip(slopes(v), slopes(w), strict=True)):
+            message[s, c] = pack_up(a[:last], b[:last])
+
+    @pl.when(jnp.logical_not(to_above))
+    def _():
+        for c in range(2):
+            message[s, c] = pack_down(v[c + 1][:last], w[c + 1][:last])
+
+
+def message_kernel(outer, v, message):
+    def step(s, carry):
+        fields = [[v[s + 4 * k, c] for c in range(3)] for k in range(2)]
+        send(message, is_even() != outer, s, *fields)
+        return carry
+
+    lax.fori_loop(0, 4, step, 0)
 
 
 def receive(inner, outer, s, c):
     even = is_even()
     return jnp.where(even, outer[s, c], inner[s, c]), jnp.where(even, inner[s, c], outer[s, c])
-
-
-def first_kernel(v0, inner, outer):
-    def step(s, carry):
-        v, w = ([v0[s + 4 * k, c] for c in range(3)] for k in range(2))
-        send(inner, outer, s, v, w, GHOST - 1)
-        return carry
-
-    lax.fori_loop(0, 4, step, 0)
 
 
 def inside(values, first_tile, last_tile):
@@ -206,39 +213,49 @@
     return jnp.concatenate(pieces, axis=0) if rows else values
 
 
-def second_kernel(v0, mass, inner, outer, v1, next_inner, next_outer):
+def base_kernel(first, v, mass, base, inner):
     def step(s, carry):
-        fields = []
-        below, above = zip(*(receive(inner, outer, s, c) for c in range(2)), strict=True)
+        fields = [[v[s + 4 * k, c] for c in range(3)] for k in range(2)]
         for k in range(2):
-            v = [v0[s + 4 * k, c] for c in range(3)]
-            zero = jnp.zeros((1, 8, LANES), F32)
-            beyond = [jnp.concatenate([unpack(above[c], k, False), zero], axis=0) for c in range(2)]
-            before = [jnp.concatenate([unpack(below[c], k, True), zero], axis=0) for c in range(2)]
-            result = apply_tiles(v, mass[...], beyond, before)
-            result = [inside(r[: GHOST - 1], True, True) for r in result]
+            result = apply_tiles(fields[k], mass[: v.shape[2]])
             for c in range(3):
-                v1[s + 4 * k, c] = result[c]
-            fields.append(result)
-        send(next_inner, next_outer, s, *fields, GHOST - 1)
+                base[s + 4 * k, c] = result[c][first : first + base.shape[2]]
+        send(inner, is_even(), s, *fields)
         return carry
 
     lax.fori_loop(0, 4, step, 0)
 
 
-def third_kernel(v1, mass, inner, outer, v2, down):
+def completed(base, inner, outer, s, k, first):
+    below, above = zip(*(receive(inner, outer, s, c) for c in range(2)), strict=True)
+    beyond = [unpack(a, k, False) for a in above]
+    before = [unpack(a, k, True) for a in below]
+    changes = [
+        beyond[0] + beyond[1] - y_prev(beyond[0]) - z_both(beyond[1])[1],
+        -beyond[0] - before[0],
+        -beyond[1] - before[1],
+    ]
+    return [inside(base[s + 4 * k, c] + changes[c][first:], first == 0, True) for c in range(3)]
+
+
+def second_kernel(outer, base, inner, v1, next_outer):
     def step(s, carry):
-        fields = []
-        below, above = zip(*(receive(inner, outer, s, c) for c in range(2)), strict=True)
+        fields = [completed(base, inner, outer, s, k, 0) for k in range(2)]
         for k in range(2):
-            v = [v1[s + 4 * k, c] for c in range(3)]
-            beyond = [unpack(above[c], k, False) for c in range(2)]
-            before = [unpack(below[c], k, True) for c in range(2)]
-            result = apply_tiles(v, mass[: GHOST - 1], beyond, before)
-            result = [inside(r[1:], False, True) for r in result]
             for c in range(3):
-                v2[s + 4 * k, c] = result[c]
-            fields.append(result)
+                v1[s + 4 * k, c] = fields[k][c]
+        send(next_outer, jnp.logical_not(is_even()), s, *fields)
+        return carry
+
+    lax.fori_loop(0, 4, step, 0)
+
+
+def third_kernel(outer, base, inner, v2, down):
+    def step(s, carry):
+        fields = [completed(base, inner, outer, s, k, 1) for k in range(2)]
+        for k in range(2):
+            for c in range(3):
+                v2[s + 4 * k, c] = fields[k][c]
         for c in range(2):
             down[s, c] = pack_down(fields[0][c + 1][:8], fields[1][c + 1][:8])
         return carry
@@ -250,7 +267,38 @@
     return jnp.concatenate([ref[:, c, first + k].reshape(64, LANES) for k in range(2)], axis=1)
 
 
-def moments_kernel(v0, v1, v2, out):
+def bend(parts):
+    return lax.dot_general(parts[:128], parts, NT, preferred_element_type=F32)
+
+
+def fold(bends):
+    return bends[:64, :64] + 2.0 * (bends[:64, 64:128] + bends[:64, 128:]) + bends[64:, 64:128]
+
+
+def moments_kernel(v0, v1, v2, mass, out, curl, curl0, scaled):
+    y, x, parity = lane_ids()
+    first_x = jnp.where((x == 0) & (lax.axis_index("space") == 0), 1.0, 0.0)
+    first_y = jnp.where(y == 0, 1.0, 0.0)
+    tile = lax.broadcasted_iota(jnp.int32, (8, 8, LANES), 0)
+    first_z = jnp.where((tile == 0) & (parity == 0) & (lax.axis_index("rx") == 0), 1.0, 0.0)
+    own = mass[1:9]
+    faces = [first_y + first_z, first_x + first_z, first_x + first_y]
+
+    def step(s, carry):
+        v = [v2[s, c] for c in range(3)]
+        z1 = z_both(v[1])[0][:8]
+        z0 = z_both(v[0])[0][:8]
+        v = [a[:8] for a in v]
+        curl0[s, 0] = y_next(v[2]) - v[2] - z1 + v[1]
+        curl[s, 0] = z0 - v[0] - x_next(v[2], 0.0) + v[2]
+        curl[s, 1] = x_next(v[1], 0.0) - v[1] - y_next(v[0]) + v[0]
+        for c in range(3):
+            scaled[s, c] = v[c] * (own + faces[c])
+        return carry
+
+    lax.fori_loop(0, 8, step, 0)
+    bends = jnp.zeros((128, 192), F32)
+    mixed = jnp.zeros((192, 192), F32)
     total = jnp.zeros((192, 576), F32)
     middles = jnp.zeros((192, 192), F32)
     for c in range(3):
@@ -261,7 +309,15 @@
                 parts[0], jnp.concatenate(parts, axis=0), NT, preferred_element_type=F32
             )
             middles = middles + lax.dot_general(parts[1], parts[1], NT, preferred_element_type=F32)
+            wide = jnp.concatenate(thirds(columns(scaled, c, k)), axis=0)
+            field = jnp.concatenate([a[128:] for a in parts], axis=0)
+            mixed = mixed + lax.dot_general(wide, field, NT, preferred_element_type=F32)
+            if c == 0:
+                bends = bends + bend(jnp.concatenate(thirds(columns(curl0, c, k)), axis=0))
     main, cross = total[:, :192] + middles, total[:, 192:384] + total[:, 384:]
+    last = fold(bends)
+    for i, j in ((0, 0), (0, 1), (1, 0), (1, 1), (0, 2), (2, 0)):
+        last = last + mixed[64 * i : 64 * i + 64, 64 * j : 64 * j + 64]
 
     def block(i, j):
         at = lambda m, p, q: m[64 * p : 64 * p + 64, 64 * q : 64 * q + 64]
@@ -269,48 +325,21 @@
 
     out[0:64, :] = jnp.concatenate([block(0, 0), block(0, 1)], axis=1)
     out[64:128, :] = jnp.concatenate([block(1, 1), block(1, 2)], axis=1)
-    out[128:192, :] = jnp.concatenate([block(2, 2), jnp.zeros((64, 64), F32)], axis=1)
-
-
-def energy_kernel(v2, mass, above, moments, out, curl, scaled):
-    y, x, parity = lane_ids()
-    first_x = jnp.where((x == 0) & (lax.axis_index("space") == 0), 1.0, 0.0)
-    first_y = jnp.where(y == 0, 1.0, 0.0)
-    tile = lax.broadcasted_iota(jnp.int32, (8, 8, LANES), 0)
-    first_z = jnp.where((tile == 0) & (parity == 0) & (lax.axis_index("rx") == 0), 1.0, 0.0)
-    own = mass[1:9]
-    faces = [first_y + first_z, first_x + first_z, first_x + first_y]
-
-    def step(s, carry):
-        for k in range(2):
-            v = [v2[s + 4 * k, c] for c in range(3)]
-            z1 = z_both(v[1])[0][:8]
-            z0 = z_both(v[0])[0][:8]
-            v = [a[:8] for a in v]
-            x1 = x_next(v[1], unpack(above[s, 0], k, False))
-            x2 = x_next(v[2], unpack(above[s, 1], k, False))
-            curl[s + 4 * k, 0] = y_next(v[2]) - v[2] - z1 + v[1]
-            curl[s + 4 * k, 1] = z0 - v[0] - x2 + v[2]
-            curl[s + 4 * k, 2] = x1 - v[1] - y_next(v[0]) + v[0]
-            for c in range(3):
-                scaled[s + 4 * k, c] = v[c] * (own + faces[c])
-        return carry
-
-    lax.fori_loop(0, 4, step, 0)
+    out[128:192, :] = jnp.concatenate([block(2, 2), last], axis=1)
+
+
+def energy_kernel(curl, above, moments, out):
     bends = jnp.zeros((128, 192), F32)
-    mixed = jnp.zeros((192, 192), F32)
-    for c in range(3):
+    for c in range(2):
         for k in range(0, 8, 2):
-            parts = jnp.concatenate(thirds(columns(curl, c, k)), axis=0)
-            bends = bends + lax.dot_general(parts[:128], parts, NT, preferred_element_type=F32)
-            wide = jnp.concatenate(thirds(columns(scaled, c, k)), axis=0)
-            field = jnp.concatenate(thirds(columns(v2, c, k)), axis=0)
-            mixed = mixed + lax.dot_general(wide, field, NT, preferred_element_type=F32)
-    last = bends[:64, :64] + 2.0 * (bends[:64, 64:128] + bends[:64, 128:]) + bends[64:, 64:128]
-    for i, j in ((0, 0), (0, 1), (1, 0), (1, 1), (0, 2), (2, 0)):
-        last = last + mixed[64 * i : 64 * i + 64, 64 * j : 64 * j + 64]
+            rows = []
+            for j in range(2):
+                beyond = jnp.concatenate([unpack(above[:, 1 - c, k + j], half, False) for half in range(2)], axis=0)
+                bent = curl[:, c, k + j] - beyond if c == 0 else curl[:, c, k + j] + beyond
+                rows.append(bent.reshape(64, LANES))
+            bends = bends + bend(jnp.concatenate(thirds(jnp.concatenate(rows, axis=1)), axis=0))
     out[0:128, :] = moments[0:128, :]
-    out[128:192, :] = jnp.concatenate([moments[128:192, :64], last], axis=1)
+    out[128:192, :] = moments[128:192, :] + jnp.concatenate([jnp.zeros((64, 64), F32), fold(bends)], axis=1)
 
 
 def spread(a, lane):
@@ -335,8 +364,7 @@
         for k in range(8):
             floor = line(spread(origin[p], first + k), k) * 2e-7
             pivot = line(cols[k], k)
-            sound = pivot > floor
-            inverse = jnp.where(sound, 1.0 / jnp.where(sound, pivot, 1.0), 0.0)
+            inverse = jnp.where(pivot > floor, 1.0 / pivot, 0.0)
             own, hit = cols[k], sub == k
             for j in range(k + 1, 8):
                 scaled = line(cols[j], k) * inverse
@@ -394,7 +422,7 @@
                 out[:, c, k + j] = mixed[:, LANES * j : LANES * j + LANES].reshape(8, 8, LANES)
 
 
-def call(kernel, outs, scratch=(), n_in=1, flops=0, where=pltpu.VMEM):
+def call(kernel, outs, scratch=(), n_in=1, flops=0, where=pltpu.VMEM, limit=48):
     single = not isinstance(outs, list)
     shapes = [outs] if single else outs
     vmem = pl.BlockSpec(memory_space=pltpu.VMEM)
@@ -405,7 +433,7 @@
         in_specs=[pl.BlockSpec(memory_space=where)] * n_in,
         out_specs=[vmem] * len(shapes),
         scratch_shapes=scratch,
-        compiler_params=pltpu.CompilerParams(vmem_limit_bytes=48 * 1024 * 1024),
+        compiler_params=pltpu.CompilerParams(vmem_limit_bytes=limit * 1024 * 1024),
         cost_estimate=pl.CostEstimate(flops=flops, bytes_accessed=4 * 1024 * 1024, transcendentals=0),
     )
     return (lambda *a: done(*a)[0]) if single else done
@@ -440,19 +468,23 @@
         + [(LANES, LANES), (67 * 8, LANES), (67 * 8, LANES), pltpu.SemaphoreType.DMA((7,))],
         n_in=7,
         where=pl.ANY,
+        limit=60,
     )(*arrays)
     v0 = exchange(outgoing, "rx")
     message = (4, 2, 10, 8, LANES)
-    inner, outer = call(first_kernel, [message] * 2)(v0)
+    outer = lax.ppermute(call(functools.partial(message_kernel, True), message)(v0), "space", beside)
+    base, inner = call(functools.partial(base_kernel, 0), [(8, 3, 10, 8, LANES), message], n_in=2, flops=10**8)(v0, mass)
+    inner = lax.ppermute(inner, "space", chips)
+    v1, outer = call(second_kernel, [(8, 3, 10, 8, LANES), message], n_in=3)(outer, base, inner)
     outer = lax.ppermute(outer, "space", beside)
+    base, inner = call(functools.partial(base_kernel, 1), [(8, 3, 9, 8, LANES), message], n_in=2, flops=10**8)(v1, mass)
     inner = lax.ppermute(inner, "space", chips)
-    v1, inner, outer = call(second_kernel, [(8, 3, 10, 8, LANES), message, message], n_in=4)(v0, mass, inner, outer)
-    outer = lax.ppermute(outer, "space", beside)
-    inner = lax.ppermute(inner, "space", chips)
-    v2, down = call(third_kernel, [(8, 3, 9, 8, LANES), (4, 2, 8, 8, LANES)], n_in=4)(v1, mass, inner, outer)
+    v2, down = call(third_kernel, [(8, 3, 9, 8, LANES), (4, 2, 8, 8, LANES)], n_in=3)(outer, base, inner)
     above = lax.ppermute(down, "space", fall)
-    moments = call(moments_kernel, (192, LANES), n_in=3, flops=10**8)(v0, v1, v2)
-    moments = call(energy_kernel, (192, LANES), [(8, 3, 8, 8, LANES)] * 2, n_in=4)(v2, mass, above, moments)
+    moments, curl = call(
+        moments_kernel, [(192, LANES), (8, 2, 8, 8, LANES)], [(8, 1, 8, 8, LANES), (8, 3, 8, 8, LANES)], n_in=4, flops=10**8
+    )(v0, v1, v2, mass)
+    moments = call(energy_kernel, (192, LANES), n_in=3)(curl, above, moments)
     moments = reduce_bricks(moments)
     mixed = call(finish_kernel, (8, 3, 8, 8, LANES), n_in=4)(moments, v0, v1, v2)
     mixed = exchange(mixed, "rx")

time: 156 us -> 147 us (0.942)
  waiting for transfers between devices: 14.1 us -> 7.98 us
  local copies, waits for them, and re-layouts: 5.21 us -> 0.05 us
  Pallas kernels: 20.3 us -> 23.5 us
    ppermute x2 -> x1, waiting for transfers between devices: 10.2 us -> 2.92 us  [body(): outer = lax.ppermute(outer, 'space', beside)]
    ppermute x0 -> x1, starting transfers between devices: none -> 5.4 us  [body(): lax.ppermute(call(functools.partial(message_kernel, True), message)(v0),...]
    unnamed x14 -> x2, local copies, waits for them, and re-layouts: 5.16 us -> 0.01 us
    pallas_call x3 -> x5, Pallas kernels: 5.27 us -> 9.38 us  [the longest x1 3.21 us: body(): call(moments_kernel, [(192, LANES), (8, 2, 8, 8, LANES)], [(8, 1, 8, 8, L...]
    ppermute x2 -> x1, starting transfers between devices: 6.51 us -> 3.36 us  [body(): outer = lax.ppermute(outer, 'space', beside)]
    ppermute x2, starting transfers between devices: 2.87 us -> 0.19 us  [body(): inner = lax.ppermute(inner, 'space', chips)]
    ppermute x0 -> x1, waiting for transfers between devices: none -> 2.51 us  [body(): lax.ppermute(call(functools.partial(message_kernel, True), message)(v0),...]
    pallas_call x4, Pallas kernels: 13.7 us -> 11.2 us  [call(): return (lambda *a: done(*a)[0]) if single else done]
  transfers between devices with their start and end apart: 5 -> 5, of which waited for: 3 -> 3; matrix products, arithmetic and copies ran while one was open for 0% -> 0% of each run, Pallas kernels for 1% -> 5%
where the time goes in v2:
time: 147 us
  blocking collectives  104 us (71%)
  Pallas kernels  23.5 us (16%)
  starting transfers between devices  10.9 us (7%)
  waiting for transfers between devices  7.98 us (5%)
    all_to_all x5, blocking collectives, exchange(): return lax.all_to_all(x, axis, split_axis=0, concat_axis=0, tiled=True)  104 us
    pallas_call x4, Pallas kernels, call(): return (lambda *a: done(*a)[0]) if single else done  11.2 us
    ppermute x1, starting transfers between devices, body(): lax.ppermute(call(functools.partial(message_kernel, True), message)(v0),...  5.4 us
    ppermute x1, starting transfers between devices, body(): outer = lax.ppermute(outer, 'space', beside)  3.36 us
    pallas_call x1, Pallas kernels, body(): call(moments_kernel, [(192, LANES), (8, 2, 8, 8, LANES)], [(8, 1, 8, 8, L...  3.21 us
  transfers between devices with their start and end apart: 5, of which 3 were waited for; matrix products, arithmetic and copies ran while one was open for 0% of the time, Pallas kernels for 5%

profile of v2, /device:TPU:1, one launch (start us, length us, event | category | flops | bytes accessed | tf_op | source)
XLA Modules:
  0.0 146.8 jit_solution(8508812698649157906)
XLA Ops:
  0.0 2.9 %shard_map.73 = (f32[8,3,11,8,128]{4,3,2,1,0:T(8,128)}, f32[11,8,128]{2,1,0:T(8,128)}) custom-call(f32[8,3,2,32,128]{4,3,2,1,0:T(8,128)} %refs_0_.1, s32[2,32,128]{2,1,0:T(8,128)} %refs_1_.1, f32[16]{0:T(128)} %refs_2_.1, s32[8]{0:T(128)} %refs_3_.1, s32[8]{0:T(128)} %refs_4_.1, s32[8]{0:T(128)} %refs_5_.1, f32[8]{0:T(128)} %refs_6_.1), custom_call_target="tpu_custom_call" | custom-call | bytes 4194304 | tf_op jit(solution)/shard_map/pallas_call | solution.py:464
  2.9 36.7 %all_to_all.25.v.v0 = f32[8,3,11,8,128]{4,3,2,1,0:T(8,128)S(1)} all-to-all(f32[8,3,11,8,128]{4,3,2,1,0:T(8,128)} %get-tuple-element.17), channel_id=1, replica_groups=mesh['space'=32,'rx'=8] {'rx'}, dimensions={0} | all-to-all | bytes 2162688 | tf_op jit(solution)/shard_map/all_to_all | solution.py:443
  39.7 0.7 shard_map.74
  40.4 5.4 %collective-permute-start = (f32[4,2,10,8,128]{4,3,2,1,0:T(8,128)S(1)}, f32[4,2,10,8,128]{4,3,2,1,0:T(8,128)S(1)}, u32[]{:S(2)}, u32[]{:S(2)}) collective-permute-start(f32[4,2,10,8,128]{4,3,2,1,0:T(8,128)S(1)} %shard_map.74), channel_id=1, source_target_pairs={{8,16},{16,8},{24,32},{32,24},{40,48},{48,40},{56,64},{64,56},{72,... | collective-permute-start | bytes 983048 | tf_op jit(solution)/shard_map/ppermute | solution.py:475
  45.8 2.1 %shard_map.75 = (f32[8,3,10,8,128]{4,3,2,1,0:T(8,128)S(1)}, f32[4,2,10,8,128]{4,3,2,1,0:T(8,128)S(1)}) custom-call(f32[8,3,11,8,128]{4,3,2,1,0:T(8,128)S(1)} %all_to_all.25.v.v0, f32[11,8,128]{2,1,0:T(8,128)S(1)} %copy-done), custom_call_target="tpu_custom_call" | custom-call | flops 100000000 | bytes 4194304 | tf_op jit(solution)/shard_map/pallas_call | solution.py:476
  47.9 0.1 collective-permute-start.1
  48.0 2.5 %collective-permute-done.outer = f32[4,2,10,8,128]{4,3,2,1,0:T(8,128)S(1)} collective-permute-done((f32[4,2,10,8,128]{4,3,2,1,0:T(8,128)S(1)}, f32[4,2,10,8,128]{4,3,2,1,0:T(8,128)S(1)}, u32[]{:S(2)}, u32[]{:S(2)}) %collective-permute-start) | collective-permute-done | bytes 327712 | tf_op jit(solution)/shard_map/ppermute | solution.py:475
  50.5 0.0 collective-permute-done.1.inner
  50.5 1.4 shard_map.76
  51.9 3.4 %collective-permute-start.2 = (f32[4,2,10,8,128]{4,3,2,1,0:T(8,128)S(1)}, f32[4,2,10,8,128]{4,3,2,1,0:T(8,128)S(1)}, u32[]{:S(2)}, u32[]{:S(2)}) collective-permute-start(f32[4,2,10,8,128]{4,3,2,1,0:T(8,128)S(1)} %get-tuple-element.22), channel_id=1, source_target_pairs={{8,16},{16,8},{24,32},{32,24},{40,48},{48,40},{56,64},{64,56},{72,... | collective-permute-start | bytes 983048 | tf_op jit(solution)/shard_map/ppermute | solution.py:479
  55.3 2.0 %shard_map.77 = (f32[8,3,9,8,128]{4,3,2,1,0:T(8,128)S(1)}, f32[4,2,10,8,128]{4,3,2,1,0:T(8,128)S(1)}) custom-call(f32[8,3,10,8,128]{4,3,2,1,0:T(8,128)S(1)} %get-tuple-element.21.v.v1, f32[11,8,128]{2,1,0:T(8,128)S(1)} %copy-done), custom_call_target="tpu_custom_call" | custom-call | flops 100000000 | bytes 4194304 | tf_op jit(solution)/shard_map/pallas_call | solution.py:480
  57.3 0.1 collective-permute-start.3
  57.4 2.9 %collective-permute-done.2.outer = f32[4,2,10,8,128]{4,3,2,1,0:T(8,128)S(1)} collective-permute-done((f32[4,2,10,8,128]{4,3,2,1,0:T(8,128)S(1)}, f32[4,2,10,8,128]{4,3,2,1,0:T(8,128)S(1)}, u32[]{:S(2)}, u32[]{:S(2)}) %collective-permute-start.2) | collective-permute-done | bytes 327712 | tf_op jit(solution)/shard_map/ppermute | solution.py:479
  60.3 0.7 shard_map.78
  61.0 1.9 %collective-permute-start.4 = (f32[4,2,8,8,128]{4,3,2,1,0:T(8,128)S(1)}, f32[4,2,8,8,128]{4,3,2,1,0:T(8,128)S(1)}, u32[]{:S(2)}, u32[]{:S(2)}) collective-permute-start(f32[4,2,8,8,128]{4,3,2,1,0:T(8,128)S(1)} %get-tuple-element.27), channel_id=1, source_target_pairs={{8,0},{16,8},{24,16},{32,24},{40,32},{48,40},{56,48},{64,56},{72,6... | collective-permute-start | bytes 786440 | tf_op jit(solution)/shard_map/ppermute | solution.py:483
  62.9 3.2 %shard_map.79 = (f32[192,128]{1,0:T(8,128)S(1)}, f32[8,2,8,8,128]{4,3,2,1,0:T(8,128)S(1)}) custom-call(f32[8,3,11,8,128]{4,3,2,1,0:T(8,128)S(1)} %all_to_all.25.v.v0, f32[8,3,10,8,128]{4,3,2,1,0:T(8,128)S(1)} %get-tuple-element.21.v.v1, f32[8,3,9,8,128]{4,3,2,1,0:T(8,128)S(1)} %get-tuple-element.25.v2, f32[11,8,128]{2,1,0:T(8,128)S(1)} %copy-done), custom_call_target="tpu_custom_call" | custom-call | flops 100000000 | bytes 4194304 | tf_op jit(solution)/shard_map/pallas_call | solution.py:484
  66.2 2.5 %collective-permute-done.4.above = f32[4,2,8,8,128]{4,3,2,1,0:T(8,128)S(1)} collective-permute-done((f32[4,2,8,8,128]{4,3,2,1,0:T(8,128)S(1)}, f32[4,2,8,8,128]{4,3,2,1,0:T(8,128)S(1)}, u32[]{:S(2)}, u32[]{:S(2)}) %collective-permute-start.4) | collective-permute-done | bytes 262176 | tf_op jit(solution)/shard_map/ppermute | solution.py:483
  68.7 0.7 shard_map.80
  69.4 18.9 %all_to_all.26 = f32[32,6,128]{2,1,0:T(8,128)S(1)} all-to-all(f32[32,6,128]{2,1,0:T(8,128)S(1)} %reshape.8), channel_id=1, replica_groups=mesh['space'=32,'rx'=8] {'space'}, dimensions={0} | all-to-all | bytes 196608 | tf_op jit(solution)/shard_map/all_to_all | solution.py:443
  88.4 9.9 %all_to_all.27 = f32[8,6,128]{2,1,0:T(8,128)S(1)} all-to-all(f32[8,6,128]{2,1,0:T(8,128)S(1)} %broadcast_in_dim.4), channel_id=1, replica_groups=mesh['space'=32,'rx'=8] {'rx'}, dimensions={0} | all-to-all | bytes 49152 | tf_op jit(solution)/shard_map/all_to_all | solution.py:443
  98.4 12.6 %all_to_all.28 = f32[32,6,128]{2,1,0:T(8,128)S(1)} all-to-all(f32[32,6,128]{2,1,0:T(8,128)S(1)} %broadcast_in_dim.5), channel_id=1, replica_groups=mesh['space'=32,'rx'=8] {'space'}, dimensions={0} | all-to-all | bytes 196608 | tf_op jit(solution)/shard_map/all_to_all | solution.py:443
  111.0 8.4 %shard_map.81 = f32[8,3,8,8,128]{4,3,2,1,0:T(8,128)S(1)} custom-call(f32[192,128]{1,0:T(8,128)S(1)} %reshape.9.moments, f32[8,3,11,8,128]{4,3,2,1,0:T(8,128)S(1)} %all_to_all.25.v.v0, f32[8,3,10,8,128]{4,3,2,1,0:T(8,128)S(1)} %get-tuple-element.21.v.v1, f32[8,3,9,8,128]{4,3,2,1,0:T(8,128)S(1)} %get-tuple-element.25.v2), custom_call_target="tpu_custom_call" | custom-call | bytes 4194304 | tf_op jit(solution)/shard_map/pallas_call | solution.py:439
  119.3 26.0 %all_to_all.29.tiles = f32[8,3,8,8,128]{4,3,2,1,0:T(8,128)S(1)} all-to-all(f32[8,3,8,8,128]{4,3,2,1,0:T(8,128)S(1)} %shard_map.81), channel_id=1, replica_groups=mesh['space'=32,'rx'=8] {'rx'}, dimensions={0} | all-to-all | bytes 1572864 | tf_op jit(solution)/shard_map/all_to_all | solution.py:443
  145.3 1.5 shard_map.82
  (9 shorter events, 0.1 us)
Async XLA Ops:
  39.7 6.1 %copy-start = (f32[11,8,128]{2,1,0:T(8,128)S(1)}, f32[11,8,128]{2,1,0:T(8,128)}, u32[]{:S(2)}) copy-start(f32[11,8,128]{2,1,0:T(8,128)} %get-tuple-element.18.mass) | copy-start | bytes 135172
  40.4 10.1 %collective-permute-start = (f32[4,2,10,8,128]{4,3,2,1,0:T(8,128)S(1)}, f32[4,2,10,8,128]{4,3,2,1,0:T(8,128)S(1)}, u32[]{:S(2)}, u32[]{:S(2)}) collective-permute-start(f32[4,2,10,8,128]{4,3,2,1,0:T(8,128)S(1)} %shard_map.74), channel_id=1, source_target_pairs={{8,16},{16,8},{24,32},{32,24},{40,48},{48,40},{56,64},{64,56},{72,... | collective-permute-start | bytes 983048 | tf_op jit(solution)/shard_map/ppermute | solution.py:475
  47.9 2.6 %collective-permute-start.1 = (f32[4,2,10,8,128]{4,3,2,1,0:T(8,128)S(1)}, f32[4,2,10,8,128]{4,3,2,1,0:T(8,128)S(1)}, u32[]{:S(2)}, u32[]{:S(2)}) collective-permute-start(f32[4,2,10,8,128]{4,3,2,1,0:T(8,128)S(1)} %get-tuple-element.20), channel_id=1, source_target_pairs={{0,8},{8,0},{16,24},{24,16},{32,40},{40,32},{48,56},{56,48},{64,72... | collective-permute-start | bytes 983048 | tf_op jit(solution)/shard_map/ppermute | solution.py:477
  51.9 8.4 %collective-permute-start.2 = (f32[4,2,10,8,128]{4,3,2,1,0:T(8,128)S(1)}, f32[4,2,10,8,128]{4,3,2,1,0:T(8,128)S(1)}, u32[]{:S(2)}, u32[]{:S(2)}) collective-permute-start(f32[4,2,10,8,128]{4,3,2,1,0:T(8,128)S(1)} %get-tuple-element.22), channel_id=1, source_target_pairs={{8,16},{16,8},{24,32},{32,24},{40,48},{48,40},{56,64},{64,56},{72,... | collective-permute-start | bytes 983048 | tf_op jit(solution)/shard_map/ppermute | solution.py:479
  57.3 3.0 %collective-permute-start.3 = (f32[4,2,10,8,128]{4,3,2,1,0:T(8,128)S(1)}, f32[4,2,10,8,128]{4,3,2,1,0:T(8,128)S(1)}, u32[]{:S(2)}, u32[]{:S(2)}) collective-permute-start(f32[4,2,10,8,128]{4,3,2,1,0:T(8,128)S(1)} %get-tuple-element.24), channel_id=1, source_target_pairs={{0,8},{8,0},{16,24},{24,16},{32,40},{40,32},{48,56},{56,48},{64,72... | collective-permute-start | bytes 983048 | tf_op jit(solution)/shard_map/ppermute | solution.py:481
  61.0 7.7 %collective-permute-start.4 = (f32[4,2,8,8,128]{4,3,2,1,0:T(8,128)S(1)}, f32[4,2,8,8,128]{4,3,2,1,0:T(8,128)S(1)}, u32[]{:S(2)}, u32[]{:S(2)}) collective-permute-start(f32[4,2,8,8,128]{4,3,2,1,0:T(8,128)S(1)} %get-tuple-element.27), channel_id=1, source_target_pairs={{8,0},{16,8},{24,16},{32,24},{40,32},{48,40},{56,48},{64,56},{72,6... | collective-permute-start | bytes 786440 | tf_op jit(solution)/shard_map/ppermute | solution.py:483

commit v3 on v2

--- a/solution.py
+++ b/solution.py
@@ -12,6 +12,7 @@
 HALF = 64
 PLANE = 32
 GHOST = 11
+SENT = 31
 F32 = jnp.float32
 BF16 = jnp.bfloat16
 NT = (((1,), (1,)), ((), ()))
@@ -101,14 +102,15 @@
 
 
 def enter_kernel(*refs):
-    sources, (out, mass_out), rest = refs[:7], refs[7:9], refs[9:]
-    targets, (flipped, padded, mass_pad, sems) = rest[:7], rest[7:]
-    copies = [pltpu.make_async_copy(a, b, sems.at[i]) for i, (a, b) in enumerate(zip(sources, targets, strict=True))]
-    for copy in copies:
+    (source, *sources), (out, mass_out), rest = refs[:7], refs[7:9], refs[9:]
+    (field, *targets), (flipped, padded, ghost, mass_pad, loads, stores) = rest[:7], rest[7:]
+    copies = [pltpu.make_async_copy(a, b, loads.at[i]) for i, (a, b) in enumerate(zip(sources, targets, strict=True))]
+    parts = [pltpu.make_async_copy(source.at[:, c], field.at[c], loads.at[6 + c]) for c in range(3)]
+    for copy in copies + parts:
         copy.start()
     for copy in copies:
         copy.wait()
-    field, ids, rate, coil_x, coil_y, coil_z, amp = targets
+    ids, rate, coil_x, coil_y, coil_z, amp = targets
     lane = lax.broadcasted_iota(jnp.int32, (64, LANES), 1)
     row = lax.broadcasted_iota(jnp.int32, (64, LANES), 0)
     classes = ids[...].reshape(64, LANES)
@@ -127,7 +129,7 @@
     base = lax.axis_index("space") * 2
 
     def right(r, c):
-        values = mass * field[r, c].reshape(64, LANES)
+        values = mass * field[c, r].reshape(64, LANES)
         if c == 2:
             return values
         near = coil_x[r] - base
@@ -140,21 +142,44 @@
         strength = jnp.where(row == plus, amp[r], jnp.where(row == minus, -amp[r], 0.0))
         return values + jnp.where(lane == coil_z[r], strength, 0.0)
 
+    sends = []
     for c in range(3):
-        padded[0:8, :] = jnp.zeros((8, LANES), F32)
-        padded[8 * 65 :, :] = jnp.zeros((16, LANES), F32)
+        parts[c].wait()
+        padded[c, 0:8, :] = jnp.zeros((8, LANES), F32)
+        padded[c, 8 * 65 :, :] = jnp.zeros((16, LANES), F32)
         for r in range(4):
             flipped[...] = jnp.transpose(jnp.concatenate([right(r, c), right(r + 4, c)], axis=0))
             even = flipped[pl.ds(0, 64, stride=2), :]
             odd = flipped[pl.ds(1, 64, stride=2), :]
-            padded[pl.ds(8 + r, 64, stride=8), :] = jnp.where(left, even, turn(odd, HALF))
-            padded[pl.ds(12 + r, 64, stride=8), :] = jnp.where(left, turn(even, HALF), odd)
-        for d in range(8):
-            out[d, c] = padded[64 * d : 64 * d + 8 * GHOST, :].reshape(GHOST, 8, LANES)
-
-
-def leave_kernel(tiles, out, gathered, flipped):
+            padded[c, pl.ds(8 + r, 64, stride=8), :] = jnp.where(left, even, turn(odd, HALF))
+            padded[c, pl.ds(12 + r, 64, stride=8), :] = jnp.where(left, turn(even, HALF), odd)
+        sends += [(padded.at[c, 64 * d : 64 * d + 80], out.at[d, 80 * c : 80 * c + 80]) for d in range(8)]
+        if c == 1:
+            for d in range(8):
+                tiles = [padded[k, 64 * d + 80 : 64 * d + 88, :] for k in range(2)]
+                ghost[8 * d : 8 * d + 8, :] = jnp.where(left[:8], tiles[0], turn(tiles[1], HALF))
+            sends += [(ghost.at[8 * d : 8 * d + 8], out.at[d, 240:248]) for d in range(8)]
+        for i, pair in enumerate(sends):
+            if i >= (0, 8, 24)[c]:
+                sends[i] = pltpu.make_async_copy(*pair, stores.at[i])
+                sends[i].start()
+    for copy in sends:
+        copy.wait()
+
+
+def first_fields(v0, s):
+    last = v0[s, pl.ds(SENT - 1, 1)]
+    ends = [last, turn(last, HALF), jnp.zeros((1, 8, LANES), F32)]
+    return [jnp.concatenate([v0[s, 10 * c : 10 * c + 10], ends[c]], axis=0) for c in range(3)]
+
+
+def fields_of(v, s):
+    return first_fields(v, s) if v.shape[1] == SENT else [v[s, c] for c in range(3)]
+
+
+def leave_kernel(tiles, out, gathered, flipped, result, sems):
     left = lax.broadcasted_iota(jnp.int32, (64, LANES), 1) < HALF
+    sends = []
     for c in range(3):
         for s in range(8):
             gathered[64 * s : 64 * s + 64, :] = tiles[s, c].reshape(64, LANES)
@@ -164,8 +189,12 @@
             flipped[pl.ds(0, 64, stride=2), :] = jnp.where(left, one, turn(two, HALF))
             flipped[pl.ds(1, 64, stride=2), :] = jnp.where(left, turn(one, HALF), two)
             back = jnp.transpose(flipped[...])
-            out[r, c] = back[:64].reshape(2, PLANE, LANES)
-            out[r + 4, c] = back[64:].reshape(2, PLANE, LANES)
+            result[c, r] = back[:64].reshape(2, PLANE, LANES)
+            result[c, r + 4] = back[64:].reshape(2, PLANE, LANES)
+        sends.append(pltpu.make_async_copy(result.at[c], out.at[:, c], sems.at[c]))
+        sends[c].start()
+    for copy in sends:
+        copy.wait()
 
 
 def is_even():
@@ -188,7 +217,7 @@
 
 def message_kernel(outer, v, message):
     def step(s, carry):
-        fields = [[v[s + 4 * k, c] for c in range(3)] for k in range(2)]
+        fields = [fields_of(v, s + 4 * k) for k in range(2)]
         send(message, is_even() != outer, s, *fields)
         return carry
 
@@ -215,9 +244,9 @@
 
 def base_kernel(first, v, mass, base, inner):
     def step(s, carry):
-        fields = [[v[s + 4 * k, c] for c in range(3)] for k in range(2)]
+        fields = [fields_of(v, s + 4 * k) for k in range(2)]
         for k in range(2):
-            result = apply_tiles(fields[k], mass[: v.shape[2]])
+            result = apply_tiles(fields[k], mass[: fields[k][0].shape[0]])
             for c in range(3):
                 base[s + 4 * k, c] = result[c][first : first + base.shape[2]]
         send(inner, is_even(), s, *fields)
@@ -264,7 +293,8 @@
 
 
 def columns(ref, c, first):
-    return jnp.concatenate([ref[:, c, first + k].reshape(64, LANES) for k in range(2)], axis=1)
+    at = lambda k: ref[:, 10 * c + k] if ref.shape[1] == SENT else ref[:, c, k]
+    return jnp.concatenate([at(first + k).reshape(64, LANES) for k in range(2)], axis=1)
 
 
 def bend(parts):
@@ -422,7 +452,7 @@
                 out[:, c, k + j] = mixed[:, LANES * j : LANES * j + LANES].reshape(8, 8, LANES)
 
 
-def call(kernel, outs, scratch=(), n_in=1, flops=0, where=pltpu.VMEM, limit=48):
+def call(kernel, outs, scratch=(), n_in=1, flops=0, where=pltpu.VMEM, limit=48, far=False):
     single = not isinstance(outs, list)
     shapes = [outs] if single else outs
     vmem = pl.BlockSpec(memory_space=pltpu.VMEM)
@@ -431,7 +461,7 @@
         kernel,
         out_shape=[jax.ShapeDtypeStruct(s, F32) for s in shapes],
         in_specs=[pl.BlockSpec(memory_space=where)] * n_in,
-        out_specs=[vmem] * len(shapes),
+        out_specs=[pl.BlockSpec(memory_space=pl.ANY) if far else vmem, *[vmem] * (len(shapes) - 1)],
         scratch_shapes=scratch,
         compiler_params=pltpu.CompilerParams(vmem_limit_bytes=limit * 1024 * 1024),
         cost_estimate=pl.CostEstimate(flops=flops, bytes_accessed=4 * 1024 * 1024, transcendentals=0),
@@ -460,17 +490,20 @@
     fall = [(i + 1, i) for i in range(size - 1)]
     beside = [pair for i in range(1, size - 1, 2) for pair in ((i, i + 1), (i + 1, i))]
     arrays = (lambda_next, class_ids, class_rate, coil_x, coil_y, coil_z, coil_amp)
-    spaces = [pltpu.VMEM] * 2 + [pltpu.SMEM] * 5
+    spaces = [pltpu.VMEM] + [pltpu.SMEM] * 5
     outgoing, mass = call(
         enter_kernel,
-        [(8, 3, GHOST, 8, LANES), (GHOST, 8, LANES)],
-        [space(a.shape, a.dtype) for space, a in zip(spaces, arrays, strict=True)]
-        + [(LANES, LANES), (67 * 8, LANES), (67 * 8, LANES), pltpu.SemaphoreType.DMA((7,))],
+        [(8, 8 * SENT, LANES), (GHOST, 8, LANES)],
+        [(3, 8, 2, PLANE, LANES)]
+        + [space(a.shape, a.dtype) for space, a in zip(spaces, arrays[1:], strict=True)]
+        + [(LANES, LANES), (3, 67 * 8, LANES), (64, LANES), (67 * 8, LANES)]
+        + [pltpu.SemaphoreType.DMA((9,)), pltpu.SemaphoreType.DMA((32,))],
         n_in=7,
         where=pl.ANY,
         limit=60,
+        far=True,
     )(*arrays)
-    v0 = exchange(outgoing, "rx")
+    v0 = exchange(outgoing, "rx").reshape(8, SENT, 8, LANES)
     message = (4, 2, 10, 8, LANES)
     outer = lax.ppermute(call(functools.partial(message_kernel, True), message)(v0), "space", beside)
     base, inner = call(functools.partial(base_kernel, 0), [(8, 3, 10, 8, LANES), message], n_in=2, flops=10**8)(v0, mass)
@@ -488,7 +521,8 @@
     moments = reduce_bricks(moments)
     mixed = call(finish_kernel, (8, 3, 8, 8, LANES), n_in=4)(moments, v0, v1, v2)
     mixed = exchange(mixed, "rx")
-    return call(leave_kernel, (8, 3, 2, PLANE, LANES), [(512, LANES), (LANES, LANES)])(mixed)
+    scratch = [(512, LANES), (LANES, LANES), (3, 8, 2, PLANE, LANES), pltpu.SemaphoreType.DMA((3,))]
+    return call(leave_kernel, (8, 3, 2, PLANE, LANES), scratch, far=True)(mixed)
 
 
 def solution(mesh):

time: 147 us -> 146 us (level)
  no operation moved by 1% of the time
where the time goes in v3:
time: 146 us
  blocking collectives  103 us (71%)
  Pallas kernels  24.2 us (17%)
  starting transfers between devices  10.6 us (7%)
  waiting for transfers between devices  7.98 us (5%)
    all_to_all x5, blocking collectives, exchange(): return lax.all_to_all(x, axis, split_axis=0, concat_axis=0, tiled=True)  103 us
    pallas_call x4, Pallas kernels, call(): return (lambda *a: done(*a)[0]) if single else done  11.1 us
    ppermute x1, starting transfers between devices, body(): lax.ppermute(call(functools.partial(message_kernel, True), message)(v0),...  5.09 us
    pallas_call x1, Pallas kernels, body(): call(enter_kernel, [(8, 8 * SENT, LANES), (GHOST, 8, LANES)], [(3, 8, 2,...  3.72 us
    ppermute x1, starting transfers between devices, body(): outer = lax.ppermute(outer, 'space', beside)  3.36 us
    pallas_call x1, Pallas kernels, body(): call(moments_kernel, [(192, LANES), (8, 2, 8, 8, LANES)], [(8, 1, 8, 8, L...  3.22 us
  transfers between devices with their start and end apart: 5, of which 3 were waited for; matrix products, arithmetic and copies ran while one was open for 0% of the time, Pallas kernels for 5%

profile of v3, /device:TPU:1, one launch (start us, length us, event | category | flops | bytes accessed | tf_op | source)
XLA Modules:
  0.0 145.9 jit_solution(7547250835176189737)
XLA Ops:
  0.0 3.7 %shard_map.73 = (f32[8,248,128]{2,1,0:T(8,128)}, f32[11,8,128]{2,1,0:T(8,128)}) custom-call(f32[8,3,2,32,128]{4,3,2,1,0:T(8,128)} %refs_0_.1, s32[2,32,128]{2,1,0:T(8,128)} %refs_1_.1, f32[16]{0:T(128)} %refs_2_.1, s32[8]{0:T(128)} %refs_3_.1, s32[8]{0:T(128)} %refs_4_.1, s32[8]{0:T(128)} %refs_5_.1, f32[8]{0:T(128)} %refs_6_.1), custom_call_target="tpu_custom_call" | custom-call | bytes 4194304 | tf_op jit(solution)/shard_map/pallas_call | solution.py:494
  3.7 35.6 %all_to_all.25 = f32[8,248,128]{2,1,0:T(8,128)S(1)} all-to-all(f32[8,248,128]{2,1,0:T(8,128)} %get-tuple-element.17), channel_id=1, replica_groups=mesh['space'=32,'rx'=8] {'rx'}, dimensions={0} | all-to-all | bytes 2031616 | tf_op jit(solution)/shard_map/all_to_all | solution.py:473
  39.4 0.7 shard_map.74
  40.1 5.1 %collective-permute-start = (f32[4,2,10,8,128]{4,3,2,1,0:T(8,128)S(1)}, f32[4,2,10,8,128]{4,3,2,1,0:T(8,128)S(1)}, u32[]{:S(2)}, u32[]{:S(2)}) collective-permute-start(f32[4,2,10,8,128]{4,3,2,1,0:T(8,128)S(1)} %shard_map.74), channel_id=1, source_target_pairs={{8,16},{16,8},{24,32},{32,24},{40,48},{48,40},{56,64},{64,56},{72,... | collective-permute-start | bytes 983048 | tf_op jit(solution)/shard_map/ppermute | solution.py:508
  45.2 2.1 %shard_map.75 = (f32[8,3,10,8,128]{4,3,2,1,0:T(8,128)S(1)}, f32[4,2,10,8,128]{4,3,2,1,0:T(8,128)S(1)}) custom-call(f32[8,31,8,128]{3,2,1,0:T(8,128)S(1)} %bitcast.2, f32[11,8,128]{2,1,0:T(8,128)S(1)} %copy-done), custom_call_target="tpu_custom_call" | custom-call | flops 100000000 | bytes 4194304 | tf_op jit(solution)/shard_map/pallas_call | solution.py:509
  47.3 0.1 collective-permute-start.1
  47.4 2.5 %collective-permute-done.outer = f32[4,2,10,8,128]{4,3,2,1,0:T(8,128)S(1)} collective-permute-done((f32[4,2,10,8,128]{4,3,2,1,0:T(8,128)S(1)}, f32[4,2,10,8,128]{4,3,2,1,0:T(8,128)S(1)}, u32[]{:S(2)}, u32[]{:S(2)}) %collective-permute-start) | collective-permute-done | bytes 327712 | tf_op jit(solution)/shard_map/ppermute | solution.py:508
  49.9 0.0 collective-permute-done.1.inner
  49.9 1.4 shard_map.76
  51.3 3.4 %collective-permute-start.2 = (f32[4,2,10,8,128]{4,3,2,1,0:T(8,128)S(1)}, f32[4,2,10,8,128]{4,3,2,1,0:T(8,128)S(1)}, u32[]{:S(2)}, u32[]{:S(2)}) collective-permute-start(f32[4,2,10,8,128]{4,3,2,1,0:T(8,128)S(1)} %get-tuple-element.22), channel_id=1, source_target_pairs={{8,16},{16,8},{24,32},{32,24},{40,48},{48,40},{56,64},{64,56},{72,... | collective-permute-start | bytes 983048 | tf_op jit(solution)/shard_map/ppermute | solution.py:512
  54.7 2.0 %shard_map.77 = (f32[8,3,9,8,128]{4,3,2,1,0:T(8,128)S(1)}, f32[4,2,10,8,128]{4,3,2,1,0:T(8,128)S(1)}) custom-call(f32[8,3,10,8,128]{4,3,2,1,0:T(8,128)S(1)} %get-tuple-element.21.v.v1, f32[11,8,128]{2,1,0:T(8,128)S(1)} %copy-done), custom_call_target="tpu_custom_call" | custom-call | flops 100000000 | bytes 4194304 | tf_op jit(solution)/shard_map/pallas_call | solution.py:513
  56.7 0.1 collective-permute-start.3
  56.8 2.9 %collective-permute-done.2.outer = f32[4,2,10,8,128]{4,3,2,1,0:T(8,128)S(1)} collective-permute-done((f32[4,2,10,8,128]{4,3,2,1,0:T(8,128)S(1)}, f32[4,2,10,8,128]{4,3,2,1,0:T(8,128)S(1)}, u32[]{:S(2)}, u32[]{:S(2)}) %collective-permute-start.2) | collective-permute-done | bytes 327712 | tf_op jit(solution)/shard_map/ppermute | solution.py:512
  59.7 0.7 shard_map.78
  60.4 1.9 %collective-permute-start.4 = (f32[4,2,8,8,128]{4,3,2,1,0:T(8,128)S(1)}, f32[4,2,8,8,128]{4,3,2,1,0:T(8,128)S(1)}, u32[]{:S(2)}, u32[]{:S(2)}) collective-permute-start(f32[4,2,8,8,128]{4,3,2,1,0:T(8,128)S(1)} %get-tuple-element.27), channel_id=1, source_target_pairs={{8,0},{16,8},{24,16},{32,24},{40,32},{48,40},{56,48},{64,56},{72,6... | collective-permute-start | bytes 786440 | tf_op jit(solution)/shard_map/ppermute | solution.py:516
  62.3 3.2 %shard_map.79 = (f32[192,128]{1,0:T(8,128)S(1)}, f32[8,2,8,8,128]{4,3,2,1,0:T(8,128)S(1)}) custom-call(f32[8,31,8,128]{3,2,1,0:T(8,128)S(1)} %bitcast.3, f32[8,3,10,8,128]{4,3,2,1,0:T(8,128)S(1)} %get-tuple-element.21.v.v1, f32[8,3,9,8,128]{4,3,2,1,0:T(8,128)S(1)} %get-tuple-element.25.v2, f32[11,8,128]{2,1,0:T(8,128)S(1)} %copy-done), custom_call_target="tpu_custom_call" | custom-call | flops 100000000 | bytes 4194304 | tf_op jit(solution)/shard_map/pallas_call | solution.py:517
  65.5 2.5 %collective-permute-done.4.above = f32[4,2,8,8,128]{4,3,2,1,0:T(8,128)S(1)} collective-permute-done((f32[4,2,8,8,128]{4,3,2,1,0:T(8,128)S(1)}, f32[4,2,8,8,128]{4,3,2,1,0:T(8,128)S(1)}, u32[]{:S(2)}, u32[]{:S(2)}) %collective-permute-start.4) | collective-permute-done | bytes 262176 | tf_op jit(solution)/shard_map/ppermute | solution.py:516
  68.1 0.7 shard_map.80
  68.8 19.2 %all_to_all.26 = f32[32,6,128]{2,1,0:T(8,128)S(1)} all-to-all(f32[32,6,128]{2,1,0:T(8,128)S(1)} %reshape.12), channel_id=1, replica_groups=mesh['space'=32,'rx'=8] {'space'}, dimensions={0} | all-to-all | bytes 196608 | tf_op jit(solution)/shard_map/all_to_all | solution.py:473
  88.1 9.4 %all_to_all.27 = f32[8,6,128]{2,1,0:T(8,128)S(1)} all-to-all(f32[8,6,128]{2,1,0:T(8,128)S(1)} %broadcast_in_dim.4), channel_id=1, replica_groups=mesh['space'=32,'rx'=8] {'rx'}, dimensions={0} | all-to-all | bytes 49152 | tf_op jit(solution)/shard_map/all_to_all | solution.py:473
  97.5 12.6 %all_to_all.28 = f32[32,6,128]{2,1,0:T(8,128)S(1)} all-to-all(f32[32,6,128]{2,1,0:T(8,128)S(1)} %broadcast_in_dim.5), channel_id=1, replica_groups=mesh['space'=32,'rx'=8] {'space'}, dimensions={0} | all-to-all | bytes 196608 | tf_op jit(solution)/shard_map/all_to_all | solution.py:473
  110.2 8.4 %shard_map.81 = f32[8,3,8,8,128]{4,3,2,1,0:T(8,128)S(1)} custom-call(f32[192,128]{1,0:T(8,128)S(1)} %reshape.13.moments, f32[8,31,8,128]{3,2,1,0:T(8,128)S(1)} %bitcast.4, f32[8,3,10,8,128]{4,3,2,1,0:T(8,128)S(1)} %get-tuple-element.21.v.v1, f32[8,3,9,8,128]{4,3,2,1,0:T(8,128)S(1)} %get-tuple-element.25.v2), custom_call_target="tpu_custom_call" | custom-call | bytes 4194304 | tf_op jit(solution)/shard_map/pallas_call | solution.py:469
  118.5 26.0 %all_to_all.29.tiles = f32[8,3,8,8,128]{4,3,2,1,0:T(8,128)S(1)} all-to-all(f32[8,3,8,8,128]{4,3,2,1,0:T(8,128)S(1)} %shard_map.81), channel_id=1, replica_groups=mesh['space'=32,'rx'=8] {'rx'}, dimensions={0} | all-to-all | bytes 1572864 | tf_op jit(solution)/shard_map/all_to_all | solution.py:473
  144.5 1.4 shard_map.82
  (9 shorter events, 0.1 us)
Async XLA Ops:
  39.4 5.8 %copy-start = (f32[11,8,128]{2,1,0:T(8,128)S(1)}, f32[11,8,128]{2,1,0:T(8,128)}, u32[]{:S(2)}) copy-start(f32[11,8,128]{2,1,0:T(8,128)} %get-tuple-element.18.mass) | copy-start | bytes 135172
  40.1 9.8 %collective-permute-start = (f32[4,2,10,8,128]{4,3,2,1,0:T(8,128)S(1)}, f32[4,2,10,8,128]{4,3,2,1,0:T(8,128)S(1)}, u32[]{:S(2)}, u32[]{:S(2)}) collective-permute-start(f32[4,2,10,8,128]{4,3,2,1,0:T(8,128)S(1)} %shard_map.74), channel_id=1, source_target_pairs={{8,16},{16,8},{24,32},{32,24},{40,48},{48,40},{56,64},{64,56},{72,... | collective-permute-start | bytes 983048 | tf_op jit(solution)/shard_map/ppermute | solution.py:508
  47.3 2.6 %collective-permute-start.1 = (f32[4,2,10,8,128]{4,3,2,1,0:T(8,128)S(1)}, f32[4,2,10,8,128]{4,3,2,1,0:T(8,128)S(1)}, u32[]{:S(2)}, u32[]{:S(2)}) collective-permute-start(f32[4,2,10,8,128]{4,3,2,1,0:T(8,128)S(1)} %get-tuple-element.20), channel_id=1, source_target_pairs={{0,8},{8,0},{16,24},{24,16},{32,40},{40,32},{48,56},{56,48},{64,72... | collective-permute-start | bytes 983048 | tf_op jit(solution)/shard_map/ppermute | solution.py:510
  51.3 8.4 %collective-permute-start.2 = (f32[4,2,10,8,128]{4,3,2,1,0:T(8,128)S(1)}, f32[4,2,10,8,128]{4,3,2,1,0:T(8,128)S(1)}, u32[]{:S(2)}, u32[]{:S(2)}) collective-permute-start(f32[4,2,10,8,128]{4,3,2,1,0:T(8,128)S(1)} %get-tuple-element.22), channel_id=1, source_target_pairs={{8,16},{16,8},{24,32},{32,24},{40,48},{48,40},{56,64},{64,56},{72,... | collective-permute-start | bytes 983048 | tf_op jit(solution)/shard_map/ppermute | solution.py:512
  56.7 3.0 %collective-permute-start.3 = (f32[4,2,10,8,128]{4,3,2,1,0:T(8,128)S(1)}, f32[4,2,10,8,128]{4,3,2,1,0:T(8,128)S(1)}, u32[]{:S(2)}, u32[]{:S(2)}) collective-permute-start(f32[4,2,10,8,128]{4,3,2,1,0:T(8,128)S(1)} %get-tuple-element.24), channel_id=1, source_target_pairs={{0,8},{8,0},{16,24},{24,16},{32,40},{40,32},{48,56},{56,48},{64,72... | collective-permute-start | bytes 983048 | tf_op jit(solution)/shard_map/ppermute | solution.py:514
  60.4 7.7 %collective-permute-start.4 = (f32[4,2,8,8,128]{4,3,2,1,0:T(8,128)S(1)}, f32[4,2,8,8,128]{4,3,2,1,0:T(8,128)S(1)}, u32[]{:S(2)}, u32[]{:S(2)}) collective-permute-start(f32[4,2,8,8,128]{4,3,2,1,0:T(8,128)S(1)} %get-tuple-element.27), channel_id=1, source_target_pairs={{8,0},{16,8},{24,16},{32,24},{40,32},{48,40},{56,48},{64,56},{72,6... | collective-permute-start | bytes 786440 | tf_op jit(solution)/shard_map/ppermute | solution.py:516

commit v4 on v3

--- a/solution.py
+++ b/solution.py
@@ -103,10 +103,10 @@
 
 def enter_kernel(*refs):
     (source, *sources), (out, mass_out), rest = refs[:7], refs[7:9], refs[9:]
-    (field, *targets), (flipped, padded, ghost, mass_pad, loads, stores) = rest[:7], rest[7:]
+    (field, *targets), (flipped, padded, mass_pad, loads) = rest[:7], rest[7:]
     copies = [pltpu.make_async_copy(a, b, loads.at[i]) for i, (a, b) in enumerate(zip(sources, targets, strict=True))]
-    parts = [pltpu.make_async_copy(source.at[:, c], field.at[c], loads.at[6 + c]) for c in range(3)]
-    for copy in copies + parts:
+    copies = [pltpu.make_async_copy(source, field, loads.at[6]), *copies]
+    for copy in copies:
         copy.start()
     for copy in copies:
         copy.wait()
@@ -118,8 +118,8 @@
     for k in range(rate.shape[0]):
         mass = jnp.where(classes == k, rate[k], mass)
     left = lane < HALF
-    flipped[...] = jnp.transpose(jnp.concatenate([mass, mass], axis=0))
-    rows = jnp.where(left, flipped[pl.ds(0, 64, stride=2), :], flipped[pl.ds(1, 64, stride=2), :])
+    flipped[12] = jnp.transpose(jnp.concatenate([mass, mass], axis=0))
+    rows = jnp.where(left, flipped[12, pl.ds(0, 64, stride=2), :], flipped[12, pl.ds(1, 64, stride=2), :])
     mass_pad[0:8, :] = jnp.zeros((8, LANES), F32)
     mass_pad[8 * 65 :, :] = jnp.zeros((16, LANES), F32)
     for r in range(8):
@@ -129,7 +129,7 @@
     base = lax.axis_index("space") * 2
 
     def right(r, c):
-        values = mass * field[c, r].reshape(64, LANES)
+        values = mass * field[r, c].reshape(64, LANES)
         if c == 2:
             return values
         near = coil_x[r] - base
@@ -142,29 +142,20 @@
         strength = jnp.where(row == plus, amp[r], jnp.where(row == minus, -amp[r], 0.0))
         return values + jnp.where(lane == coil_z[r], strength, 0.0)
 
-    sends = []
     for c in range(3):
-        parts[c].wait()
         padded[c, 0:8, :] = jnp.zeros((8, LANES), F32)
         padded[c, 8 * 65 :, :] = jnp.zeros((16, LANES), F32)
         for r in range(4):
-            flipped[...] = jnp.transpose(jnp.concatenate([right(r, c), right(r + 4, c)], axis=0))
-            even = flipped[pl.ds(0, 64, stride=2), :]
-            odd = flipped[pl.ds(1, 64, stride=2), :]
+            flipped[c * 4 + r] = jnp.transpose(jnp.concatenate([right(r, c), right(r + 4, c)], axis=0))
+            even = flipped[c * 4 + r, pl.ds(0, 64, stride=2), :]
+            odd = flipped[c * 4 + r, pl.ds(1, 64, stride=2), :]
             padded[c, pl.ds(8 + r, 64, stride=8), :] = jnp.where(left, even, turn(odd, HALF))
             padded[c, pl.ds(12 + r, 64, stride=8), :] = jnp.where(left, turn(even, HALF), odd)
-        sends += [(padded.at[c, 64 * d : 64 * d + 80], out.at[d, 80 * c : 80 * c + 80]) for d in range(8)]
-        if c == 1:
-            for d in range(8):
-                tiles = [padded[k, 64 * d + 80 : 64 * d + 88, :] for k in range(2)]
-                ghost[8 * d : 8 * d + 8, :] = jnp.where(left[:8], tiles[0], turn(tiles[1], HALF))
-            sends += [(ghost.at[8 * d : 8 * d + 8], out.at[d, 240:248]) for d in range(8)]
-        for i, pair in enumerate(sends):
-            if i >= (0, 8, 24)[c]:
-                sends[i] = pltpu.make_async_copy(*pair, stores.at[i])
-                sends[i].start()
-    for copy in sends:
-        copy.wait()
+        for d in range(8):
+            out[d, 80 * c : 80 * c + 80] = padded[c, 64 * d : 64 * d + 80, :]
+    for d in range(8):
+        tiles = [padded[k, 64 * d + 80 : 64 * d + 88, :] for k in range(2)]
+        out[d, 240:248] = jnp.where(left[:8], tiles[0], turn(tiles[1], HALF))
 
 
 def first_fields(v0, s):
@@ -225,8 +216,10 @@
 
 
 def receive(inner, outer, s, c):
-    even = is_even()
-    return jnp.where(even, outer[s, c], inner[s, c]), jnp.where(even, inner[s, c], outer[s, c])
+    even, index = is_even(), lax.axis_index("space")
+    edge = (index == 0) | (index == lax.axis_size("space") - 1)
+    near, far = inner[s, c], jnp.where(edge, 0.0, outer[s, c])
+    return jnp.where(even, far, near), jnp.where(even, near, far)
 
 
 def inside(values, first_tile, last_tile):
@@ -360,11 +353,13 @@
 
 def energy_kernel(curl, above, moments, out):
     bends = jnp.zeros((128, 192), F32)
+    edge = lax.axis_index("space") == lax.axis_size("space") - 1
     for c in range(2):
         for k in range(0, 8, 2):
             rows = []
             for j in range(2):
                 beyond = jnp.concatenate([unpack(above[:, 1 - c, k + j], half, False) for half in range(2)], axis=0)
+                beyond = jnp.where(edge, 0.0, beyond)
                 bent = curl[:, c, k + j] - beyond if c == 0 else curl[:, c, k + j] + beyond
                 rows.append(bent.reshape(64, LANES))
             bends = bends + bend(jnp.concatenate(thirds(jnp.concatenate(rows, axis=1)), axis=0))
@@ -487,21 +482,20 @@
 def body(lambda_next, class_ids, class_rate, coil_x, coil_y, coil_z, coil_amp):
     size = lax.axis_size("space")
     chips = [(i, i ^ 1) for i in range(size)]
-    fall = [(i + 1, i) for i in range(size - 1)]
-    beside = [pair for i in range(1, size - 1, 2) for pair in ((i, i + 1), (i + 1, i))]
+    fall = [((i + 1) % size, i) for i in range(size)]
+    beside = [pair for i in range(1, size, 2) for pair in ((i, (i + 1) % size), ((i + 1) % size, i))]
     arrays = (lambda_next, class_ids, class_rate, coil_x, coil_y, coil_z, coil_amp)
     spaces = [pltpu.VMEM] + [pltpu.SMEM] * 5
     outgoing, mass = call(
         enter_kernel,
         [(8, 8 * SENT, LANES), (GHOST, 8, LANES)],
-        [(3, 8, 2, PLANE, LANES)]
+        [(8, 3, 2, PLANE, LANES)]
         + [space(a.shape, a.dtype) for space, a in zip(spaces, arrays[1:], strict=True)]
-        + [(LANES, LANES), (3, 67 * 8, LANES), (64, LANES), (67 * 8, LANES)]
-        + [pltpu.SemaphoreType.DMA((9,)), pltpu.SemaphoreType.DMA((32,))],
+        + [(13, LANES, LANES), (3, 67 * 8, LANES), (67 * 8, LANES)]
+        + [pltpu.SemaphoreType.DMA((7,))],
         n_in=7,
         where=pl.ANY,
         limit=60,
-        far=True,
     )(*arrays)
     v0 = exchange(outgoing, "rx").reshape(8, SENT, 8, LANES)
     message = (4, 2, 10, 8, LANES)

time: 146 us -> 143 us (0.979)
  waiting for transfers between devices: 7.98 us -> 2.51 us
  starting transfers between devices: 10.6 us -> 15.1 us
    ppermute x2, starting transfers between devices: 0.19 us -> 8.07 us  [body(): inner = lax.ppermute(inner, 'space', chips)]
    ppermute x1, waiting for transfers between devices: 2.92 us -> 0.01 us  [body(): outer = lax.ppermute(outer, 'space', beside)]
    ppermute x1, starting transfers between devices: 3.36 us -> 0.71 us  [body(): outer = lax.ppermute(outer, 'space', beside)]
    ppermute x1, waiting for transfers between devices: 2.54 us -> 0.01 us  [body(): above = lax.ppermute(down, 'space', fall)]
    ppermute x1, starting transfers between devices: 5.09 us -> 3.27 us  [body(): lax.ppermute(call(functools.partial(message_kernel, True), message)(v0),...]
    ppermute x1, waiting for transfers between devices: 2.52 us -> 0.72 us  [body(): lax.ppermute(call(functools.partial(message_kernel, True), message)(v0),...]
    ppermute x2, waiting for transfers between devices: 0.01 us -> 1.79 us  [body(): inner = lax.ppermute(inner, 'space', chips)]
where the time goes in v4:
time: 143 us
  blocking collectives  102 us (71%)
  Pallas kernels  23.3 us (16%)
  starting transfers between devices  15.1 us (11%)
  waiting for transfers between devices  2.51 us (2%)
    all_to_all x5, blocking collectives, exchange(): return lax.all_to_all(x, axis, split_axis=0, concat_axis=0, tiled=True)  102 us
    pallas_call x4, Pallas kernels, call(): return (lambda *a: done(*a)[0]) if single else done  11.1 us
    ppermute x2, starting transfers between devices, body(): inner = lax.ppermute(inner, 'space', chips)  8.07 us
    ppermute x1, starting transfers between devices, body(): lax.ppermute(call(functools.partial(message_kernel, True), message)(v0),...  3.27 us
    pallas_call x1, Pallas kernels, body(): call(moments_kernel, [(192, LANES), (8, 2, 8, 8, LANES)], [(8, 1, 8, 8, L...  3.2 us
    ppermute x1, starting transfers between devices, body(): above = lax.ppermute(down, 'space', fall)  3.01 us
  transfers between devices with their start and end apart: 5, of which 3 were waited for; matrix products, arithmetic and copies ran while one was open for 0% of the time, Pallas kernels for 5%

profile of v4, /device:TPU:1, one launch (start us, length us, event | category | flops | bytes accessed | tf_op | source)
XLA Modules:
  0.0 143.1 jit_solution(17777865457204449338)
XLA Ops:
  0.0 2.8 %shard_map.73 = (f32[8,248,128]{2,1,0:T(8,128)}, f32[11,8,128]{2,1,0:T(8,128)}) custom-call(f32[8,3,2,32,128]{4,3,2,1,0:T(8,128)} %refs_0_.1, s32[2,32,128]{2,1,0:T(8,128)} %refs_1_.1, f32[16]{0:T(128)} %refs_2_.1, s32[8]{0:T(128)} %refs_3_.1, s32[8]{0:T(128)} %refs_4_.1, s32[8]{0:T(128)} %refs_5_.1, f32[8]{0:T(128)} %refs_6_.1), custom_call_target="tpu_custom_call" | custom-call | bytes 4194304 | tf_op jit(solution)/shard_map/pallas_call | solution.py:489
  2.8 35.6 %all_to_all.25 = f32[8,248,128]{2,1,0:T(8,128)S(1)} all-to-all(f32[8,248,128]{2,1,0:T(8,128)} %get-tuple-element.17), channel_id=1, replica_groups=mesh['space'=32,'rx'=8] {'rx'}, dimensions={0} | all-to-all | bytes 2031616 | tf_op jit(solution)/shard_map/all_to_all | solution.py:468
  38.4 0.7 shard_map.74
  39.2 3.3 %collective-permute-start = (f32[4,2,10,8,128]{4,3,2,1,0:T(8,128)S(1)}, f32[4,2,10,8,128]{4,3,2,1,0:T(8,128)S(1)}, u32[]{:S(2)}, u32[]{:S(2)}) collective-permute-start(f32[4,2,10,8,128]{4,3,2,1,0:T(8,128)S(1)} %shard_map.74), channel_id=1, source_target_pairs={{8,16},{16,8},{24,32},{32,24},{40,48},{48,40},{56,64},{64,56},{72,... | collective-permute-start | bytes 983048 | tf_op jit(solution)/shard_map/ppermute | solution.py:502
  42.4 2.1 %shard_map.75 = (f32[8,3,10,8,128]{4,3,2,1,0:T(8,128)S(1)}, f32[4,2,10,8,128]{4,3,2,1,0:T(8,128)S(1)}) custom-call(f32[8,31,8,128]{3,2,1,0:T(8,128)S(1)} %bitcast.2, f32[11,8,128]{2,1,0:T(8,128)S(1)} %copy-done), custom_call_target="tpu_custom_call" | custom-call | flops 100000000 | bytes 4194304 | tf_op jit(solution)/shard_map/pallas_call | solution.py:503
  44.5 2.2 %collective-permute-start.1 = (f32[4,2,10,8,128]{4,3,2,1,0:T(8,128)S(1)}, f32[4,2,10,8,128]{4,3,2,1,0:T(8,128)S(1)}, u32[]{:S(2)}, u32[]{:S(2)}) collective-permute-start(f32[4,2,10,8,128]{4,3,2,1,0:T(8,128)S(1)} %get-tuple-element.20), channel_id=1, source_target_pairs={{0,8},{8,0},{16,24},{24,16},{32,40},{40,32},{48,56},{56,48},{64,72... | collective-permute-start | bytes 983048 | tf_op jit(solution)/shard_map/ppermute | solution.py:504
  46.8 0.7 collective-permute-done.outer
  47.5 0.5 collective-permute-done.1.inner
  48.0 1.3 shard_map.76
  49.4 0.7 collective-permute-start.2
  50.1 2.0 %shard_map.77 = (f32[8,3,9,8,128]{4,3,2,1,0:T(8,128)S(1)}, f32[4,2,10,8,128]{4,3,2,1,0:T(8,128)S(1)}) custom-call(f32[8,3,10,8,128]{4,3,2,1,0:T(8,128)S(1)} %get-tuple-element.21.v.v1, f32[11,8,128]{2,1,0:T(8,128)S(1)} %copy-done), custom_call_target="tpu_custom_call" | custom-call | flops 100000000 | bytes 4194304 | tf_op jit(solution)/shard_map/pallas_call | solution.py:507
  52.1 5.9 %collective-permute-start.3 = (f32[4,2,10,8,128]{4,3,2,1,0:T(8,128)S(1)}, f32[4,2,10,8,128]{4,3,2,1,0:T(8,128)S(1)}, u32[]{:S(2)}, u32[]{:S(2)}) collective-permute-start(f32[4,2,10,8,128]{4,3,2,1,0:T(8,128)S(1)} %get-tuple-element.24), channel_id=1, source_target_pairs={{0,8},{8,0},{16,24},{24,16},{32,40},{40,32},{48,56},{56,48},{64,72... | collective-permute-start | bytes 983048 | tf_op jit(solution)/shard_map/ppermute | solution.py:508
  58.0 0.0 collective-permute-done.2.outer
  58.0 1.3 collective-permute-done.3.inner
  59.2 0.7 shard_map.78
  59.9 3.0 %collective-permute-start.4 = (f32[4,2,8,8,128]{4,3,2,1,0:T(8,128)S(1)}, f32[4,2,8,8,128]{4,3,2,1,0:T(8,128)S(1)}, u32[]{:S(2)}, u32[]{:S(2)}) collective-permute-start(f32[4,2,8,8,128]{4,3,2,1,0:T(8,128)S(1)} %get-tuple-element.27), channel_id=1, source_target_pairs={{8,0},{16,8},{24,16},{32,24},{40,32},{48,40},{56,48},{64,56},{72,6... | collective-permute-start | bytes 786440 | tf_op jit(solution)/shard_map/ppermute | solution.py:510
  62.9 3.2 %shard_map.79 = (f32[192,128]{1,0:T(8,128)S(1)}, f32[8,2,8,8,128]{4,3,2,1,0:T(8,128)S(1)}) custom-call(f32[8,31,8,128]{3,2,1,0:T(8,128)S(1)} %bitcast.3, f32[8,3,10,8,128]{4,3,2,1,0:T(8,128)S(1)} %get-tuple-element.21.v.v1, f32[8,3,9,8,128]{4,3,2,1,0:T(8,128)S(1)} %get-tuple-element.25.v2, f32[11,8,128]{2,1,0:T(8,128)S(1)} %copy-done), custom_call_target="tpu_custom_call" | custom-call | flops 100000000 | bytes 4194304 | tf_op jit(solution)/shard_map/pallas_call | solution.py:511
  66.1 0.7 shard_map.80
  66.8 18.3 %all_to_all.26 = f32[32,6,128]{2,1,0:T(8,128)S(1)} all-to-all(f32[32,6,128]{2,1,0:T(8,128)S(1)} %reshape.12), channel_id=1, replica_groups=mesh['space'=32,'rx'=8] {'space'}, dimensions={0} | all-to-all | bytes 196608 | tf_op jit(solution)/shard_map/all_to_all | solution.py:468
  85.2 9.5 %all_to_all.27 = f32[8,6,128]{2,1,0:T(8,128)S(1)} all-to-all(f32[8,6,128]{2,1,0:T(8,128)S(1)} %broadcast_in_dim.4), channel_id=1, replica_groups=mesh['space'=32,'rx'=8] {'rx'}, dimensions={0} | all-to-all | bytes 49152 | tf_op jit(solution)/shard_map/all_to_all | solution.py:468
  94.7 12.6 %all_to_all.28 = f32[32,6,128]{2,1,0:T(8,128)S(1)} all-to-all(f32[32,6,128]{2,1,0:T(8,128)S(1)} %broadcast_in_dim.5), channel_id=1, replica_groups=mesh['space'=32,'rx'=8] {'space'}, dimensions={0} | all-to-all | bytes 196608 | tf_op jit(solution)/shard_map/all_to_all | solution.py:468
  107.3 8.4 %shard_map.81 = f32[8,3,8,8,128]{4,3,2,1,0:T(8,128)S(1)} custom-call(f32[192,128]{1,0:T(8,128)S(1)} %reshape.13.moments, f32[8,31,8,128]{3,2,1,0:T(8,128)S(1)} %bitcast.4, f32[8,3,10,8,128]{4,3,2,1,0:T(8,128)S(1)} %get-tuple-element.21.v.v1, f32[8,3,9,8,128]{4,3,2,1,0:T(8,128)S(1)} %get-tuple-element.25.v2), custom_call_target="tpu_custom_call" | custom-call | bytes 4194304 | tf_op jit(solution)/shard_map/pallas_call | solution.py:464
  115.6 26.0 %all_to_all.29.tiles = f32[8,3,8,8,128]{4,3,2,1,0:T(8,128)S(1)} all-to-all(f32[8,3,8,8,128]{4,3,2,1,0:T(8,128)S(1)} %shard_map.81), channel_id=1, replica_groups=mesh['space'=32,'rx'=8] {'rx'}, dimensions={0} | all-to-all | bytes 1572864 | tf_op jit(solution)/shard_map/all_to_all | solution.py:468
  141.6 1.4 shard_map.82
  (9 shorter events, 0.1 us)
Async XLA Ops:
  38.4 4.0 %copy-start = (f32[11,8,128]{2,1,0:T(8,128)S(1)}, f32[11,8,128]{2,1,0:T(8,128)}, u32[]{:S(2)}) copy-start(f32[11,8,128]{2,1,0:T(8,128)} %get-tuple-element.18.mass) | copy-start | bytes 135172
  39.2 8.3 %collective-permute-start = (f32[4,2,10,8,128]{4,3,2,1,0:T(8,128)S(1)}, f32[4,2,10,8,128]{4,3,2,1,0:T(8,128)S(1)}, u32[]{:S(2)}, u32[]{:S(2)}) collective-permute-start(f32[4,2,10,8,128]{4,3,2,1,0:T(8,128)S(1)} %shard_map.74), channel_id=1, source_target_pairs={{8,16},{16,8},{24,32},{32,24},{40,48},{48,40},{56,64},{64,56},{72,... | collective-permute-start | bytes 983048 | tf_op jit(solution)/shard_map/ppermute | solution.py:502
  44.5 3.5 %collective-permute-start.1 = (f32[4,2,10,8,128]{4,3,2,1,0:T(8,128)S(1)}, f32[4,2,10,8,128]{4,3,2,1,0:T(8,128)S(1)}, u32[]{:S(2)}, u32[]{:S(2)}) collective-permute-start(f32[4,2,10,8,128]{4,3,2,1,0:T(8,128)S(1)} %get-tuple-element.20), channel_id=1, source_target_pairs={{0,8},{8,0},{16,24},{24,16},{32,40},{40,32},{48,56},{56,48},{64,72... | collective-permute-start | bytes 983048 | tf_op jit(solution)/shard_map/ppermute | solution.py:504
  49.4 8.6 %collective-permute-start.2 = (f32[4,2,10,8,128]{4,3,2,1,0:T(8,128)S(1)}, f32[4,2,10,8,128]{4,3,2,1,0:T(8,128)S(1)}, u32[]{:S(2)}, u32[]{:S(2)}) collective-permute-start(f32[4,2,10,8,128]{4,3,2,1,0:T(8,128)S(1)} %get-tuple-element.22), channel_id=1, source_target_pairs={{8,16},{16,8},{24,32},{32,24},{40,48},{48,40},{56,64},{64,56},{72,... | collective-permute-start | bytes 983048 | tf_op jit(solution)/shard_map/ppermute | solution.py:506
  52.1 7.1 %collective-permute-start.3 = (f32[4,2,10,8,128]{4,3,2,1,0:T(8,128)S(1)}, f32[4,2,10,8,128]{4,3,2,1,0:T(8,128)S(1)}, u32[]{:S(2)}, u32[]{:S(2)}) collective-permute-start(f32[4,2,10,8,128]{4,3,2,1,0:T(8,128)S(1)} %get-tuple-element.24), channel_id=1, source_target_pairs={{0,8},{8,0},{16,24},{24,16},{32,40},{40,32},{48,56},{56,48},{64,72... | collective-permute-start | bytes 983048 | tf_op jit(solution)/shard_map/ppermute | solution.py:508
  59.9 6.2 %collective-permute-start.4 = (f32[4,2,8,8,128]{4,3,2,1,0:T(8,128)S(1)}, f32[4,2,8,8,128]{4,3,2,1,0:T(8,128)S(1)}, u32[]{:S(2)}, u32[]{:S(2)}) collective-permute-start(f32[4,2,8,8,128]{4,3,2,1,0:T(8,128)S(1)} %get-tuple-element.27), channel_id=1, source_target_pairs={{8,0},{16,8},{24,16},{32,24},{40,32},{48,40},{56,48},{64,56},{72,6... | collective-permute-start | bytes 786440 | tf_op jit(solution)/shard_map/ppermute | solution.py:510

commit v5 on v4

--- a/solution.py
+++ b/solution.py
@@ -298,7 +298,8 @@
     return bends[:64, :64] + 2.0 * (bends[:64, 64:128] + bends[:64, 128:]) + bends[64:, 64:128]
 
 
-def moments_kernel(v0, v1, v2, mass, out, curl, curl0, scaled):
+def moments_kernel(v0, v1, v2, mass, down, out, curl, inner, curl0, scaled):
+    inner[...] = down[...]
     y, x, parity = lane_ids()
     first_x = jnp.where((x == 0) & (lax.axis_index("space") == 0), 1.0, 0.0)
     first_y = jnp.where(y == 0, 1.0, 0.0)
@@ -351,15 +352,15 @@
     out[128:192, :] = jnp.concatenate([block(2, 2), last], axis=1)
 
 
-def energy_kernel(curl, above, moments, out):
+def energy_kernel(outer, curl, inner, moments, out):
     bends = jnp.zeros((128, 192), F32)
-    edge = lax.axis_index("space") == lax.axis_size("space") - 1
+    even, edge = is_even(), lax.axis_index("space") == lax.axis_size("space") - 1
     for c in range(2):
         for k in range(0, 8, 2):
             rows = []
             for j in range(2):
-                beyond = jnp.concatenate([unpack(above[:, 1 - c, k + j], half, False) for half in range(2)], axis=0)
-                beyond = jnp.where(edge, 0.0, beyond)
+                above = jnp.where(even, inner[:, 1 - c, k + j], jnp.where(edge, 0.0, outer[:, 1 - c, k + j]))
+                beyond = jnp.concatenate([unpack(above, half, False) for half in range(2)], axis=0)
                 bent = curl[:, c, k + j] - beyond if c == 0 else curl[:, c, k + j] + beyond
                 rows.append(bent.reshape(64, LANES))
             bends = bends + bend(jnp.concatenate(thirds(jnp.concatenate(rows, axis=1)), axis=0))
@@ -482,8 +483,13 @@
 def body(lambda_next, class_ids, class_rate, coil_x, coil_y, coil_z, coil_amp):
     size = lax.axis_size("space")
     chips = [(i, i ^ 1) for i in range(size)]
-    fall = [((i + 1) % size, i) for i in range(size)]
-    beside = [pair for i in range(1, size, 2) for pair in ((i, (i + 1) % size), ((i + 1) % size, i))]
+    depth = lax.axis_size("rx")
+    beside = []
+    for i in range(size):
+        for z in range(depth):
+            end = i in (0, size - 1)
+            other = (i, z ^ 1) if end else (i + 1 if i % 2 else i - 1, z)
+            beside.append((i * depth + z, other[0] * depth + other[1]))
     arrays = (lambda_next, class_ids, class_rate, coil_x, coil_y, coil_z, coil_amp)
     spaces = [pltpu.VMEM] + [pltpu.SMEM] * 5
     outgoing, mass = call(
@@ -499,19 +505,24 @@
     )(*arrays)
     v0 = exchange(outgoing, "rx").reshape(8, SENT, 8, LANES)
     message = (4, 2, 10, 8, LANES)
-    outer = lax.ppermute(call(functools.partial(message_kernel, True), message)(v0), "space", beside)
+    outer = lax.ppermute(call(functools.partial(message_kernel, True), message)(v0), ("space", "rx"), beside)
     base, inner = call(functools.partial(base_kernel, 0), [(8, 3, 10, 8, LANES), message], n_in=2, flops=10**8)(v0, mass)
     inner = lax.ppermute(inner, "space", chips)
     v1, outer = call(second_kernel, [(8, 3, 10, 8, LANES), message], n_in=3)(outer, base, inner)
-    outer = lax.ppermute(outer, "space", beside)
+    outer = lax.ppermute(outer, ("space", "rx"), beside)
     base, inner = call(functools.partial(base_kernel, 1), [(8, 3, 9, 8, LANES), message], n_in=2, flops=10**8)(v1, mass)
     inner = lax.ppermute(inner, "space", chips)
     v2, down = call(third_kernel, [(8, 3, 9, 8, LANES), (4, 2, 8, 8, LANES)], n_in=3)(outer, base, inner)
-    above = lax.ppermute(down, "space", fall)
-    moments, curl = call(
-        moments_kernel, [(192, LANES), (8, 2, 8, 8, LANES)], [(8, 1, 8, 8, LANES), (8, 3, 8, 8, LANES)], n_in=4, flops=10**8
-    )(v0, v1, v2, mass)
-    moments = call(energy_kernel, (192, LANES), n_in=3)(curl, above, moments)
+    outer = lax.ppermute(down, ("space", "rx"), beside)
+    moments, curl, inner = call(
+        moments_kernel,
+        [(192, LANES), (8, 2, 8, 8, LANES), (4, 2, 8, 8, LANES)],
+        [(8, 1, 8, 8, LANES), (8, 3, 8, 8, LANES)],
+        n_in=5,
+        flops=10**8,
+    )(v0, v1, v2, mass, down)
+    inner = lax.ppermute(inner, "space", chips)
+    moments = call(energy_kernel, (192, LANES), n_in=4)(outer, curl, inner, moments)
     moments = reduce_bricks(moments)
     mixed = call(finish_kernel, (8, 3, 8, 8, LANES), n_in=4)(moments, v0, v1, v2)
     mixed = exchange(mixed, "rx")

time: 143 us -> 140 us (0.979)
  starting transfers between devices: 15.1 us -> 6.42 us
  waiting for transfers between devices: 2.51 us -> 7.61 us
    ppermute x2 -> x3, starting transfers between devices: 8.07 us -> 0.95 us  [body(): inner = lax.ppermute(inner, 'space', chips)]
    ppermute x2, waiting for transfers between devices: 0.01 us -> 4.76 us  [the longest x1 3.48 us: body(): outer = lax.ppermute(outer, ('space', 'rx'), beside)]
    ppermute x1, waiting for transfers between devices: 0.72 us -> 2.84 us  [body(): lax.ppermute(call(functools.partial(message_kernel, True), message)(v0),...]
    ppermute x2 -> x3, waiting for transfers between devices: 1.79 us -> 0.01 us  [body(): inner = lax.ppermute(inner, 'space', chips)]
    ppermute x2, starting transfers between devices: 3.72 us -> 2.2 us  [the longest x1 1.25 us: body(): outer = lax.ppermute(outer, ('space', 'rx'), beside)]
  transfers between devices with their start and end apart: 5 -> 6, of which waited for: 3 -> 3; matrix products, arithmetic and copies ran while one was open for 0% -> 0% of each run, Pallas kernels for 5% -> 5%
where the time goes in v5:
time: 140 us
  blocking collectives  102 us (73%)
  Pallas kernels  23.3 us (17%)
  waiting for transfers between devices  7.61 us (5%)
  starting transfers between devices  6.42 us (5%)
    all_to_all x5, blocking collectives, exchange(): return lax.all_to_all(x, axis, split_axis=0, concat_axis=0, tiled=True)  102 us
    pallas_call x4, Pallas kernels, call(): return (lambda *a: done(*a)[0]) if single else done  11.1 us
    ppermute x1, waiting for transfers between devices, body(): outer = lax.ppermute(outer, ('space', 'rx'), beside)  3.48 us
    ppermute x1, starting transfers between devices, body(): lax.ppermute(call(functools.partial(message_kernel, True), message)(v0),...  3.27 us
    pallas_call x1, Pallas kernels, body(): call(moments_kernel, [(192, LANES), (8, 2, 8, 8, LANES), (4, 2, 8, 8, LAN...  3.23 us
    ppermute x1, waiting for transfers between devices, body(): lax.ppermute(call(functools.partial(message_kernel, True), message)(v0),...  2.84 us
    pallas_call x1, Pallas kernels, body(): call(enter_kernel, [(8, 8 * SENT, LANES), (GHOST, 8, LANES)], [(8, 3, 2,...  2.81 us
  transfers between devices with their start and end apart: 6, of which 3 were waited for; matrix products, arithmetic and copies ran while one was open for 0% of the time, Pallas kernels for 5%

profile of v5, /device:TPU:1, one launch (start us, length us, event | category | flops | bytes accessed | tf_op | source)
XLA Modules:
  0.0 139.7 jit_solution(13654089957302233420)
XLA Ops:
  0.0 2.8 %shard_map.73 = (f32[8,248,128]{2,1,0:T(8,128)}, f32[11,8,128]{2,1,0:T(8,128)}) custom-call(f32[8,3,2,32,128]{4,3,2,1,0:T(8,128)} %refs_0_.1, s32[2,32,128]{2,1,0:T(8,128)} %refs_1_.1, f32[16]{0:T(128)} %refs_2_.1, s32[8]{0:T(128)} %refs_3_.1, s32[8]{0:T(128)} %refs_4_.1, s32[8]{0:T(128)} %refs_5_.1, f32[8]{0:T(128)} %refs_6_.1), custom_call_target="tpu_custom_call" | custom-call | bytes 4194304 | tf_op jit(solution)/shard_map/pallas_call | solution.py:495
  2.8 35.6 %all_to_all.25 = f32[8,248,128]{2,1,0:T(8,128)S(1)} all-to-all(f32[8,248,128]{2,1,0:T(8,128)} %get-tuple-element.18), channel_id=1, replica_groups=mesh['space'=32,'rx'=8] {'rx'}, dimensions={0} | all-to-all | bytes 2031616 | tf_op jit(solution)/shard_map/all_to_all | solution.py:469
  38.4 0.7 shard_map.74
  39.2 3.3 %collective-permute-start = (f32[4,2,10,8,128]{4,3,2,1,0:T(8,128)S(1)}, f32[4,2,10,8,128]{4,3,2,1,0:T(8,128)S(1)}, u32[]{:S(2)}, u32[]{:S(2)}) collective-permute-start(f32[4,2,10,8,128]{4,3,2,1,0:T(8,128)S(1)} %shard_map.74), channel_id=1, source_target_pairs={{0,1},{1,0},{2,3},{3,2},{4,5},{5,4},{6,7},{7,6},{8,16},{9,17},{10,... | collective-permute-start | bytes 983048 | tf_op jit(solution)/shard_map/ppermute | solution.py:508
  42.4 2.1 %shard_map.75 = (f32[8,3,10,8,128]{4,3,2,1,0:T(8,128)S(1)}, f32[4,2,10,8,128]{4,3,2,1,0:T(8,128)S(1)}) custom-call(f32[8,31,8,128]{3,2,1,0:T(8,128)S(1)} %bitcast.2, f32[11,8,128]{2,1,0:T(8,128)S(1)} %copy-done), custom_call_target="tpu_custom_call" | custom-call | flops 100000000 | bytes 4194304 | tf_op jit(solution)/shard_map/pallas_call | solution.py:509
  44.6 0.1 collective-permute-start.1
  44.7 2.8 %collective-permute-done.outer = f32[4,2,10,8,128]{4,3,2,1,0:T(8,128)S(1)} collective-permute-done((f32[4,2,10,8,128]{4,3,2,1,0:T(8,128)S(1)}, f32[4,2,10,8,128]{4,3,2,1,0:T(8,128)S(1)}, u32[]{:S(2)}, u32[]{:S(2)}) %collective-permute-start) | collective-permute-done | bytes 327712 | tf_op jit(solution)/shard_map/ppermute | solution.py:508
  47.5 1.4 shard_map.76
  48.9 1.2 collective-permute-start.2
  50.1 2.0 %shard_map.77 = (f32[8,3,9,8,128]{4,3,2,1,0:T(8,128)S(1)}, f32[4,2,10,8,128]{4,3,2,1,0:T(8,128)S(1)}) custom-call(f32[8,3,10,8,128]{4,3,2,1,0:T(8,128)S(1)} %get-tuple-element.23.v.v1, f32[11,8,128]{2,1,0:T(8,128)S(1)} %copy-done), custom_call_target="tpu_custom_call" | custom-call | flops 100000000 | bytes 4194304 | tf_op jit(solution)/shard_map/pallas_call | solution.py:513
  52.1 0.1 collective-permute-start.3
  52.3 3.5 %collective-permute-done.2.outer = f32[4,2,10,8,128]{4,3,2,1,0:T(8,128)S(1)} collective-permute-done((f32[4,2,10,8,128]{4,3,2,1,0:T(8,128)S(1)}, f32[4,2,10,8,128]{4,3,2,1,0:T(8,128)S(1)}, u32[]{:S(2)}, u32[]{:S(2)}) %collective-permute-start.2) | collective-permute-done | bytes 327712 | tf_op jit(solution)/shard_map/ppermute | solution.py:512
  55.7 0.7 shard_map.78
  56.5 1.0 collective-permute-start.4
  57.4 3.2 %shard_map.79 = (f32[192,128]{1,0:T(8,128)S(1)}, f32[8,2,8,8,128]{4,3,2,1,0:T(8,128)S(1)}, f32[4,2,8,8,128]{4,3,2,1,0:T(8,128)S(1)}) custom-call(f32[8,31,8,128]{3,2,1,0:T(8,128)S(1)} %bitcast.3, f32[8,3,10,8,128]{4,3,2,1,0:T(8,128)S(1)} %get-tuple-element.23.v.v1, f32[8,3,9,8,128]{4,3,2,1,0:T(8,128)S(1)} %get-tuple-element.27.v2, ...), custom_call_target="tpu_custom_call" | custom-call | flops 100000000 | bytes 4194304 | tf_op jit(solution)/shard_map/pallas_call | solution.py:517
  60.6 0.7 collective-permute-start.5
  61.3 1.3 collective-permute-done.4.outer
  62.6 0.7 shard_map.80
  63.3 18.4 %all_to_all.26 = f32[32,6,128]{2,1,0:T(8,128)S(1)} all-to-all(f32[32,6,128]{2,1,0:T(8,128)S(1)} %reshape.12), channel_id=1, replica_groups=mesh['space'=32,'rx'=8] {'space'}, dimensions={0} | all-to-all | bytes 196608 | tf_op jit(solution)/shard_map/all_to_all | solution.py:469
  81.8 9.4 %all_to_all.27 = f32[8,6,128]{2,1,0:T(8,128)S(1)} all-to-all(f32[8,6,128]{2,1,0:T(8,128)S(1)} %broadcast_in_dim.4), channel_id=1, replica_groups=mesh['space'=32,'rx'=8] {'rx'}, dimensions={0} | all-to-all | bytes 49152 | tf_op jit(solution)/shard_map/all_to_all | solution.py:469
  91.2 12.6 %all_to_all.28 = f32[32,6,128]{2,1,0:T(8,128)S(1)} all-to-all(f32[32,6,128]{2,1,0:T(8,128)S(1)} %broadcast_in_dim.5), channel_id=1, replica_groups=mesh['space'=32,'rx'=8] {'space'}, dimensions={0} | all-to-all | bytes 196608 | tf_op jit(solution)/shard_map/all_to_all | solution.py:469
  103.9 8.4 %shard_map.81 = f32[8,3,8,8,128]{4,3,2,1,0:T(8,128)S(1)} custom-call(f32[192,128]{1,0:T(8,128)S(1)} %reshape.13.moments, f32[8,31,8,128]{3,2,1,0:T(8,128)S(1)} %bitcast.4, f32[8,3,10,8,128]{4,3,2,1,0:T(8,128)S(1)} %get-tuple-element.23.v.v1, f32[8,3,9,8,128]{4,3,2,1,0:T(8,128)S(1)} %get-tuple-element.27.v2), custom_call_target="tpu_custom_call" | custom-call | bytes 4194304 | tf_op jit(solution)/shard_map/pallas_call | solution.py:465
  112.2 26.0 %all_to_all.29.tiles = f32[8,3,8,8,128]{4,3,2,1,0:T(8,128)S(1)} all-to-all(f32[8,3,8,8,128]{4,3,2,1,0:T(8,128)S(1)} %shard_map.81), channel_id=1, replica_groups=mesh['space'=32,'rx'=8] {'rx'}, dimensions={0} | all-to-all | bytes 1572864 | tf_op jit(solution)/shard_map/all_to_all | solution.py:469
  138.2 1.4 shard_map.82
  (11 shorter events, 0.1 us)
Async XLA Ops:
  38.4 4.0 %copy-start = (f32[11,8,128]{2,1,0:T(8,128)S(1)}, f32[11,8,128]{2,1,0:T(8,128)}, u32[]{:S(2)}) copy-start(f32[11,8,128]{2,1,0:T(8,128)} %get-tuple-element.19.mass) | copy-start | bytes 135172
  39.2 8.3 %collective-permute-start = (f32[4,2,10,8,128]{4,3,2,1,0:T(8,128)S(1)}, f32[4,2,10,8,128]{4,3,2,1,0:T(8,128)S(1)}, u32[]{:S(2)}, u32[]{:S(2)}) collective-permute-start(f32[4,2,10,8,128]{4,3,2,1,0:T(8,128)S(1)} %shard_map.74), channel_id=1, source_target_pairs={{0,1},{1,0},{2,3},{3,2},{4,5},{5,4},{6,7},{7,6},{8,16},{9,17},{10,... | collective-permute-start | bytes 983048 | tf_op jit(solution)/shard_map/ppermute | solution.py:508
  44.6 2.9 %collective-permute-start.1 = (f32[4,2,10,8,128]{4,3,2,1,0:T(8,128)S(1)}, f32[4,2,10,8,128]{4,3,2,1,0:T(8,128)S(1)}, u32[]{:S(2)}, u32[]{:S(2)}) collective-permute-start(f32[4,2,10,8,128]{4,3,2,1,0:T(8,128)S(1)} %get-tuple-element.21), channel_id=1, source_target_pairs={{0,8},{8,0},{16,24},{24,16},{32,40},{40,32},{48,56},{56,48},{64,72... | collective-permute-start | bytes 983048 | tf_op jit(solution)/shard_map/ppermute | solution.py:510
  48.9 6.9 %collective-permute-start.2 = (f32[4,2,10,8,128]{4,3,2,1,0:T(8,128)S(1)}, f32[4,2,10,8,128]{4,3,2,1,0:T(8,128)S(1)}, u32[]{:S(2)}, u32[]{:S(2)}) collective-permute-start(f32[4,2,10,8,128]{4,3,2,1,0:T(8,128)S(1)} %get-tuple-element.22), channel_id=1, source_target_pairs={{0,1},{1,0},{2,3},{3,2},{4,5},{5,4},{6,7},{7,6},{8,16},{9,17},{10,... | collective-permute-start | bytes 983048 | tf_op jit(solution)/shard_map/ppermute | solution.py:512
  52.1 3.6 %collective-permute-start.3 = (f32[4,2,10,8,128]{4,3,2,1,0:T(8,128)S(1)}, f32[4,2,10,8,128]{4,3,2,1,0:T(8,128)S(1)}, u32[]{:S(2)}, u32[]{:S(2)}) collective-permute-start(f32[4,2,10,8,128]{4,3,2,1,0:T(8,128)S(1)} %get-tuple-element.25), channel_id=1, source_target_pairs={{0,8},{8,0},{16,24},{24,16},{32,40},{40,32},{48,56},{56,48},{64,72... | collective-permute-start | bytes 983048 | tf_op jit(solution)/shard_map/ppermute | solution.py:514
  56.5 6.2 %collective-permute-start.4 = (f32[4,2,8,8,128]{4,3,2,1,0:T(8,128)S(1)}, f32[4,2,8,8,128]{4,3,2,1,0:T(8,128)S(1)}, u32[]{:S(2)}, u32[]{:S(2)}) collective-permute-start(f32[4,2,8,8,128]{4,3,2,1,0:T(8,128)S(1)} %get-tuple-element.26.down), channel_id=1, source_target_pairs={{0,1},{1,0},{2,3},{3,2},{4,5},{5,4},{6,7},{7,6},{8,16},{9,17},{10,... | collective-permute-start | bytes 786440 | tf_op jit(solution)/shard_map/ppermute | solution.py:516
  60.6 2.0 %collective-permute-start.5 = (f32[4,2,8,8,128]{4,3,2,1,0:T(8,128)S(1)}, f32[4,2,8,8,128]{4,3,2,1,0:T(8,128)S(1)}, u32[]{:S(2)}, u32[]{:S(2)}) collective-permute-start(f32[4,2,8,8,128]{4,3,2,1,0:T(8,128)S(1)} %get-tuple-element.29), channel_id=1, source_target_pairs={{0,8},{8,0},{16,24},{24,16},{32,40},{40,32},{48,56},{56,48},{64,72... | collective-permute-start | bytes 786440 | tf_op jit(solution)/shard_map/ppermute | solution.py:524

commit v6 on v5

--- a/solution.py
+++ b/solution.py
@@ -108,7 +108,7 @@
     copies = [pltpu.make_async_copy(source, field, loads.at[6]), *copies]
     for copy in copies:
         copy.start()
-    for copy in copies:
+    for copy in copies[1:]:
         copy.wait()
     ids, rate, coil_x, coil_y, coil_z, amp = targets
     lane = lax.broadcasted_iota(jnp.int32, (64, LANES), 1)
@@ -127,6 +127,7 @@
     first = pl.multiple_of(lax.axis_index("rx") * 64, 64)
     mass_out[...] = mass_pad[pl.ds(first, 8 * GHOST), :].reshape(GHOST, 8, LANES) - SHIFT
     base = lax.axis_index("space") * 2
+    copies[0].wait()
 
     def right(r, c):
         values = mass * field[r, c].reshape(64, LANES)
@@ -290,12 +291,26 @@
     return jnp.concatenate([at(first + k).reshape(64, LANES) for k in range(2)], axis=1)
 
 
-def bend(parts):
-    return lax.dot_general(parts[:128], parts, NT, preferred_element_type=F32)
-
-
-def fold(bends):
-    return bends[:64, :64] + 2.0 * (bends[:64, 64:128] + bends[:64, 128:]) + bends[64:, 64:128]
+SIX = ((0, 0), (0, 1), (1, 0), (1, 1), (0, 2), (2, 0))
+
+
+def six(products):
+    return sum(products[64 * i : 64 * i + 64, 64 * j : 64 * j + 64] for i, j in SIX)
+
+
+def squares(tiles):
+    parts = jnp.concatenate(thirds(tiles), axis=0)
+    return lax.dot_general(parts, parts, NT, preferred_element_type=F32)
+
+
+def square_ids():
+    shape = (64, 64)
+    return lax.broadcasted_iota(jnp.int32, shape, 0), lax.broadcasted_iota(jnp.int32, shape, 1)
+
+
+def diagonal(a):
+    row, column = square_ids()
+    return jnp.sum(jnp.where(row == column, a, 0.0), axis=0, keepdims=True)
 
 
 def moments_kernel(v0, v1, v2, mass, down, out, curl, inner, curl0, scaled):
@@ -321,7 +336,7 @@
         return carry
 
     lax.fori_loop(0, 8, step, 0)
-    bends = jnp.zeros((128, 192), F32)
+    bends = jnp.zeros((192, 192), F32)
     mixed = jnp.zeros((192, 192), F32)
     total = jnp.zeros((192, 576), F32)
     middles = jnp.zeros((192, 192), F32)
@@ -337,23 +352,24 @@
             field = jnp.concatenate([a[128:] for a in parts], axis=0)
             mixed = mixed + lax.dot_general(wide, field, NT, preferred_element_type=F32)
             if c == 0:
-                bends = bends + bend(jnp.concatenate(thirds(columns(curl0, c, k)), axis=0))
+                bends = bends + squares(columns(curl0, c, k))
     main, cross = total[:, :192] + middles, total[:, 192:384] + total[:, 384:]
-    last = fold(bends)
-    for i, j in ((0, 0), (0, 1), (1, 0), (1, 1), (0, 2), (2, 0)):
-        last = last + mixed[64 * i : 64 * i + 64, 64 * j : 64 * j + 64]
+    cross = cross + jnp.transpose(jnp.concatenate([cross, jnp.zeros((192, 64), F32)], axis=1))[:192, :]
+    total = main + cross
 
     def block(i, j):
-        at = lambda m, p, q: m[64 * p : 64 * p + 64, 64 * q : 64 * q + 64]
-        return at(main, i, j) + at(cross, i, j) + at(cross, j, i)
-
-    out[0:64, :] = jnp.concatenate([block(0, 0), block(0, 1)], axis=1)
-    out[64:128, :] = jnp.concatenate([block(1, 1), block(1, 2)], axis=1)
-    out[128:192, :] = jnp.concatenate([block(2, 2), last], axis=1)
+        return total[64 * i : 64 * i + 64, 64 * j : 64 * j + 64]
+
+    n = [block(0, 0), block(0, 1), block(1, 1), block(1, 2), block(2, 2), six(bends) + six(mixed)]
+    row, column = square_ids()
+    packed = [jnp.where(row <= column, n[2 * i], n[2 * i + 1]) for i in range(3)]
+    diagonals = jnp.concatenate([diagonal(n[1]), diagonal(n[3]), diagonal(n[5]), jnp.zeros((61, 64), F32)], axis=0)
+    out[0:64, :] = jnp.concatenate(packed[:2], axis=1)
+    out[64:128, :] = jnp.concatenate([packed[2], diagonals], axis=1)
 
 
 def energy_kernel(outer, curl, inner, moments, out):
-    bends = jnp.zeros((128, 192), F32)
+    bends = jnp.zeros((192, 192), F32)
     even, edge = is_even(), lax.axis_index("space") == lax.axis_size("space") - 1
     for c in range(2):
         for k in range(0, 8, 2):
@@ -363,9 +379,13 @@
                 beyond = jnp.concatenate([unpack(above, half, False) for half in range(2)], axis=0)
                 bent = curl[:, c, k + j] - beyond if c == 0 else curl[:, c, k + j] + beyond
                 rows.append(bent.reshape(64, LANES))
-            bends = bends + bend(jnp.concatenate(thirds(jnp.concatenate(rows, axis=1)), axis=0))
-    out[0:128, :] = moments[0:128, :]
-    out[128:192, :] = moments[128:192, :] + jnp.concatenate([jnp.zeros((64, 64), F32), fold(bends)], axis=1)
+            bends = bends + squares(jnp.concatenate(rows, axis=1))
+    last = six(bends)
+    row, column = square_ids()
+    lower = jnp.where(row > column, last, 0.0)
+    third = jnp.where(row == 2, diagonal(last), 0.0)
+    out[0:64, :] = moments[0:64, :]
+    out[64:128, :] = moments[64:128, :] + jnp.concatenate([lower, third], axis=1)
 
 
 def spread(a, lane):
@@ -376,21 +396,21 @@
     return jnp.broadcast_to(a[k : k + 1], (8, LANES))
 
 
-def invert(matrix):
+def invert(matrix, nothing):
     unit = lax.broadcasted_iota(jnp.int32, (64, 64), 0) == lax.broadcasted_iota(jnp.int32, (64, 64), 1)
     both = jnp.concatenate([matrix, jnp.where(unit, 1.0, 0.0)], axis=1)
     tiles = [both[8 * i : 8 * i + 8] for i in range(8)]
-    origin = list(tiles)
     sub = lax.broadcasted_iota(jnp.int32, (8, LANES), 0)
     lane = lax.broadcasted_iota(jnp.int32, (8, LANES), 1)
     zero = jnp.zeros((8, LANES), F32)
+    own = [jnp.sum(jnp.where(lane == sub + 8 * p, tiles[p], 0.0), axis=1, keepdims=True) for p in range(8)]
+    floors = [jnp.broadcast_to(a * 2e-7, (8, LANES)) + nothing for a in own]
     for p in range(8):
         rows, first = tiles[p], 8 * p
-        cols = [spread(rows, first + k) for k in range(8)]
+        cols = [spread(rows, first + k) + nothing for k in range(8)]
         for k in range(8):
-            floor = line(spread(origin[p], first + k), k) * 2e-7
             pivot = line(cols[k], k)
-            inverse = jnp.where(pivot > floor, 1.0 / pivot, 0.0)
+            inverse = jnp.where(pivot > line(floors[p], k), 1.0 / pivot, 0.0)
             own, hit = cols[k], sub == k
             for j in range(k + 1, 8):
                 scaled = line(cols[j], k) * inverse
@@ -411,29 +431,32 @@
     return jnp.concatenate(tiles, axis=0)[:, 64:]
 
 
-def solve_blocks(n, h):
-    first = multiply(invert(h[0]), jnp.concatenate([h[1], h[2], n[0]], axis=1))
+def solve_blocks(n, h, nothing):
+    first = multiply(invert(h[0], nothing), jnp.concatenate([h[1], h[2], n[0]], axis=1))
     change = multiply(jnp.concatenate([h[1], h[2]], axis=0), first)
     second = jnp.concatenate([h[2], h[3], n[1]], axis=1) - change[:64]
     third = jnp.concatenate([h[3], h[4], n[2]], axis=1) - change[64:]
     below = third[:, :64]
-    second = multiply(invert(second[:, :64]), second[:, 64:])
+    second = multiply(invert(second[:, :64], nothing), second[:, 64:])
     third = third[:, 64:] - multiply(below, second)
-    y2 = multiply(invert(third[:, :64]), third[:, 64:])
+    y2 = multiply(invert(third[:, :64], nothing), third[:, 64:])
     y1 = second[:, 64:] - multiply(second[:, :64], y2)
     y0 = first[:, 128:] - multiply(first[:, :64], y1) - multiply(first[:, 64:128], y2)
     return jnp.concatenate([y0, y1, y2], axis=0)
 
 
-def finish_kernel(moments, v0, v1, v2, out):
+def finish_kernel(moments, v0, v1, v2, out, zeros):
+    zeros[...] = jnp.zeros((8, LANES), F32)
+    row, column = square_ids()
+    one, two = moments[0:64, :], moments[64:128, :]
+    turned = [jnp.transpose(jnp.concatenate([a, a], axis=0))[:, :64] for a in (one, two)]
+    pairs = [(one[:, :64], turned[0][:64]), (one[:, 64:], turned[0][64:]), (two[:, :64], turned[1][:64])]
     n = []
-    for b in range(3):
-        block = moments[64 * b : 64 * b + 64, :]
-        other = jnp.transpose(jnp.concatenate([block, block], axis=0))
-        n.append(0.5 * (block[:, :64] + other[:64, :64]))
-        n.append(0.5 * (block[:, 64:] + other[64:, :64]))
+    for i, (block, other) in enumerate(pairs):
+        n.append(jnp.where(row <= column, block, other))
+        n.append(jnp.where(row > column, block, jnp.where(row < column, other, two[i : i + 1, 64:])))
     h = [n[m + 1] + SHIFT * n[m] for m in range(5)]
-    solved = solve_blocks(n, h)
+    solved = solve_blocks(n, h, zeros[...])
     weights = jnp.transpose(jnp.concatenate([solved, solved], axis=1))[64:]
     high, low = halves(weights)
     both = jnp.concatenate([high, low], axis=0)
@@ -516,15 +539,15 @@
     outer = lax.ppermute(down, ("space", "rx"), beside)
     moments, curl, inner = call(
         moments_kernel,
-        [(192, LANES), (8, 2, 8, 8, LANES), (4, 2, 8, 8, LANES)],
+        [(128, LANES), (8, 2, 8, 8, LANES), (4, 2, 8, 8, LANES)],
         [(8, 1, 8, 8, LANES), (8, 3, 8, 8, LANES)],
         n_in=5,
         flops=10**8,
     )(v0, v1, v2, mass, down)
     inner = lax.ppermute(inner, "space", chips)
-    moments = call(energy_kernel, (192, LANES), n_in=4)(outer, curl, inner, moments)
+    moments = call(energy_kernel, (128, LANES), n_in=4)(outer, curl, inner, moments)
     moments = reduce_bricks(moments)
-    mixed = call(finish_kernel, (8, 3, 8, 8, LANES), n_in=4)(moments, v0, v1, v2)
+    mixed = call(finish_kernel, (8, 3, 8, 8, LANES), [(8, LANES)], n_in=4)(moments, v0, v1, v2)
     mixed = exchange(mixed, "rx")
     scratch = [(512, LANES), (LANES, LANES), (3, 8, 2, PLANE, LANES), pltpu.SemaphoreType.DMA((3,))]
     return call(leave_kernel, (8, 3, 2, PLANE, LANES), scratch, far=True)(mixed)

time: 140 us -> 138 us (0.986)
  transfers between devices with their start and end apart: 6 -> 6, of which waited for: 3 -> 4; matrix products, arithmetic and copies ran while one was open for 0% -> 0% of each run, Pallas kernels for 5% -> 6%
where the time goes in v6:
time: 138 us
  blocking collectives  101 us (73%)
  Pallas kernels  23 us (17%)
  waiting for transfers between devices  7.48 us (5%)
  starting transfers between devices  6.41 us (5%)
    all_to_all x5, blocking collectives, exchange(): return lax.all_to_all(x, axis, split_axis=0, concat_axis=0, tiled=True)  101 us
    pallas_call x4, Pallas kernels, call(): return (lambda *a: done(*a)[0]) if single else done  10.4 us
    pallas_call x1, Pallas kernels, body(): call(moments_kernel, [(128, LANES), (8, 2, 8, 8, LANES), (4, 2, 8, 8, LAN...  3.55 us
    ppermute x1, waiting for transfers between devices, body(): outer = lax.ppermute(outer, ('space', 'rx'), beside)  3.48 us
    ppermute x1, starting transfers between devices, body(): lax.ppermute(call(functools.partial(message_kernel, True), message)(v0),...  3.27 us
    ppermute x1, waiting for transfers between devices, body(): lax.ppermute(call(functools.partial(message_kernel, True), message)(v0),...  2.84 us
    pallas_call x1, Pallas kernels, body(): call(enter_kernel, [(8, 8 * SENT, LANES), (GHOST, 8, LANES)], [(8, 3, 2,...  2.84 us
  transfers between devices with their start and end apart: 6, of which 4 were waited for; matrix products, arithmetic and copies ran while one was open for 0% of the time, Pallas kernels for 6%

profile of v6, /device:TPU:1, one launch (start us, length us, event | category | flops | bytes accessed | tf_op | source)
XLA Modules:
  0.0 138.1 jit_solution(2221311562283116794)
XLA Ops:
  0.0 2.8 %shard_map.73 = (f32[8,248,128]{2,1,0:T(8,128)}, f32[11,8,128]{2,1,0:T(8,128)}) custom-call(f32[8,3,2,32,128]{4,3,2,1,0:T(8,128)} %refs_0_.1, s32[2,32,128]{2,1,0:T(8,128)} %refs_1_.1, f32[16]{0:T(128)} %refs_2_.1, s32[8]{0:T(128)} %refs_3_.1, s32[8]{0:T(128)} %refs_4_.1, s32[8]{0:T(128)} %refs_5_.1, f32[8]{0:T(128)} %refs_6_.1), custom_call_target="tpu_custom_call" | custom-call | bytes 4194304 | tf_op jit(solution)/shard_map/pallas_call | solution.py:518
  2.8 35.6 %all_to_all.25 = f32[8,248,128]{2,1,0:T(8,128)S(1)} all-to-all(f32[8,248,128]{2,1,0:T(8,128)} %get-tuple-element.18), channel_id=1, replica_groups=mesh['space'=32,'rx'=8] {'rx'}, dimensions={0} | all-to-all | bytes 2031616 | tf_op jit(solution)/shard_map/all_to_all | solution.py:492
  38.5 0.7 shard_map.74
  39.2 3.3 %collective-permute-start = (f32[4,2,10,8,128]{4,3,2,1,0:T(8,128)S(1)}, f32[4,2,10,8,128]{4,3,2,1,0:T(8,128)S(1)}, u32[]{:S(2)}, u32[]{:S(2)}) collective-permute-start(f32[4,2,10,8,128]{4,3,2,1,0:T(8,128)S(1)} %shard_map.74), channel_id=1, source_target_pairs={{0,1},{1,0},{2,3},{3,2},{4,5},{5,4},{6,7},{7,6},{8,16},{9,17},{10,... | collective-permute-start | bytes 983048 | tf_op jit(solution)/shard_map/ppermute | solution.py:531
  42.5 2.1 %shard_map.75 = (f32[8,3,10,8,128]{4,3,2,1,0:T(8,128)S(1)}, f32[4,2,10,8,128]{4,3,2,1,0:T(8,128)S(1)}) custom-call(f32[8,31,8,128]{3,2,1,0:T(8,128)S(1)} %bitcast.4, f32[11,8,128]{2,1,0:T(8,128)S(1)} %copy-done), custom_call_target="tpu_custom_call" | custom-call | flops 100000000 | bytes 4194304 | tf_op jit(solution)/shard_map/pallas_call | solution.py:532
  44.7 2.8 %collective-permute-done.outer = f32[4,2,10,8,128]{4,3,2,1,0:T(8,128)S(1)} collective-permute-done((f32[4,2,10,8,128]{4,3,2,1,0:T(8,128)S(1)}, f32[4,2,10,8,128]{4,3,2,1,0:T(8,128)S(1)}, u32[]{:S(2)}, u32[]{:S(2)}) %collective-permute-start) | collective-permute-done | bytes 327712 | tf_op jit(solution)/shard_map/ppermute | solution.py:531
  47.5 1.4 shard_map.76
  48.9 1.2 collective-permute-start.2
  50.1 2.0 %shard_map.77 = (f32[8,3,9,8,128]{4,3,2,1,0:T(8,128)S(1)}, f32[4,2,10,8,128]{4,3,2,1,0:T(8,128)S(1)}) custom-call(f32[8,3,10,8,128]{4,3,2,1,0:T(8,128)S(1)} %get-tuple-element.23.v.v1, f32[11,8,128]{2,1,0:T(8,128)S(1)} %copy-done), custom_call_target="tpu_custom_call" | custom-call | flops 100000000 | bytes 4194304 | tf_op jit(solution)/shard_map/pallas_call | solution.py:536
  52.1 0.1 collective-permute-start.3
  52.3 3.5 %collective-permute-done.2.outer = f32[4,2,10,8,128]{4,3,2,1,0:T(8,128)S(1)} collective-permute-done((f32[4,2,10,8,128]{4,3,2,1,0:T(8,128)S(1)}, f32[4,2,10,8,128]{4,3,2,1,0:T(8,128)S(1)}, u32[]{:S(2)}, u32[]{:S(2)}) %collective-permute-start.2) | collective-permute-done | bytes 327712 | tf_op jit(solution)/shard_map/ppermute | solution.py:535
  55.8 0.7 shard_map.78
  56.5 1.0 collective-permute-start.4
  57.4 3.6 %shard_map.79 = (f32[128,128]{1,0:T(8,128)S(1)}, f32[8,2,8,8,128]{4,3,2,1,0:T(8,128)S(1)}, f32[4,2,8,8,128]{4,3,2,1,0:T(8,128)S(1)}) custom-call(f32[8,31,8,128]{3,2,1,0:T(8,128)S(1)} %bitcast.5, f32[8,3,10,8,128]{4,3,2,1,0:T(8,128)S(1)} %get-tuple-element.23.v.v1, f32[8,3,9,8,128]{4,3,2,1,0:T(8,128)S(1)} %get-tuple-element.27.v2, ...), custom_call_target="tpu_custom_call" | custom-call | flops 100000000 | bytes 4194304 | tf_op jit(solution)/shard_map/pallas_call | solution.py:540
  61.0 0.7 collective-permute-start.5
  61.7 1.0 collective-permute-done.4.outer
  62.7 0.2 collective-permute-done.5.inner
  62.9 0.6 shard_map.80
  63.5 17.9 %all_to_all.26 = f32[32,4,128]{2,1,0:T(4,128)S(1)} all-to-all(f32[32,4,128]{2,1,0:T(4,128)S(1)} %bitcast.8), channel_id=1, replica_groups=mesh['space'=32,'rx'=8] {'space'}, dimensions={0} | all-to-all | bytes 131072 | tf_op jit(solution)/shard_map/all_to_all | solution.py:492
  81.4 9.1 %all_to_all.27 = f32[8,4,128]{2,1,0:T(4,128)S(1)} all-to-all(f32[8,4,128]{2,1,0:T(4,128)S(1)} %broadcast_in_dim.4), channel_id=1, replica_groups=mesh['space'=32,'rx'=8] {'rx'}, dimensions={0} | all-to-all | bytes 32768 | tf_op jit(solution)/shard_map/all_to_all | solution.py:492
  90.5 12.3 %all_to_all.28 = f32[32,4,128]{2,1,0:T(4,128)S(1)} all-to-all(f32[32,4,128]{2,1,0:T(4,128)S(1)} %broadcast_in_dim.5), channel_id=1, replica_groups=mesh['space'=32,'rx'=8] {'space'}, dimensions={0} | all-to-all | bytes 131072 | tf_op jit(solution)/shard_map/all_to_all | solution.py:492
  102.8 7.7 %shard_map.81 = f32[8,3,8,8,128]{4,3,2,1,0:T(8,128)S(1)} custom-call(f32[128,128]{1,0:T(8,128)S(1)} %bitcast.7, f32[8,31,8,128]{3,2,1,0:T(8,128)S(1)} %bitcast.6, f32[8,3,10,8,128]{4,3,2,1,0:T(8,128)S(1)} %get-tuple-element.23.v.v1, f32[8,3,9,8,128]{4,3,2,1,0:T(8,128)S(1)} %get-tuple-element.27.v2), custom_call_target="tpu_custom_call" | custom-call | bytes 4194304 | tf_op jit(solution)/shard_map/pallas_call | solution.py:488
  110.5 26.0 %all_to_all.29.tiles = f32[8,3,8,8,128]{4,3,2,1,0:T(8,128)S(1)} all-to-all(f32[8,3,8,8,128]{4,3,2,1,0:T(8,128)S(1)} %shard_map.81), channel_id=1, replica_groups=mesh['space'=32,'rx'=8] {'rx'}, dimensions={0} | all-to-all | bytes 1572864 | tf_op jit(solution)/shard_map/all_to_all | solution.py:492
  136.5 1.4 shard_map.82
  (9 shorter events, 0.2 us)
Async XLA Ops:
  38.5 4.0 %copy-start = (f32[11,8,128]{2,1,0:T(8,128)S(1)}, f32[11,8,128]{2,1,0:T(8,128)}, u32[]{:S(2)}) copy-start(f32[11,8,128]{2,1,0:T(8,128)} %get-tuple-element.19.mass) | copy-start | bytes 135172
  39.2 8.3 %collective-permute-start = (f32[4,2,10,8,128]{4,3,2,1,0:T(8,128)S(1)}, f32[4,2,10,8,128]{4,3,2,1,0:T(8,128)S(1)}, u32[]{:S(2)}, u32[]{:S(2)}) collective-permute-start(f32[4,2,10,8,128]{4,3,2,1,0:T(8,128)S(1)} %shard_map.74), channel_id=1, source_target_pairs={{0,1},{1,0},{2,3},{3,2},{4,5},{5,4},{6,7},{7,6},{8,16},{9,17},{10,... | collective-permute-start | bytes 983048 | tf_op jit(solution)/shard_map/ppermute | solution.py:531
  44.6 2.9 %collective-permute-start.1 = (f32[4,2,10,8,128]{4,3,2,1,0:T(8,128)S(1)}, f32[4,2,10,8,128]{4,3,2,1,0:T(8,128)S(1)}, u32[]{:S(2)}, u32[]{:S(2)}) collective-permute-start(f32[4,2,10,8,128]{4,3,2,1,0:T(8,128)S(1)} %get-tuple-element.21), channel_id=1, source_target_pairs={{0,8},{8,0},{16,24},{24,16},{32,40},{40,32},{48,56},{56,48},{64,72... | collective-permute-start | bytes 983048 | tf_op jit(solution)/shard_map/ppermute | solution.py:533
  48.9 6.9 %collective-permute-start.2 = (f32[4,2,10,8,128]{4,3,2,1,0:T(8,128)S(1)}, f32[4,2,10,8,128]{4,3,2,1,0:T(8,128)S(1)}, u32[]{:S(2)}, u32[]{:S(2)}) collective-permute-start(f32[4,2,10,8,128]{4,3,2,1,0:T(8,128)S(1)} %get-tuple-element.22), channel_id=1, source_target_pairs={{0,1},{1,0},{2,3},{3,2},{4,5},{5,4},{6,7},{7,6},{8,16},{9,17},{10,... | collective-permute-start | bytes 983048 | tf_op jit(solution)/shard_map/ppermute | solution.py:535
  52.1 3.6 %collective-permute-start.3 = (f32[4,2,10,8,128]{4,3,2,1,0:T(8,128)S(1)}, f32[4,2,10,8,128]{4,3,2,1,0:T(8,128)S(1)}, u32[]{:S(2)}, u32[]{:S(2)}) collective-permute-start(f32[4,2,10,8,128]{4,3,2,1,0:T(8,128)S(1)} %get-tuple-element.25), channel_id=1, source_target_pairs={{0,8},{8,0},{16,24},{24,16},{32,40},{40,32},{48,56},{56,48},{64,72... | collective-permute-start | bytes 983048 | tf_op jit(solution)/shard_map/ppermute | solution.py:537
  56.5 6.2 %collective-permute-start.4 = (f32[4,2,8,8,128]{4,3,2,1,0:T(8,128)S(1)}, f32[4,2,8,8,128]{4,3,2,1,0:T(8,128)S(1)}, u32[]{:S(2)}, u32[]{:S(2)}) collective-permute-start(f32[4,2,8,8,128]{4,3,2,1,0:T(8,128)S(1)} %get-tuple-element.26.down), channel_id=1, source_target_pairs={{0,1},{1,0},{2,3},{3,2},{4,5},{5,4},{6,7},{7,6},{8,16},{9,17},{10,... | collective-permute-start | bytes 786440 | tf_op jit(solution)/shard_map/ppermute | solution.py:539
  61.0 1.9 %collective-permute-start.5 = (f32[4,2,8,8,128]{4,3,2,1,0:T(8,128)S(1)}, f32[4,2,8,8,128]{4,3,2,1,0:T(8,128)S(1)}, u32[]{:S(2)}, u32[]{:S(2)}) collective-permute-start(f32[4,2,8,8,128]{4,3,2,1,0:T(8,128)S(1)} %get-tuple-element.29), channel_id=1, source_target_pairs={{0,8},{8,0},{16,24},{24,16},{32,40},{40,32},{48,56},{56,48},{64,72... | collective-permute-start | bytes 786440 | tf_op jit(solution)/shard_map/ppermute | solution.py:547

commit v7 on v6

--- a/solution.py
+++ b/solution.py
@@ -313,8 +313,7 @@
     return jnp.sum(jnp.where(row == column, a, 0.0), axis=0, keepdims=True)
 
 
-def moments_kernel(v0, v1, v2, mass, down, out, curl, inner, curl0, scaled):
-    inner[...] = down[...]
+def moments_kernel(v0, v1, v2, mass, out, curl, curl0, scaled):
     y, x, parity = lane_ids()
     first_x = jnp.where((x == 0) & (lax.axis_index("space") == 0), 1.0, 0.0)
     first_y = jnp.where(y == 0, 1.0, 0.0)
@@ -368,15 +367,15 @@
     out[64:128, :] = jnp.concatenate([packed[2], diagonals], axis=1)
 
 
-def energy_kernel(outer, curl, inner, moments, out):
+def energy_kernel(curl, above, moments, out):
     bends = jnp.zeros((192, 192), F32)
-    even, edge = is_even(), lax.axis_index("space") == lax.axis_size("space") - 1
+    edge = lax.axis_index("space") == lax.axis_size("space") - 1
     for c in range(2):
         for k in range(0, 8, 2):
             rows = []
             for j in range(2):
-                above = jnp.where(even, inner[:, 1 - c, k + j], jnp.where(edge, 0.0, outer[:, 1 - c, k + j]))
-                beyond = jnp.concatenate([unpack(above, half, False) for half in range(2)], axis=0)
+                message = jnp.where(edge, 0.0, above[:, 1 - c, k + j])
+                beyond = jnp.concatenate([unpack(message, half, False) for half in range(2)], axis=0)
                 bent = curl[:, c, k + j] - beyond if c == 0 else curl[:, c, k + j] + beyond
                 rows.append(bent.reshape(64, LANES))
             bends = bends + squares(jnp.concatenate(rows, axis=1))
@@ -536,16 +535,15 @@
     base, inner = call(functools.partial(base_kernel, 1), [(8, 3, 9, 8, LANES), message], n_in=2, flops=10**8)(v1, mass)
     inner = lax.ppermute(inner, "space", chips)
     v2, down = call(third_kernel, [(8, 3, 9, 8, LANES), (4, 2, 8, 8, LANES)], n_in=3)(outer, base, inner)
-    outer = lax.ppermute(down, ("space", "rx"), beside)
-    moments, curl, inner = call(
+    above = lax.ppermute(down, "space", [((i + 1) % size, i) for i in range(size)])
+    moments, curl = call(
         moments_kernel,
-        [(128, LANES), (8, 2, 8, 8, LANES), (4, 2, 8, 8, LANES)],
+        [(128, LANES), (8, 2, 8, 8, LANES)],
         [(8, 1, 8, 8, LANES), (8, 3, 8, 8, LANES)],
-        n_in=5,
+        n_in=4,
         flops=10**8,
-    )(v0, v1, v2, mass, down)
-    inner = lax.ppermute(inner, "space", chips)
-    moments = call(energy_kernel, (128, LANES), n_in=4)(outer, curl, inner, moments)
+    )(v0, v1, v2, mass)
+    moments = call(energy_kernel, (128, LANES), n_in=3)(curl, above, moments)
     moments = reduce_bricks(moments)
     mixed = call(finish_kernel, (8, 3, 8, 8, LANES), [(8, LANES)], n_in=4)(moments, v0, v1, v2)
     mixed = exchange(mixed, "rx")

time: 138 us -> 138 us (level)
  transfers between devices with their start and end apart: 6 -> 5, of which waited for: 4 -> 3; matrix products, arithmetic and copies ran while one was open for 0% -> 0% of each run, Pallas kernels for 6% -> 6%
where the time goes in v7:
time: 138 us
  blocking collectives  101 us (73%)
  Pallas kernels  22.9 us (17%)
  waiting for transfers between devices  7.67 us (6%)
  starting transfers between devices  5.75 us (4%)
    all_to_all x5, blocking collectives, exchange(): return lax.all_to_all(x, axis, split_axis=0, concat_axis=0, tiled=True)  101 us
    pallas_call x4, Pallas kernels, call(): return (lambda *a: done(*a)[0]) if single else done  10.4 us
    pallas_call x1, Pallas kernels, body(): call(moments_kernel, [(128, LANES), (8, 2, 8, 8, LANES)], [(8, 1, 8, 8, L...  3.53 us
    ppermute x1, waiting for transfers between devices, body(): outer = lax.ppermute(outer, ('space', 'rx'), beside)  3.48 us
    ppermute x1, starting transfers between devices, body(): lax.ppermute(call(functools.partial(message_kernel, True), message)(v0),...  3.27 us
    ppermute x1, waiting for transfers between devices, body(): lax.ppermute(call(functools.partial(message_kernel, True), message)(v0),...  2.84 us
    pallas_call x1, Pallas kernels, body(): call(enter_kernel, [(8, 8 * SENT, LANES), (GHOST, 8, LANES)], [(8, 3, 2,...  2.82 us
  transfers between devices with their start and end apart: 5, of which 3 were waited for; matrix products, arithmetic and copies ran while one was open for 0% of the time, Pallas kernels for 6%

profile of v7, /device:TPU:1, one launch (start us, length us, event | category | flops | bytes accessed | tf_op | source)
XLA Modules:
  0.0 138.0 jit_solution(9110549559607920550)
XLA Ops:
  0.0 2.8 %shard_map.73 = (f32[8,248,128]{2,1,0:T(8,128)}, f32[11,8,128]{2,1,0:T(8,128)}) custom-call(f32[8,3,2,32,128]{4,3,2,1,0:T(8,128)} %refs_0_.1, s32[2,32,128]{2,1,0:T(8,128)} %refs_1_.1, f32[16]{0:T(128)} %refs_2_.1, s32[8]{0:T(128)} %refs_3_.1, s32[8]{0:T(128)} %refs_4_.1, s32[8]{0:T(128)} %refs_5_.1, f32[8]{0:T(128)} %refs_6_.1), custom_call_target="tpu_custom_call" | custom-call | bytes 4194304 | tf_op jit(solution)/shard_map/pallas_call | solution.py:517
  2.8 35.6 %all_to_all.25 = f32[8,248,128]{2,1,0:T(8,128)S(1)} all-to-all(f32[8,248,128]{2,1,0:T(8,128)} %get-tuple-element.17), channel_id=1, replica_groups=mesh['space'=32,'rx'=8] {'rx'}, dimensions={0} | all-to-all | bytes 2031616 | tf_op jit(solution)/shard_map/all_to_all | solution.py:491
  38.5 0.7 shard_map.74
  39.2 3.3 %collective-permute-start = (f32[4,2,10,8,128]{4,3,2,1,0:T(8,128)S(1)}, f32[4,2,10,8,128]{4,3,2,1,0:T(8,128)S(1)}, u32[]{:S(2)}, u32[]{:S(2)}) collective-permute-start(f32[4,2,10,8,128]{4,3,2,1,0:T(8,128)S(1)} %shard_map.74), channel_id=1, source_target_pairs={{0,1},{1,0},{2,3},{3,2},{4,5},{5,4},{6,7},{7,6},{8,16},{9,17},{10,... | collective-permute-start | bytes 983048 | tf_op jit(solution)/shard_map/ppermute | solution.py:530
  42.5 2.1 %shard_map.75 = (f32[8,3,10,8,128]{4,3,2,1,0:T(8,128)S(1)}, f32[4,2,10,8,128]{4,3,2,1,0:T(8,128)S(1)}) custom-call(f32[8,31,8,128]{3,2,1,0:T(8,128)S(1)} %bitcast.4, f32[11,8,128]{2,1,0:T(8,128)S(1)} %copy-done), custom_call_target="tpu_custom_call" | custom-call | flops 100000000 | bytes 4194304 | tf_op jit(solution)/shard_map/pallas_call | solution.py:531
  44.6 0.1 collective-permute-start.1
  44.7 2.8 %collective-permute-done.outer = f32[4,2,10,8,128]{4,3,2,1,0:T(8,128)S(1)} collective-permute-done((f32[4,2,10,8,128]{4,3,2,1,0:T(8,128)S(1)}, f32[4,2,10,8,128]{4,3,2,1,0:T(8,128)S(1)}, u32[]{:S(2)}, u32[]{:S(2)}) %collective-permute-start) | collective-permute-done | bytes 327712 | tf_op jit(solution)/shard_map/ppermute | solution.py:530
  47.5 0.0 collective-permute-done.1.inner
  47.5 1.4 shard_map.76
  48.9 1.2 collective-permute-start.2
  50.1 2.0 %shard_map.77 = (f32[8,3,9,8,128]{4,3,2,1,0:T(8,128)S(1)}, f32[4,2,10,8,128]{4,3,2,1,0:T(8,128)S(1)}) custom-call(f32[8,3,10,8,128]{4,3,2,1,0:T(8,128)S(1)} %get-tuple-element.21.v.v1, f32[11,8,128]{2,1,0:T(8,128)S(1)} %copy-done), custom_call_target="tpu_custom_call" | custom-call | flops 100000000 | bytes 4194304 | tf_op jit(solution)/shard_map/pallas_call | solution.py:535
  52.1 0.1 collective-permute-start.3
  52.3 3.5 %collective-permute-done.2.outer = f32[4,2,10,8,128]{4,3,2,1,0:T(8,128)S(1)} collective-permute-done((f32[4,2,10,8,128]{4,3,2,1,0:T(8,128)S(1)}, f32[4,2,10,8,128]{4,3,2,1,0:T(8,128)S(1)}, u32[]{:S(2)}, u32[]{:S(2)}) %collective-permute-start.2) | collective-permute-done | bytes 327712 | tf_op jit(solution)/shard_map/ppermute | solution.py:534
  55.8 0.7 shard_map.78
  56.5 1.0 collective-permute-start.4
  57.5 3.5 %shard_map.79 = (f32[128,128]{1,0:T(8,128)S(1)}, f32[8,2,8,8,128]{4,3,2,1,0:T(8,128)S(1)}) custom-call(f32[8,31,8,128]{3,2,1,0:T(8,128)S(1)} %bitcast.5, f32[8,3,10,8,128]{4,3,2,1,0:T(8,128)S(1)} %get-tuple-element.21.v.v1, f32[8,3,9,8,128]{4,3,2,1,0:T(8,128)S(1)} %get-tuple-element.25.v2, f32[11,8,128]{2,1,0:T(8,128)S(1)} %copy-done), custom_call_target="tpu_custom_call" | custom-call | flops 100000000 | bytes 4194304 | tf_op jit(solution)/shard_map/pallas_call | solution.py:539
  61.0 1.3 collective-permute-done.4.above
  62.3 0.6 shard_map.80
  63.0 18.3 %all_to_all.26 = f32[32,4,128]{2,1,0:T(4,128)S(1)} all-to-all(f32[32,4,128]{2,1,0:T(4,128)S(1)} %bitcast.8), channel_id=1, replica_groups=mesh['space'=32,'rx'=8] {'space'}, dimensions={0} | all-to-all | bytes 131072 | tf_op jit(solution)/shard_map/all_to_all | solution.py:491
  81.4 9.1 %all_to_all.27 = f32[8,4,128]{2,1,0:T(4,128)S(1)} all-to-all(f32[8,4,128]{2,1,0:T(4,128)S(1)} %broadcast_in_dim.4), channel_id=1, replica_groups=mesh['space'=32,'rx'=8] {'rx'}, dimensions={0} | all-to-all | bytes 32768 | tf_op jit(solution)/shard_map/all_to_all | solution.py:491
  90.5 12.3 %all_to_all.28 = f32[32,4,128]{2,1,0:T(4,128)S(1)} all-to-all(f32[32,4,128]{2,1,0:T(4,128)S(1)} %broadcast_in_dim.5), channel_id=1, replica_groups=mesh['space'=32,'rx'=8] {'space'}, dimensions={0} | all-to-all | bytes 131072 | tf_op jit(solution)/shard_map/all_to_all | solution.py:491
  102.8 7.7 %shard_map.81 = f32[8,3,8,8,128]{4,3,2,1,0:T(8,128)S(1)} custom-call(f32[128,128]{1,0:T(8,128)S(1)} %bitcast.7, f32[8,31,8,128]{3,2,1,0:T(8,128)S(1)} %bitcast.6, f32[8,3,10,8,128]{4,3,2,1,0:T(8,128)S(1)} %get-tuple-element.21.v.v1, f32[8,3,9,8,128]{4,3,2,1,0:T(8,128)S(1)} %get-tuple-element.25.v2), custom_call_target="tpu_custom_call" | custom-call | bytes 4194304 | tf_op jit(solution)/shard_map/pallas_call | solution.py:487
  110.5 26.0 %all_to_all.29.tiles = f32[8,3,8,8,128]{4,3,2,1,0:T(8,128)S(1)} all-to-all(f32[8,3,8,8,128]{4,3,2,1,0:T(8,128)S(1)} %shard_map.81), channel_id=1, replica_groups=mesh['space'=32,'rx'=8] {'rx'}, dimensions={0} | all-to-all | bytes 1572864 | tf_op jit(solution)/shard_map/all_to_all | solution.py:491
  136.5 1.4 shard_map.82
  (7 shorter events, 0.1 us)
Async XLA Ops:
  38.5 4.0 %copy-start = (f32[11,8,128]{2,1,0:T(8,128)S(1)}, f32[11,8,128]{2,1,0:T(8,128)}, u32[]{:S(2)}) copy-start(f32[11,8,128]{2,1,0:T(8,128)} %get-tuple-element.18.mass) | copy-start | bytes 135172
  39.2 8.3 %collective-permute-start = (f32[4,2,10,8,128]{4,3,2,1,0:T(8,128)S(1)}, f32[4,2,10,8,128]{4,3,2,1,0:T(8,128)S(1)}, u32[]{:S(2)}, u32[]{:S(2)}) collective-permute-start(f32[4,2,10,8,128]{4,3,2,1,0:T(8,128)S(1)} %shard_map.74), channel_id=1, source_target_pairs={{0,1},{1,0},{2,3},{3,2},{4,5},{5,4},{6,7},{7,6},{8,16},{9,17},{10,... | collective-permute-start | bytes 983048 | tf_op jit(solution)/shard_map/ppermute | solution.py:530
  44.6 2.9 %collective-permute-start.1 = (f32[4,2,10,8,128]{4,3,2,1,0:T(8,128)S(1)}, f32[4,2,10,8,128]{4,3,2,1,0:T(8,128)S(1)}, u32[]{:S(2)}, u32[]{:S(2)}) collective-permute-start(f32[4,2,10,8,128]{4,3,2,1,0:T(8,128)S(1)} %get-tuple-element.20), channel_id=1, source_target_pairs={{0,8},{8,0},{16,24},{24,16},{32,40},{40,32},{48,56},{56,48},{64,72... | collective-permute-start | bytes 983048 | tf_op jit(solution)/shard_map/ppermute | solution.py:532
  48.9 6.9 %collective-permute-start.2 = (f32[4,2,10,8,128]{4,3,2,1,0:T(8,128)S(1)}, f32[4,2,10,8,128]{4,3,2,1,0:T(8,128)S(1)}, u32[]{:S(2)}, u32[]{:S(2)}) collective-permute-start(f32[4,2,10,8,128]{4,3,2,1,0:T(8,128)S(1)} %get-tuple-element.22), channel_id=1, source_target_pairs={{0,1},{1,0},{2,3},{3,2},{4,5},{5,4},{6,7},{7,6},{8,16},{9,17},{10,... | collective-permute-start | bytes 983048 | tf_op jit(solution)/shard_map/ppermute | solution.py:534
  52.1 3.6 %collective-permute-start.3 = (f32[4,2,10,8,128]{4,3,2,1,0:T(8,128)S(1)}, f32[4,2,10,8,128]{4,3,2,1,0:T(8,128)S(1)}, u32[]{:S(2)}, u32[]{:S(2)}) collective-permute-start(f32[4,2,10,8,128]{4,3,2,1,0:T(8,128)S(1)} %get-tuple-element.24), channel_id=1, source_target_pairs={{0,8},{8,0},{16,24},{24,16},{32,40},{40,32},{48,56},{56,48},{64,72... | collective-permute-start | bytes 983048 | tf_op jit(solution)/shard_map/ppermute | solution.py:536
  56.5 5.9 %collective-permute-start.4 = (f32[4,2,8,8,128]{4,3,2,1,0:T(8,128)S(1)}, f32[4,2,8,8,128]{4,3,2,1,0:T(8,128)S(1)}, u32[]{:S(2)}, u32[]{:S(2)}) collective-permute-start(f32[4,2,8,8,128]{4,3,2,1,0:T(8,128)S(1)} %get-tuple-element.27), channel_id=1, source_target_pairs={{8,0},{16,8},{24,16},{32,24},{40,32},{48,40},{56,48},{64,56},{72,6... | collective-permute-start | bytes 786440 | tf_op jit(solution)/shard_map/ppermute | solution.py:538

commit v8 on v7

--- a/solution.py
+++ b/solution.py
@@ -236,13 +236,13 @@
     return jnp.concatenate(pieces, axis=0) if rows else values
 
 
-def base_kernel(first, v, mass, base, inner):
+def base_kernel(v, mass, base, inner):
     def step(s, carry):
         fields = [fields_of(v, s + 4 * k) for k in range(2)]
         for k in range(2):
-            result = apply_tiles(fields[k], mass[: fields[k][0].shape[0]])
+            result = apply_tiles(fields[k], mass[...])
             for c in range(3):
-                base[s + 4 * k, c] = result[c][first : first + base.shape[2]]
+                base[s + 4 * k, c] = result[c][: base.shape[2]]
         send(inner, is_even(), s, *fields)
         return carry
 
@@ -261,26 +261,45 @@
     return [inside(base[s + 4 * k, c] + changes[c][first:], first == 0, True) for c in range(3)]
 
 
-def second_kernel(outer, base, inner, v1, next_outer):
+def at_first(base, inner, outer, s, c, k):
+    return base[s + 4 * k, c + 1] - unpack(receive(inner, outer, s, c)[0], k, True)[10 - base.shape[2] :]
+
+
+def outer_kernel(outer, base, inner, message):
+    def step(s, carry):
+        @pl.when(is_even())
+        def _():
+            for c in range(2):
+                parts = [inside(at_first(base, inner, outer, s, c, k), True, True) for k in range(2)]
+                message[s, c] = pack_down(*parts)
+
+        @pl.when(jnp.logical_not(is_even()))
+        def _():
+            send(message, True, s, *[completed(base, inner, outer, s, k, 0) for k in range(2)])
+
+        return carry
+
+    lax.fori_loop(0, 4, step, 0)
+
+
+def second_kernel(outer, base, inner, mass, v1, next_base, next_inner):
     def step(s, carry):
         fields = [completed(base, inner, outer, s, k, 0) for k in range(2)]
         for k in range(2):
+            result = apply_tiles(fields[k], mass[:10])
             for c in range(3):
                 v1[s + 4 * k, c] = fields[k][c]
-        send(next_outer, jnp.logical_not(is_even()), s, *fields)
+                next_base[s + 4 * k, c] = result[c][1:]
+        send(next_inner, is_even(), s, *fields)
         return carry
 
     lax.fori_loop(0, 4, step, 0)
 
 
-def third_kernel(outer, base, inner, v2, down):
+def down_kernel(outer, base, inner, down):
     def step(s, carry):
-        fields = [completed(base, inner, outer, s, k, 1) for k in range(2)]
-        for k in range(2):
-            for c in range(3):
-                v2[s + 4 * k, c] = fields[k][c]
         for c in range(2):
-            down[s, c] = pack_down(fields[0][c + 1][:8], fields[1][c + 1][:8])
+            down[s, c] = pack_down(*[at_first(base, inner, outer, s, c, k)[:8] for k in range(2)])
         return carry
 
     lax.fori_loop(0, 4, step, 0)
@@ -313,7 +332,7 @@
     return jnp.sum(jnp.where(row == column, a, 0.0), axis=0, keepdims=True)
 
 
-def moments_kernel(v0, v1, v2, mass, out, curl, curl0, scaled):
+def moments_kernel(outer, base, inner, v0, v1, mass, out, curl, v2, curl0, scaled):
     y, x, parity = lane_ids()
     first_x = jnp.where((x == 0) & (lax.axis_index("space") == 0), 1.0, 0.0)
     first_y = jnp.where(y == 0, 1.0, 0.0)
@@ -323,18 +342,21 @@
     faces = [first_y + first_z, first_x + first_z, first_x + first_y]
 
     def step(s, carry):
-        v = [v2[s, c] for c in range(3)]
-        z1 = z_both(v[1])[0][:8]
-        z0 = z_both(v[0])[0][:8]
-        v = [a[:8] for a in v]
-        curl0[s, 0] = y_next(v[2]) - v[2] - z1 + v[1]
-        curl[s, 0] = z0 - v[0] - x_next(v[2], 0.0) + v[2]
-        curl[s, 1] = x_next(v[1], 0.0) - v[1] - y_next(v[0]) + v[0]
-        for c in range(3):
-            scaled[s, c] = v[c] * (own + faces[c])
+        for k in range(2):
+            v, at = completed(base, inner, outer, s, k, 1), s + 4 * k
+            for c in range(3):
+                v2[at, c] = v[c]
+            z1 = z_both(v[1])[0][:8]
+            z0 = z_both(v[0])[0][:8]
+            v = [a[:8] for a in v]
+            curl0[at, 0] = y_next(v[2]) - v[2] - z1 + v[1]
+            curl[at, 0] = z0 - v[0] - x_next(v[2], 0.0) + v[2]
+            curl[at, 1] = x_next(v[1], 0.0) - v[1] - y_next(v[0]) + v[0]
+            for c in range(3):
+                scaled[at, c] = v[c] * (own + faces[c])
         return carry
 
-    lax.fori_loop(0, 8, step, 0)
+    lax.fori_loop(0, 4, step, 0)
     bends = jnp.zeros((192, 192), F32)
     mixed = jnp.zeros((192, 192), F32)
     total = jnp.zeros((192, 576), F32)
@@ -528,21 +550,22 @@
     v0 = exchange(outgoing, "rx").reshape(8, SENT, 8, LANES)
     message = (4, 2, 10, 8, LANES)
     outer = lax.ppermute(call(functools.partial(message_kernel, True), message)(v0), ("space", "rx"), beside)
-    base, inner = call(functools.partial(base_kernel, 0), [(8, 3, 10, 8, LANES), message], n_in=2, flops=10**8)(v0, mass)
+    base, inner = call(base_kernel, [(8, 3, 10, 8, LANES), message], n_in=2, flops=10**8)(v0, mass)
     inner = lax.ppermute(inner, "space", chips)
-    v1, outer = call(second_kernel, [(8, 3, 10, 8, LANES), message], n_in=3)(outer, base, inner)
-    outer = lax.ppermute(outer, ("space", "rx"), beside)
-    base, inner = call(functools.partial(base_kernel, 1), [(8, 3, 9, 8, LANES), message], n_in=2, flops=10**8)(v1, mass)
+    following = call(outer_kernel, message, n_in=3)(outer, base, inner)
+    shapes = [(8, 3, 10, 8, LANES), (8, 3, 9, 8, LANES), message]
+    v1, base, inner = call(second_kernel, shapes, n_in=4, flops=10**8)(outer, base, inner, mass)
+    outer = lax.ppermute(following, ("space", "rx"), beside)
     inner = lax.ppermute(inner, "space", chips)
-    v2, down = call(third_kernel, [(8, 3, 9, 8, LANES), (4, 2, 8, 8, LANES)], n_in=3)(outer, base, inner)
+    down = call(down_kernel, (4, 2, 8, 8, LANES), n_in=3)(outer, base, inner)
     above = lax.ppermute(down, "space", [((i + 1) % size, i) for i in range(size)])
-    moments, curl = call(
+    moments, curl, v2 = call(
         moments_kernel,
-        [(128, LANES), (8, 2, 8, 8, LANES)],
+        [(128, LANES), (8, 2, 8, 8, LANES), (8, 3, 9, 8, LANES)],
         [(8, 1, 8, 8, LANES), (8, 3, 8, 8, LANES)],
-        n_in=4,
+        n_in=6,
         flops=10**8,
-    )(v0, v1, v2, mass)
+    )(outer, base, inner, v0, v1, mass)
     moments = call(energy_kernel, (128, LANES), n_in=3)(curl, above, moments)
     moments = reduce_bricks(moments)
     mixed = call(finish_kernel, (8, 3, 8, 8, LANES), [(8, LANES)], n_in=4)(moments, v0, v1, v2)

time: 138 us -> 138 us (level)
    pallas_call x4 -> x6, Pallas kernels: 10.4 us -> 12.1 us  [call(): return (lambda *a: done(*a)[0]) if single else done]
    pallas_call x5 -> x3, Pallas kernels: 9.69 us -> 8.41 us  [the longest x1 3.93 us: body(): call(moments_kernel, [(128, LANES), (8, 2, 8, 8, LANES), (8, 3, 9, 8, LAN...]
where the time goes in v8:
time: 138 us
  blocking collectives  101 us (73%)
  Pallas kernels  23.3 us (17%)
  waiting for transfers between devices  7.73 us (6%)
  starting transfers between devices  4.9 us (4%)
    all_to_all x5, blocking collectives, exchange(): return lax.all_to_all(x, axis, split_axis=0, concat_axis=0, tiled=True)  101 us
    pallas_call x6, Pallas kernels, call(): return (lambda *a: done(*a)[0]) if single else done  12.1 us
    pallas_call x1, Pallas kernels, body(): call(moments_kernel, [(128, LANES), (8, 2, 8, 8, LANES), (8, 3, 9, 8, LAN...  3.93 us
    ppermute x1, waiting for transfers between devices, body(): outer = lax.ppermute(following, ('space', 'rx'), beside)  3.52 us
    ppermute x1, starting transfers between devices, body(): lax.ppermute(call(functools.partial(message_kernel, True), message)(v0),...  3.27 us
    ppermute x1, waiting for transfers between devices, body(): lax.ppermute(call(functools.partial(message_kernel, True), message)(v0),...  2.84 us
    pallas_call x1, Pallas kernels, body(): call(enter_kernel, [(8, 8 * SENT, LANES), (GHOST, 8, LANES)], [(8, 3, 2,...  2.84 us
  transfers between devices with their start and end apart: 5, of which 3 were waited for; matrix products, arithmetic and copies ran while one was open for 0% of the time, Pallas kernels for 6%

profile of v8, /device:TPU:1, one launch (start us, length us, event | category | flops | bytes accessed | tf_op | source)
XLA Modules:
  0.0 137.6 jit_solution(16462984370227417112)
XLA Ops:
  0.0 2.8 %shard_map.73 = (f32[8,248,128]{2,1,0:T(8,128)}, f32[11,8,128]{2,1,0:T(8,128)}) custom-call(f32[8,3,2,32,128]{4,3,2,1,0:T(8,128)} %refs_0_.1, s32[2,32,128]{2,1,0:T(8,128)} %refs_1_.1, f32[16]{0:T(128)} %refs_2_.1, s32[8]{0:T(128)} %refs_3_.1, s32[8]{0:T(128)} %refs_4_.1, s32[8]{0:T(128)} %refs_5_.1, f32[8]{0:T(128)} %refs_6_.1), custom_call_target="tpu_custom_call" | custom-call | bytes 4194304 | tf_op jit(solution)/shard_map/pallas_call | solution.py:539
  2.8 35.6 %all_to_all.25 = f32[8,248,128]{2,1,0:T(8,128)S(1)} all-to-all(f32[8,248,128]{2,1,0:T(8,128)} %get-tuple-element.15), channel_id=1, replica_groups=mesh['space'=32,'rx'=8] {'rx'}, dimensions={0} | all-to-all | bytes 2031616 | tf_op jit(solution)/shard_map/all_to_all | solution.py:513
  38.5 0.7 shard_map.74
  39.2 3.3 %collective-permute-start = (f32[4,2,10,8,128]{4,3,2,1,0:T(8,128)S(1)}, f32[4,2,10,8,128]{4,3,2,1,0:T(8,128)S(1)}, u32[]{:S(2)}, u32[]{:S(2)}) collective-permute-start(f32[4,2,10,8,128]{4,3,2,1,0:T(8,128)S(1)} %shard_map.74), channel_id=1, source_target_pairs={{0,1},{1,0},{2,3},{3,2},{4,5},{5,4},{6,7},{7,6},{8,16},{9,17},{10,... | collective-permute-start | bytes 983048 | tf_op jit(solution)/shard_map/ppermute | solution.py:552
  42.5 2.1 %shard_map.75 = (f32[8,3,10,8,128]{4,3,2,1,0:T(8,128)S(1)}, f32[4,2,10,8,128]{4,3,2,1,0:T(8,128)S(1)}) custom-call(f32[8,31,8,128]{3,2,1,0:T(8,128)S(1)} %bitcast.4, f32[11,8,128]{2,1,0:T(8,128)S(1)} %copy-done), custom_call_target="tpu_custom_call" | custom-call | flops 100000000 | bytes 4194304 | tf_op jit(solution)/shard_map/pallas_call | solution.py:553
  44.6 0.1 collective-permute-start.1
  44.7 2.8 %collective-permute-done.outer = f32[4,2,10,8,128]{4,3,2,1,0:T(8,128)S(1)} collective-permute-done((f32[4,2,10,8,128]{4,3,2,1,0:T(8,128)S(1)}, f32[4,2,10,8,128]{4,3,2,1,0:T(8,128)S(1)}, u32[]{:S(2)}, u32[]{:S(2)}) %collective-permute-start) | collective-permute-done | bytes 327712 | tf_op jit(solution)/shard_map/ppermute | solution.py:552
  47.5 0.0 collective-permute-done.1.inner
  47.5 1.2 shard_map.76
  48.8 0.8 collective-permute-start.2
  49.6 2.4 %shard_map.77 = (f32[8,3,10,8,128]{4,3,2,1,0:T(8,128)S(1)}, f32[8,3,9,8,128]{4,3,2,1,0:T(8,128)S(1)}, f32[4,2,10,8,128]{4,3,2,1,0:T(8,128)S(1)}) custom-call(f32[4,2,10,8,128]{4,3,2,1,0:T(8,128)S(1)} %collective-permute-done.outer, f32[8,3,10,8,128]{4,3,2,1,0:T(8,128)S(1)} %get-tuple-element.17.base, f32[4,2,10,8,128]{4,3,2,1,0:T(8,128)S(1)} %collective-permute-done.1.inner, ...), custom_call_target="tpu_custom_call" | custom-call | flops 100000000 | bytes 4194304 | tf_op jit(solution)/shard_map/pallas_call | solution.py:557
  52.0 0.1 collective-permute-start.3
  52.1 3.5 %collective-permute-done.2.outer = f32[4,2,10,8,128]{4,3,2,1,0:T(8,128)S(1)} collective-permute-done((f32[4,2,10,8,128]{4,3,2,1,0:T(8,128)S(1)}, f32[4,2,10,8,128]{4,3,2,1,0:T(8,128)S(1)}, u32[]{:S(2)}, u32[]{:S(2)}) %collective-permute-start.2) | collective-permute-done | bytes 327712 | tf_op jit(solution)/shard_map/ppermute | solution.py:558
  55.6 0.4 shard_map.79
  56.1 0.6 collective-permute-start.4
  56.7 3.9 %shard_map.78 = (f32[128,128]{1,0:T(8,128)S(1)}, f32[8,2,8,8,128]{4,3,2,1,0:T(8,128)S(1)}, f32[8,3,9,8,128]{4,3,2,1,0:T(8,128)S(1)}) custom-call(f32[4,2,10,8,128]{4,3,2,1,0:T(8,128)S(1)} %collective-permute-done.2.outer, f32[8,3,9,8,128]{4,3,2,1,0:T(8,128)S(1)} %get-tuple-element.19.base, f32[4,2,10,8,128]{4,3,2,1,0:T(8,128)S(1)} %collective-permute-done.3.inner, ...), custom_call_target="tpu_custom_call" | custom-call | flops 100000000 | bytes 4194304 | tf_op jit(solution)/shard_map/pallas_call | solution.py:562
  60.6 1.4 collective-permute-done.4.above
  62.0 0.6 shard_map.80
  62.6 18.3 %all_to_all.26 = f32[32,4,128]{2,1,0:T(4,128)S(1)} all-to-all(f32[32,4,128]{2,1,0:T(4,128)S(1)} %bitcast.8), channel_id=1, replica_groups=mesh['space'=32,'rx'=8] {'space'}, dimensions={0} | all-to-all | bytes 131072 | tf_op jit(solution)/shard_map/all_to_all | solution.py:513
  81.0 9.1 %all_to_all.27 = f32[8,4,128]{2,1,0:T(4,128)S(1)} all-to-all(f32[8,4,128]{2,1,0:T(4,128)S(1)} %broadcast_in_dim.4), channel_id=1, replica_groups=mesh['space'=32,'rx'=8] {'rx'}, dimensions={0} | all-to-all | bytes 32768 | tf_op jit(solution)/shard_map/all_to_all | solution.py:513
  90.1 12.3 %all_to_all.28 = f32[32,4,128]{2,1,0:T(4,128)S(1)} all-to-all(f32[32,4,128]{2,1,0:T(4,128)S(1)} %broadcast_in_dim.5), channel_id=1, replica_groups=mesh['space'=32,'rx'=8] {'space'}, dimensions={0} | all-to-all | bytes 131072 | tf_op jit(solution)/shard_map/all_to_all | solution.py:513
  102.4 7.7 %shard_map.81 = f32[8,3,8,8,128]{4,3,2,1,0:T(8,128)S(1)} custom-call(f32[128,128]{1,0:T(8,128)S(1)} %bitcast.7, f32[8,31,8,128]{3,2,1,0:T(8,128)S(1)} %bitcast.6, f32[8,3,10,8,128]{4,3,2,1,0:T(8,128)S(1)} %get-tuple-element.21.v1, f32[8,3,9,8,128]{4,3,2,1,0:T(8,128)S(1)} %get-tuple-element.24.v2), custom_call_target="tpu_custom_call" | custom-call | bytes 4194304 | tf_op jit(solution)/shard_map/pallas_call | solution.py:509
  110.1 26.0 %all_to_all.29.tiles = f32[8,3,8,8,128]{4,3,2,1,0:T(8,128)S(1)} all-to-all(f32[8,3,8,8,128]{4,3,2,1,0:T(8,128)S(1)} %shard_map.81), channel_id=1, replica_groups=mesh['space'=32,'rx'=8] {'rx'}, dimensions={0} | all-to-all | bytes 1572864 | tf_op jit(solution)/shard_map/all_to_all | solution.py:513
  136.1 1.4 shard_map.82
  (7 shorter events, 0.1 us)
Async XLA Ops:
  38.5 4.0 %copy-start = (f32[11,8,128]{2,1,0:T(8,128)S(1)}, f32[11,8,128]{2,1,0:T(8,128)}, u32[]{:S(2)}) copy-start(f32[11,8,128]{2,1,0:T(8,128)} %get-tuple-element.16.mass) | copy-start | bytes 135172
  39.2 8.3 %collective-permute-start = (f32[4,2,10,8,128]{4,3,2,1,0:T(8,128)S(1)}, f32[4,2,10,8,128]{4,3,2,1,0:T(8,128)S(1)}, u32[]{:S(2)}, u32[]{:S(2)}) collective-permute-start(f32[4,2,10,8,128]{4,3,2,1,0:T(8,128)S(1)} %shard_map.74), channel_id=1, source_target_pairs={{0,1},{1,0},{2,3},{3,2},{4,5},{5,4},{6,7},{7,6},{8,16},{9,17},{10,... | collective-permute-start | bytes 983048 | tf_op jit(solution)/shard_map/ppermute | solution.py:552
  44.6 2.9 %collective-permute-start.1 = (f32[4,2,10,8,128]{4,3,2,1,0:T(8,128)S(1)}, f32[4,2,10,8,128]{4,3,2,1,0:T(8,128)S(1)}, u32[]{:S(2)}, u32[]{:S(2)}) collective-permute-start(f32[4,2,10,8,128]{4,3,2,1,0:T(8,128)S(1)} %get-tuple-element.18), channel_id=1, source_target_pairs={{0,8},{8,0},{16,24},{24,16},{32,40},{40,32},{48,56},{56,48},{64,72... | collective-permute-start | bytes 983048 | tf_op jit(solution)/shard_map/ppermute | solution.py:554
  48.8 6.9 %collective-permute-start.2 = (f32[4,2,10,8,128]{4,3,2,1,0:T(8,128)S(1)}, f32[4,2,10,8,128]{4,3,2,1,0:T(8,128)S(1)}, u32[]{:S(2)}, u32[]{:S(2)}) collective-permute-start(f32[4,2,10,8,128]{4,3,2,1,0:T(8,128)S(1)} %shard_map.76), channel_id=1, source_target_pairs={{0,1},{1,0},{2,3},{3,2},{4,5},{5,4},{6,7},{7,6},{8,16},{9,17},{10,... | collective-permute-start | bytes 983048 | tf_op jit(solution)/shard_map/ppermute | solution.py:558
  52.0 3.7 %collective-permute-start.3 = (f32[4,2,10,8,128]{4,3,2,1,0:T(8,128)S(1)}, f32[4,2,10,8,128]{4,3,2,1,0:T(8,128)S(1)}, u32[]{:S(2)}, u32[]{:S(2)}) collective-permute-start(f32[4,2,10,8,128]{4,3,2,1,0:T(8,128)S(1)} %get-tuple-element.20), channel_id=1, source_target_pairs={{0,8},{8,0},{16,24},{24,16},{32,40},{40,32},{48,56},{56,48},{64,72... | collective-permute-start | bytes 983048 | tf_op jit(solution)/shard_map/ppermute | solution.py:559
  56.1 5.9 %collective-permute-start.4 = (f32[4,2,8,8,128]{4,3,2,1,0:T(8,128)S(1)}, f32[4,2,8,8,128]{4,3,2,1,0:T(8,128)S(1)}, u32[]{:S(2)}, u32[]{:S(2)}) collective-permute-start(f32[4,2,8,8,128]{4,3,2,1,0:T(8,128)S(1)} %shard_map.79), channel_id=1, source_target_pairs={{8,0},{16,8},{24,16},{32,24},{40,32},{48,40},{56,48},{64,56},{72,6... | collective-permute-start | bytes 786440 | tf_op jit(solution)/shard_map/ppermute | solution.py:561

commit v9 on v8

--- a/solution.py
+++ b/solution.py
@@ -417,7 +417,22 @@
     return jnp.broadcast_to(a[k : k + 1], (8, LANES))
 
 
-def invert(matrix, nothing):
+def tall_multiply(a, b):
+    ah, am, al = thirds(a)
+    bh, bm, bl = thirds(b)
+    dot = lambda x, y: lax.dot_general(x, y, NN, preferred_element_type=F32)
+    rows = a.shape[0]
+    one = dot(jnp.concatenate([ah, am, al], axis=0), bh)
+    two = dot(jnp.concatenate([ah, am], axis=0), bm)
+    corner = dot(ah, bl)
+    return ((one[:rows] + one[rows : 2 * rows]) + (one[2 * rows :] + two[:rows])) + (two[rows:] + corner)
+
+
+def total(f):
+    return ((f[0] + f[1]) + (f[2] + f[3])) + ((f[4] + f[5]) + (f[6] + f[7]))
+
+
+def invert(matrix):
     unit = lax.broadcasted_iota(jnp.int32, (64, 64), 0) == lax.broadcasted_iota(jnp.int32, (64, 64), 1)
     both = jnp.concatenate([matrix, jnp.where(unit, 1.0, 0.0)], axis=1)
     tiles = [both[8 * i : 8 * i + 8] for i in range(8)]
@@ -425,49 +440,64 @@
     lane = lax.broadcasted_iota(jnp.int32, (8, LANES), 1)
     zero = jnp.zeros((8, LANES), F32)
     own = [jnp.sum(jnp.where(lane == sub + 8 * p, tiles[p], 0.0), axis=1, keepdims=True) for p in range(8)]
-    floors = [jnp.broadcast_to(a * 2e-7, (8, LANES)) + nothing for a in own]
+    floors = [jnp.broadcast_to(a * 2e-7, (8, LANES)) for a in own]
+    cols = [spread(tiles[0], k) for k in range(8)]
+    raw, scaled = [], []
     for p in range(8):
-        rows, first = tiles[p], 8 * p
-        cols = [spread(rows, first + k) + nothing for k in range(8)]
+        rows, first, after = tiles[p], 8 * p, p + 1
+        raw.append(rows)
+        aside, near, far = [], list(range(after, min(after + 2, 8))), list(range(after + 2, 8))
+        if near:
+            factors = {i: [spread(tiles[i], first + k) for k in range(8)] for i in near}
+            aside = [spread(rows, first + 8 + k) for k in range(8)]
+            ahead = [spread(tiles[after], first + 8 + k) for k in range(8)]
         for k in range(8):
             pivot = line(cols[k], k)
             inverse = jnp.where(pivot > line(floors[p], k), 1.0 / pivot, 0.0)
-            own, hit = cols[k], sub == k
+            column, hit = cols[k], sub == k
+
+            def eliminate(x):
+                top = line(x, k) * inverse
+                return jnp.where(hit, top, x - column * top)
+
             for j in range(k + 1, 8):
-                scaled = line(cols[j], k) * inverse
-                cols[j] = jnp.where(hit, scaled, cols[j] - own * scaled)
-            scaled = line(rows, k) * inverse
-            rows = jnp.where(hit, scaled, rows - own * scaled)
-        tiles[p] = rows
-        inside_panel = (lane >= first) & (lane < first + 8)
-        apart = [zero if i in (p, p + 1) else jnp.where(inside_panel, tiles[i], 0.0) for i in range(8)]
-        placed = [rows if i == p else zero for i in range(8)]
-        change = multiply(jnp.concatenate(apart, axis=0)[:, :64], jnp.concatenate(placed, axis=0))
-        for i in range(8):
-            if i == p + 1:
-                f = [spread(tiles[i], first + k) * line(rows, k) for k in range(8)]
-                tiles[i] = tiles[i] - (((f[0] + f[1]) + (f[2] + f[3])) + ((f[4] + f[5]) + (f[6] + f[7])))
-            elif i != p:
-                tiles[i] = tiles[i] - change[8 * i : 8 * i + 8]
-    return jnp.concatenate(tiles, axis=0)[:, 64:]
-
-
-def solve_blocks(n, h, nothing):
-    first = multiply(invert(h[0], nothing), jnp.concatenate([h[1], h[2], n[0]], axis=1))
+                cols[j] = eliminate(cols[j])
+            rows = eliminate(rows)
+            aside = [eliminate(x) for x in aside]
+        scaled.append(rows)
+        if not near:
+            break
+        lines = [line(rows, k) for k in range(8)]
+        cols = [ahead[j] - total([factors[after][k] * line(aside[j], k) for k in range(8)]) for j in range(8)]
+        tiles = list(tiles)
+        if far:
+            panel = (lane >= first) & (lane < first + 8)
+            apart = jnp.concatenate([jnp.where(panel, tiles[i], 0.0) for i in far], axis=0)[:, :64]
+            change = tall_multiply(apart, jnp.concatenate([rows if i == p else zero for i in range(8)], axis=0))
+            for n, i in enumerate(far):
+                tiles[i] = tiles[i] - change[8 * n : 8 * n + 8]
+        for i in near:
+            tiles[i] = tiles[i] - total([factors[i][k] * lines[k] for k in range(8)])
+    left = jnp.concatenate(raw, axis=0)
+    left = jnp.transpose(jnp.concatenate([left, left], axis=0))[64:, :64]
+    return multiply(left, jnp.concatenate(scaled, axis=0)[:, 64:])
+
+
+def solve_blocks(n, h):
+    first = multiply(invert(h[0]), jnp.concatenate([h[1], h[2], n[0]], axis=1))
     change = multiply(jnp.concatenate([h[1], h[2]], axis=0), first)
     second = jnp.concatenate([h[2], h[3], n[1]], axis=1) - change[:64]
     third = jnp.concatenate([h[3], h[4], n[2]], axis=1) - change[64:]
     below = third[:, :64]
-    second = multiply(invert(second[:, :64], nothing), second[:, 64:])
+    second = multiply(invert(second[:, :64]), second[:, 64:])
     third = third[:, 64:] - multiply(below, second)
-    y2 = multiply(invert(third[:, :64], nothing), third[:, 64:])
+    y2 = multiply(invert(third[:, :64]), third[:, 64:])
     y1 = second[:, 64:] - multiply(second[:, :64], y2)
     y0 = first[:, 128:] - multiply(first[:, :64], y1) - multiply(first[:, 64:128], y2)
     return jnp.concatenate([y0, y1, y2], axis=0)
 
 
-def finish_kernel(moments, v0, v1, v2, out, zeros):
-    zeros[...] = jnp.zeros((8, LANES), F32)
+def finish_kernel(moments, v0, v1, v2, out):
     row, column = square_ids()
     one, two = moments[0:64, :], moments[64:128, :]
     turned = [jnp.transpose(jnp.concatenate([a, a], axis=0))[:, :64] for a in (one, two)]
@@ -477,7 +507,7 @@
         n.append(jnp.where(row <= column, block, other))
         n.append(jnp.where(row > column, block, jnp.where(row < column, other, two[i : i + 1, 64:])))
     h = [n[m + 1] + SHIFT * n[m] for m in range(5)]
-    solved = solve_blocks(n, h, zeros[...])
+    solved = solve_blocks(n, h)
     weights = jnp.transpose(jnp.concatenate([solved, solved], axis=1))[64:]
     high, low = halves(weights)
     both = jnp.concatenate([high, low], axis=0)
@@ -568,7 +598,7 @@
     )(outer, base, inner, v0, v1, mass)
     moments = call(energy_kernel, (128, LANES), n_in=3)(curl, above, moments)
     moments = reduce_bricks(moments)
-    mixed = call(finish_kernel, (8, 3, 8, 8, LANES), [(8, LANES)], n_in=4)(moments, v0, v1, v2)
+    mixed = call(finish_kernel, (8, 3, 8, 8, LANES), n_in=4)(moments, v0, v1, v2)
     mixed = exchange(mixed, "rx")
     scratch = [(512, LANES), (LANES, LANES), (3, 8, 2, PLANE, LANES), pltpu.SemaphoreType.DMA((3,))]
     return call(leave_kernel, (8, 3, 2, PLANE, LANES), scratch, far=True)(mixed)

time: 138 us -> 138 us (level)
  no operation moved by 1% of the time
where the time goes in v9:
time: 138 us
  blocking collectives  101 us (73%)
  Pallas kernels  23.3 us (17%)
  waiting for transfers between devices  7.73 us (6%)
  starting transfers between devices  4.9 us (4%)
    all_to_all x5, blocking collectives, exchange(): return lax.all_to_all(x, axis, split_axis=0, concat_axis=0, tiled=True)  101 us
    pallas_call x6, Pallas kernels, call(): return (lambda *a: done(*a)[0]) if single else done  12 us
    pallas_call x1, Pallas kernels, body(): call(moments_kernel, [(128, LANES), (8, 2, 8, 8, LANES), (8, 3, 9, 8, LAN...  3.93 us
    ppermute x1, waiting for transfers between devices, body(): outer = lax.ppermute(following, ('space', 'rx'), beside)  3.52 us
    ppermute x1, starting transfers between devices, body(): lax.ppermute(call(functools.partial(message_kernel, True), message)(v0),...  3.27 us
    ppermute x1, waiting for transfers between devices, body(): lax.ppermute(call(functools.partial(message_kernel, True), message)(v0),...  2.84 us
    pallas_call x1, Pallas kernels, body(): call(enter_kernel, [(8, 8 * SENT, LANES), (GHOST, 8, LANES)], [(8, 3, 2,...  2.84 us
  transfers between devices with their start and end apart: 5, of which 3 were waited for; matrix products, arithmetic and copies ran while one was open for 0% of the time, Pallas kernels for 6%

profile of v9, /device:TPU:1, one launch (start us, length us, event | category | flops | bytes accessed | tf_op | source)
XLA Modules:
  0.0 137.6 jit_solution(15634065039230781218)
XLA Ops:
  0.0 2.8 %shard_map.73 = (f32[8,248,128]{2,1,0:T(8,128)}, f32[11,8,128]{2,1,0:T(8,128)}) custom-call(f32[8,3,2,32,128]{4,3,2,1,0:T(8,128)} %refs_0_.1, s32[2,32,128]{2,1,0:T(8,128)} %refs_1_.1, f32[16]{0:T(128)} %refs_2_.1, s32[8]{0:T(128)} %refs_3_.1, s32[8]{0:T(128)} %refs_4_.1, s32[8]{0:T(128)} %refs_5_.1, f32[8]{0:T(128)} %refs_6_.1), custom_call_target="tpu_custom_call" | custom-call | bytes 4194304 | tf_op jit(solution)/shard_map/pallas_call | solution.py:569
  2.8 35.6 %all_to_all.25 = f32[8,248,128]{2,1,0:T(8,128)S(1)} all-to-all(f32[8,248,128]{2,1,0:T(8,128)} %get-tuple-element.15), channel_id=1, replica_groups=mesh['space'=32,'rx'=8] {'rx'}, dimensions={0} | all-to-all | bytes 2031616 | tf_op jit(solution)/shard_map/all_to_all | solution.py:543
  38.5 0.7 shard_map.74
  39.2 3.3 %collective-permute-start = (f32[4,2,10,8,128]{4,3,2,1,0:T(8,128)S(1)}, f32[4,2,10,8,128]{4,3,2,1,0:T(8,128)S(1)}, u32[]{:S(2)}, u32[]{:S(2)}) collective-permute-start(f32[4,2,10,8,128]{4,3,2,1,0:T(8,128)S(1)} %shard_map.74), channel_id=1, source_target_pairs={{0,1},{1,0},{2,3},{3,2},{4,5},{5,4},{6,7},{7,6},{8,16},{9,17},{10,... | collective-permute-start | bytes 983048 | tf_op jit(solution)/shard_map/ppermute | solution.py:582
  42.5 2.1 %shard_map.75 = (f32[8,3,10,8,128]{4,3,2,1,0:T(8,128)S(1)}, f32[4,2,10,8,128]{4,3,2,1,0:T(8,128)S(1)}) custom-call(f32[8,31,8,128]{3,2,1,0:T(8,128)S(1)} %bitcast.4, f32[11,8,128]{2,1,0:T(8,128)S(1)} %copy-done), custom_call_target="tpu_custom_call" | custom-call | flops 100000000 | bytes 4194304 | tf_op jit(solution)/shard_map/pallas_call | solution.py:583
  44.6 0.1 collective-permute-start.1
  44.7 2.8 %collective-permute-done.outer = f32[4,2,10,8,128]{4,3,2,1,0:T(8,128)S(1)} collective-permute-done((f32[4,2,10,8,128]{4,3,2,1,0:T(8,128)S(1)}, f32[4,2,10,8,128]{4,3,2,1,0:T(8,128)S(1)}, u32[]{:S(2)}, u32[]{:S(2)}) %collective-permute-start) | collective-permute-done | bytes 327712 | tf_op jit(solution)/shard_map/ppermute | solution.py:582
  47.5 0.0 collective-permute-done.1.inner
  47.5 1.2 shard_map.76
  48.8 0.8 collective-permute-start.2
  49.6 2.4 %shard_map.77 = (f32[8,3,10,8,128]{4,3,2,1,0:T(8,128)S(1)}, f32[8,3,9,8,128]{4,3,2,1,0:T(8,128)S(1)}, f32[4,2,10,8,128]{4,3,2,1,0:T(8,128)S(1)}) custom-call(f32[4,2,10,8,128]{4,3,2,1,0:T(8,128)S(1)} %collective-permute-done.outer, f32[8,3,10,8,128]{4,3,2,1,0:T(8,128)S(1)} %get-tuple-element.17.base, f32[4,2,10,8,128]{4,3,2,1,0:T(8,128)S(1)} %collective-permute-done.1.inner, ...), custom_call_target="tpu_custom_call" | custom-call | flops 100000000 | bytes 4194304 | tf_op jit(solution)/shard_map/pallas_call | solution.py:587
  52.0 0.1 collective-permute-start.3
  52.1 3.5 %collective-permute-done.2.outer = f32[4,2,10,8,128]{4,3,2,1,0:T(8,128)S(1)} collective-permute-done((f32[4,2,10,8,128]{4,3,2,1,0:T(8,128)S(1)}, f32[4,2,10,8,128]{4,3,2,1,0:T(8,128)S(1)}, u32[]{:S(2)}, u32[]{:S(2)}) %collective-permute-start.2) | collective-permute-done | bytes 327712 | tf_op jit(solution)/shard_map/ppermute | solution.py:588
  55.6 0.4 shard_map.79
  56.1 0.6 collective-permute-start.4
  56.7 3.9 %shard_map.78 = (f32[128,128]{1,0:T(8,128)S(1)}, f32[8,2,8,8,128]{4,3,2,1,0:T(8,128)S(1)}, f32[8,3,9,8,128]{4,3,2,1,0:T(8,128)S(1)}) custom-call(f32[4,2,10,8,128]{4,3,2,1,0:T(8,128)S(1)} %collective-permute-done.2.outer, f32[8,3,9,8,128]{4,3,2,1,0:T(8,128)S(1)} %get-tuple-element.19.base, f32[4,2,10,8,128]{4,3,2,1,0:T(8,128)S(1)} %collective-permute-done.3.inner, ...), custom_call_target="tpu_custom_call" | custom-call | flops 100000000 | bytes 4194304 | tf_op jit(solution)/shard_map/pallas_call | solution.py:592
  60.6 1.4 collective-permute-done.4.above
  62.0 0.6 shard_map.80
  62.6 18.3 %all_to_all.26 = f32[32,4,128]{2,1,0:T(4,128)S(1)} all-to-all(f32[32,4,128]{2,1,0:T(4,128)S(1)} %bitcast.8), channel_id=1, replica_groups=mesh['space'=32,'rx'=8] {'space'}, dimensions={0} | all-to-all | bytes 131072 | tf_op jit(solution)/shard_map/all_to_all | solution.py:543
  81.0 9.1 %all_to_all.27 = f32[8,4,128]{2,1,0:T(4,128)S(1)} all-to-all(f32[8,4,128]{2,1,0:T(4,128)S(1)} %broadcast_in_dim.4), channel_id=1, replica_groups=mesh['space'=32,'rx'=8] {'rx'}, dimensions={0} | all-to-all | bytes 32768 | tf_op jit(solution)/shard_map/all_to_all | solution.py:543
  90.1 12.3 %all_to_all.28 = f32[32,4,128]{2,1,0:T(4,128)S(1)} all-to-all(f32[32,4,128]{2,1,0:T(4,128)S(1)} %broadcast_in_dim.5), channel_id=1, replica_groups=mesh['space'=32,'rx'=8] {'space'}, dimensions={0} | all-to-all | bytes 131072 | tf_op jit(solution)/shard_map/all_to_all | solution.py:543
  102.4 7.7 %shard_map.81 = f32[8,3,8,8,128]{4,3,2,1,0:T(8,128)S(1)} custom-call(f32[128,128]{1,0:T(8,128)S(1)} %bitcast.7, f32[8,31,8,128]{3,2,1,0:T(8,128)S(1)} %bitcast.6, f32[8,3,10,8,128]{4,3,2,1,0:T(8,128)S(1)} %get-tuple-element.21.v1, f32[8,3,9,8,128]{4,3,2,1,0:T(8,128)S(1)} %get-tuple-element.24.v2), custom_call_target="tpu_custom_call" | custom-call | bytes 4194304 | tf_op jit(solution)/shard_map/pallas_call | solution.py:539
  110.1 26.0 %all_to_all.29.tiles = f32[8,3,8,8,128]{4,3,2,1,0:T(8,128)S(1)} all-to-all(f32[8,3,8,8,128]{4,3,2,1,0:T(8,128)S(1)} %shard_map.81), channel_id=1, replica_groups=mesh['space'=32,'rx'=8] {'rx'}, dimensions={0} | all-to-all | bytes 1572864 | tf_op jit(solution)/shard_map/all_to_all | solution.py:543
  136.0 1.4 shard_map.82
  (7 shorter events, 0.1 us)
Async XLA Ops:
  38.5 4.0 %copy-start = (f32[11,8,128]{2,1,0:T(8,128)S(1)}, f32[11,8,128]{2,1,0:T(8,128)}, u32[]{:S(2)}) copy-start(f32[11,8,128]{2,1,0:T(8,128)} %get-tuple-element.16.mass) | copy-start | bytes 135172
  39.2 8.3 %collective-permute-start = (f32[4,2,10,8,128]{4,3,2,1,0:T(8,128)S(1)}, f32[4,2,10,8,128]{4,3,2,1,0:T(8,128)S(1)}, u32[]{:S(2)}, u32[]{:S(2)}) collective-permute-start(f32[4,2,10,8,128]{4,3,2,1,0:T(8,128)S(1)} %shard_map.74), channel_id=1, source_target_pairs={{0,1},{1,0},{2,3},{3,2},{4,5},{5,4},{6,7},{7,6},{8,16},{9,17},{10,... | collective-permute-start | bytes 983048 | tf_op jit(solution)/shard_map/ppermute | solution.py:582
  44.6 2.9 %collective-permute-start.1 = (f32[4,2,10,8,128]{4,3,2,1,0:T(8,128)S(1)}, f32[4,2,10,8,128]{4,3,2,1,0:T(8,128)S(1)}, u32[]{:S(2)}, u32[]{:S(2)}) collective-permute-start(f32[4,2,10,8,128]{4,3,2,1,0:T(8,128)S(1)} %get-tuple-element.18), channel_id=1, source_target_pairs={{0,8},{8,0},{16,24},{24,16},{32,40},{40,32},{48,56},{56,48},{64,72... | collective-permute-start | bytes 983048 | tf_op jit(solution)/shard_map/ppermute | solution.py:584
  48.8 6.9 %collective-permute-start.2 = (f32[4,2,10,8,128]{4,3,2,1,0:T(8,128)S(1)}, f32[4,2,10,8,128]{4,3,2,1,0:T(8,128)S(1)}, u32[]{:S(2)}, u32[]{:S(2)}) collective-permute-start(f32[4,2,10,8,128]{4,3,2,1,0:T(8,128)S(1)} %shard_map.76), channel_id=1, source_target_pairs={{0,1},{1,0},{2,3},{3,2},{4,5},{5,4},{6,7},{7,6},{8,16},{9,17},{10,... | collective-permute-start | bytes 983048 | tf_op jit(solution)/shard_map/ppermute | solution.py:588
  52.0 3.7 %collective-permute-start.3 = (f32[4,2,10,8,128]{4,3,2,1,0:T(8,128)S(1)}, f32[4,2,10,8,128]{4,3,2,1,0:T(8,128)S(1)}, u32[]{:S(2)}, u32[]{:S(2)}) collective-permute-start(f32[4,2,10,8,128]{4,3,2,1,0:T(8,128)S(1)} %get-tuple-element.20), channel_id=1, source_target_pairs={{0,8},{8,0},{16,24},{24,16},{32,40},{40,32},{48,56},{56,48},{64,72... | collective-permute-start | bytes 983048 | tf_op jit(solution)/shard_map/ppermute | solution.py:589
  56.1 5.9 %collective-permute-start.4 = (f32[4,2,8,8,128]{4,3,2,1,0:T(8,128)S(1)}, f32[4,2,8,8,128]{4,3,2,1,0:T(8,128)S(1)}, u32[]{:S(2)}, u32[]{:S(2)}) collective-permute-start(f32[4,2,8,8,128]{4,3,2,1,0:T(8,128)S(1)} %shard_map.79), channel_id=1, source_target_pairs={{8,0},{16,8},{24,16},{32,24},{40,32},{48,40},{56,48},{64,56},{72,6... | collective-permute-start | bytes 786440 | tf_op jit(solution)/shard_map/ppermute | solution.py:591
